TPU v7x, 256 devices: a whole 4x4x8 slice. The times are simulated.
256 devices in a mesh: gz: 64 (over y, x_lo, z), view: 4 (over x_hi, core).
Axes of the slice: x: 4 (x_hi: 2, x_lo: 2; x = x_hi * 2 + x_lo), y: 4, z: 8, core: 2. Of those that a mesh axis runs over, the one named last changes fastest.
Arguments:
- estimate: float32 [1280, 128, 128], P('gz'), may hold values from 0.25 to 4
- recordings: bfloat16 [8, 1280, 128, 128], P('view', 'gz'), may hold values from 0.25 to 4
- psf_taps: float32 [8, 3, 2, 21], P('view'), may hold values from 0.05 to 1
Outputs:
- updated: float32 [1280, 128, 128], P('gz', 'view')
All inputs are finite; a program needn't handle non-finite values.
Results may differ from a plain program's by a relative error of at most 0.00075.
Values may be sent and summed in bfloat16 or wider, within the bound.
No kernel may reach another device: no remote copies, remote signals or barrier semaphores. Data moves between devices by JAX's collectives and lax.ppermute only.
A program may use at most 128 MiB of HBM per device.

v0:
```python
import jax
import jax.numpy as jnp
from jax import lax
from jax.experimental import pallas as pl
from jax.experimental.pallas import tpu as pltpu
from jax.sharding import PartitionSpec as P

F32 = jnp.float32
BF16 = jnp.bfloat16
VMEM = pl.BlockSpec(memory_space=pltpu.VMEM)
SMEM = pl.BlockSpec(memory_space=pltpu.SMEM)
LIMIT = 48 * 1024 * 1024


def split(value):
    high = value.astype(BF16)
    return high, (value - high.astype(F32)).astype(BF16)


def params(flops, nbytes):
    return dict(
        compiler_params=pltpu.CompilerParams(vmem_limit_bytes=LIMIT),
        cost_estimate=pl.CostEstimate(flops=flops, bytes_accessed=nbytes, transcendentals=0),
    )


def matrices_kernel(place_ref, taps_ref, z_ref, x_ref, y_ref):
    views, taps = taps_ref.shape[0], taps_ref.shape[3]
    half = (taps - 1) // 2
    rows = x_ref.shape[3] // 2
    place = place_ref[0]
    zeros = jnp.zeros((rows, rows), BF16)

    def inverse(values):
        total = values[0]
        for value in values[1:]:
            total = total + value
        return total

    for v in range(views):
        tap = {
            (d, r): [taps_ref[v, d, r, j] for j in range(taps)] for d in range(3) for r in range(2)
        }
        scale = {}
        for r in range(2):
            for d in range(2):
                scale[d, r] = 1.0 / jnp.full((8, 128), inverse(tap[d, r]), F32)[0:1]
            scale[2, r] = 1.0 / jnp.full((8, 128), inverse(tap[2, 0] + tap[2, 1]), F32)[0:1]
        for direction in range(2):
            for part in range(2):
                for r in range(2):
                    other = 1 - r
                    x_ref[direction, v, part, r * rows : (r + 1) * rows, other * rows : (other + 1) * rows] = zeros
        step = 32
        for first in range(0, rows, step):
            diff = (
                lax.broadcasted_iota(jnp.int32, (step, rows), 0)
                - lax.broadcasted_iota(jnp.int32, (step, rows), 1)
                + (first + half)
            )
            made = {(d, r, m): jnp.zeros((step, rows), F32) for d in range(2) for r in range(2) for m in range(2)}
            for j in range(taps):
                here = diff == j
                for d, r, m in made:
                    pick = tap[d, r][j] if m == 0 else tap[d, r][taps - 1 - j]
                    made[d, r, m] = jnp.where(here, pick, made[d, r, m])
            for (d, r, m), value in made.items():
                parts = split(value * scale[d, r])
                for part in range(2):
                    lanes = slice(r * rows, (r + 1) * rows)
                    if d == 0:
                        x_ref[m, v, part, r * rows + first : r * rows + first + step, lanes] = parts[part]
                    elif m == 1:
                        y_ref[0, v, part, first : first + step, lanes] = parts[part]
                    else:
                        target = pl.multiple_of(jnp.bitwise_xor(first // step, place) * step, step)
                        y_ref[1, v, part, pl.ds(target, step), lanes] = parts[part]
        tall = z_ref.shape[3] // 2
        wide = z_ref.shape[4]
        step = 16
        for first in range(0, tall, step):
            diff = (
                lax.broadcasted_iota(jnp.int32, (step, wide), 1)
                - lax.broadcasted_iota(jnp.int32, (step, wide), 0)
                - first
            )
            made = {(r, m): jnp.zeros((step, wide), F32) for r in range(2) for m in range(2)}
            for j in range(taps):
                here = diff == 8 * j
                for r, m in made:
                    pick = tap[2, r][j] if m == 0 else tap[2, r][taps - 1 - j]
                    made[r, m] = jnp.where(here, pick, made[r, m])
            for (r, m), value in made.items():
                parts = split(value * scale[2, r][0:1, 0:1])
                for part in range(2):
                    z_ref[m, v, part, r * tall + first : r * tall + first + step, :] = parts[part]


def dot(a, b):
    return jnp.dot(a, b, preferred_element_type=F32)


def filter_to(pieces, z_ref, x_ref, y_ref, g_ref, exact, emit):
    tall = z_ref.shape[1] // 2
    z_out = tall // 8
    taps_reach = sum(piece.shape[0] for piece in pieces) - 2 * z_out
    rows = y_ref.shape[1]
    for pair in range(rows // 16):
        at = slice(pair * 16, pair * 16 + 16)
        block = jnp.concatenate([piece[:, at, :].astype(F32) for piece in pieces], axis=0)
        planes = block.shape[0]
        octets = [block[:, 8 * o : 8 * o + 8, :].reshape(planes * 8, rows).astype(BF16) for o in range(2)]
        octets = jnp.concatenate(octets, axis=1)
        for part in range(2):
            begin = part * z_out * 8
            data = octets[begin : begin + (z_out + taps_reach) * 8]
            depth = data.shape[0]
            e = dot(z_ref[0, :, :depth], data) + dot(z_ref[1, :, :depth], data)
            e = jnp.concatenate(
                [
                    jnp.concatenate([e[:tall, o * rows : (o + 1) * rows], e[tall:, o * rows : (o + 1) * rows]], axis=1)
                    for o in range(2)
                ],
                axis=0,
            )
            if exact:
                high, low = split(e)
                g = dot(high, x_ref[0]) + dot(high, x_ref[1]) + dot(low, x_ref[0])
            else:
                high = e.astype(BF16)
                g = dot(high, x_ref[0]) + dot(high, x_ref[1])
            for r in range(2):
                lanes = slice(r * rows, (r + 1) * rows)
                g_rows = jnp.concatenate([g[o * tall : (o + 1) * tall, lanes].reshape(z_out, 8, rows) for o in range(2)], axis=1)
                target = slice(r * rows + pair * 16, r * rows + pair * 16 + 16)
                planes_at = slice(part * z_out, (part + 1) * z_out)
                if exact:
                    high, low = split(g_rows)
                    g_ref[0, planes_at, target, :] = high
                    g_ref[1, planes_at, target, :] = low
                else:
                    g_ref[0, planes_at, target, :] = g_rows.astype(BF16)
    for z in range(0, 2 * z_out, 2):
        data = jnp.concatenate([g_ref[0, z], g_ref[0, z + 1]], axis=1)
        out = dot(y_ref[0], data) + dot(y_ref[1], data)
        if exact:
            data = jnp.concatenate([g_ref[1, z], g_ref[1, z + 1]], axis=1)
            out = out + dot(y_ref[0], data)
        emit(z, out[:, :rows])
        emit(z + 1, out[:, rows:])


def quotient_kernel(v, before_ref, own_ref, after_ref, rec_ref, z_ref, x_ref, y_ref, low_ref, high_ref, g_ref):
    margin = low_ref.shape[0]

    def emit(z, blurred):
        quotient = (rec_ref[v, z].astype(F32) / blurred).astype(BF16)
        if z < margin:
            low_ref[z] = quotient
        else:
            high_ref[z - margin] = quotient

    pieces = [before_ref, own_ref, after_ref]
    filter_to(pieces, z_ref.at[0, v], x_ref.at[0, v], y_ref.at[0, v], g_ref, False, emit)


def first_correction_kernel(v, before_ref, low_ref, high_ref, after_ref, z_ref, x_ref, y_ref, out_ref, g_ref):
    def emit(z, correction):
        out_ref[z] = correction

    pieces = [before_ref, low_ref, high_ref, after_ref]
    filter_to(pieces, z_ref.at[1, v], x_ref.at[1, v], y_ref.at[1, v], g_ref, True, emit)


def last_correction_kernel(
    v, before_ref, low_ref, high_ref, after_ref, earlier_ref, z_ref, x_ref, y_ref, keep_ref, send_ref, g_ref
):
    part = keep_ref.shape[2]

    def emit(z, correction):
        product = correction * earlier_ref[z]
        for b in range(4):
            rows = product[b * part : (b + 1) * part]
            if b % 2 == 0:
                keep_ref[b // 2, z] = rows
            else:
                send_ref[b // 2, z] = rows

    pieces = [before_ref, low_ref, high_ref, after_ref]
    filter_to(pieces, z_ref.at[1, v], x_ref.at[1, v], y_ref.at[1, v], g_ref, True, emit)


def local(estimate, recordings, psf_taps):
    planes, rows, cols = estimate.shape
    taps = psf_taps.shape[-1]
    margin = (taps - 1) // 2
    views = recordings.shape[0]
    devices = lax.axis_size("gz")
    place = lax.axis_index("view")
    up = [(i, i + 1) for i in range(devices - 1)]
    down = [(i + 1, i) for i in range(devices - 1)]
    z_out = planes // 2

    before = lax.ppermute(estimate[planes - margin :].astype(BF16), "gz", up)
    after = lax.ppermute(estimate[:margin].astype(BF16), "gz", down)

    shape = jax.ShapeDtypeStruct
    wide = -(-(z_out + taps - 1) * 8 // 128) * 128
    z_mat, x_mat, y_mat = pl.pallas_call(
        matrices_kernel,
        out_shape=[
            shape((2, views, 2, 2 * z_out * 8, wide), BF16),
            shape((2, views, 2, 2 * cols, 2 * cols), BF16),
            shape((2, views, 2, rows, 2 * rows), BF16),
        ],
        in_specs=[SMEM, SMEM],
        out_specs=[VMEM] * 3,
        name="matrices",
        **params(10**9, 10**7),
    )(place.reshape(1).astype(jnp.int32), psf_taps)

    halves = []
    for v in range(views):
        halves.append(
            pl.pallas_call(
                lambda *refs, v=v: quotient_kernel(v, *refs),
                out_shape=[shape((margin, rows, cols), BF16), shape((planes - margin, rows, cols), BF16)],
                in_specs=[VMEM] * 7,
                out_specs=[VMEM] * 2,
                scratch_shapes=[pltpu.VMEM((1, planes, 2 * rows, cols), BF16)],
                name="quotient",
                **params(3 * 10**9, 5 * 10**6),
            )(before, estimate, after, recordings, z_mat, x_mat, y_mat)
        )
    sent = [(lax.ppermute(high, "gz", up), lax.ppermute(low, "gz", down)) for low, high in halves]
    product = pl.pallas_call(
        lambda *refs: first_correction_kernel(0, *refs),
        out_shape=shape((planes, rows, cols), F32),
        in_specs=[VMEM] * 7,
        out_specs=VMEM,
        scratch_shapes=[pltpu.VMEM((2, planes, 2 * rows, cols), BF16)],
        name="correction",
        **params(3 * 10**9, 5 * 10**6),
    )(sent[0][0], *halves[0], sent[0][1], z_mat, x_mat, y_mat)
    part = rows // 4
    keep, send = pl.pallas_call(
        lambda *refs: last_correction_kernel(1, *refs),
        out_shape=[shape((2, planes, part, cols), F32)] * 2,
        in_specs=[VMEM] * 8,
        out_specs=[VMEM] * 2,
        scratch_shapes=[pltpu.VMEM((2, planes, 2 * rows, cols), BF16)],
        name="corrections",
        **params(3 * 10**9, 5 * 10**6),
    )(sent[1][0], *halves[1], sent[1][1], product, z_mat, x_mat, y_mat)
    core = lax.ppermute(send, "view", [(i, i ^ 1) for i in range(4)])
    across = lax.ppermute(keep[1] * core[1], "view", [(i, i ^ 2) for i in range(4)])
    own = lax.dynamic_slice_in_dim(estimate, place * part, part, 1)
    return own * (keep[0] * core[0]) * across


def solution(mesh):
    in_specs = (P("gz", None, None), P("view", "gz", None, None), P("view", None, None, None))
    out_specs = P("gz", "view", None)
    return jax.shard_map(local, mesh=mesh, in_specs=in_specs, out_specs=out_specs, check_vma=False)
```

profile of v0, /device:TPU:24, one launch (start us, length us, event | category | flops | bytes accessed | tf_op | source)
XLA Modules:
  0.0 69.3 jit_solution(1490377309599596016)
XLA Ops:
  0.0 0.0 copy-start.2
  0.0 1.4 %convert.4 = bf16[20,128,128]{2,1,0:T(8,128)(2,1)S(1)} convert(f32[20,128,128]{2,1,0:T(8,128)} %refs_1_.3) | non-fusion elementwise | flops 327680 | bytes 1966080 | tf_op jit(solution)/shard_map/convert.1
  1.5 8.9 %collective-permute-start.1 = (bf16[10,128,128]{2,1,0:T(8,128)(2,1)S(1)}, bf16[10,128,128]{2,1,0:T(8,128)(2,1)S(1)}, u32[]{:S(2)}, u32[]{:S(2)}) collective-permute-start(bf16[10,128,128]{2,1,0:T(8,128)(2,1)S(1)} %get-tuple-element.23), channel_id=1, source_target_pairs={{4,0},{8,4},{12,8},{16,12},{20,16},{24,20},{28,24},{32,28},{36,32}... | collective-permute-start | bytes 983048 | tf_op jit(solution)/shard_map/ppermute | solution.py:205
  10.4 1.9 %collective-permute-start = (bf16[10,128,128]{2,1,0:T(8,128)(2,1)S(1)}, bf16[10,128,128]{2,1,0:T(8,128)(2,1)S(1)}, u32[]{:S(2)}, u32[]{:S(2)}) collective-permute-start(bf16[10,128,128]{2,1,0:T(8,128)(2,1)S(1)} %get-tuple-element.24), channel_id=1, source_target_pairs={{0,4},{4,8},{8,12},{12,16},{16,20},{20,24},{24,28},{28,32},{32,36}... | collective-permute-start | bytes 983048 | tf_op jit(solution)/shard_map/ppermute | solution.py:204
  12.3 0.0 copy-done.2
  12.3 0.0 copy-start
  12.3 0.0 copy-start.1
  12.3 2.8 %matrices.1 = (bf16[2,2,2,160,256]{4,3,2,1,0:T(8,128)(2,1)S(1)}, bf16[2,2,2,256,256]{4,3,2,1,0:T(8,128)(2,1)S(1)}, bf16[2,2,2,128,256]{4,3,2,1,0:T(8,128)(2,1)S(1)}) custom-call(s32[1]{0:T(128)} %bitcast.place_ref, f32[2,3,2,21]{3,2,1,0:T(2,128)S(1)} %copy-done.2), custom_call_target="tpu_custom_call" | custom-call | flops 1000000000 | bytes 10000000 | tf_op jit(solution)/shard_map/matrices/pallas_call | solution.py:209
  15.1 2.2 %collective-permute-done.1.refs_2_ = bf16[10,128,128]{2,1,0:T(8,128)(2,1)S(1)} collective-permute-done((bf16[10,128,128]{2,1,0:T(8,128)(2,1)S(1)}, bf16[10,128,128]{2,1,0:T(8,128)(2,1)S(1)}, u32[]{:S(2)}, u32[]{:S(2)}) %collective-permute-start.1) | collective-permute-done | bytes 327712 | tf_op jit(solution)/shard_map/ppermute | solution.py:205
  17.3 7.1 %collective-permute-done.refs_0_ = bf16[10,128,128]{2,1,0:T(8,128)(2,1)S(1)} collective-permute-done((bf16[10,128,128]{2,1,0:T(8,128)(2,1)S(1)}, bf16[10,128,128]{2,1,0:T(8,128)(2,1)S(1)}, u32[]{:S(2)}, u32[]{:S(2)}) %collective-permute-start) | collective-permute-done | bytes 327712 | tf_op jit(solution)/shard_map/ppermute | solution.py:204
  24.4 0.0 copy-done
  24.5 0.0 copy-done.1
  24.5 2.1 %quotient.3 = (bf16[10,128,128]{2,1,0:T(8,128)(2,1)S(1)}, bf16[10,128,128]{2,1,0:T(8,128)(2,1)S(1)}) custom-call(bf16[10,128,128]{2,1,0:T(8,128)(2,1)S(1)} %collective-permute-done.refs_0_, f32[20,128,128]{2,1,0:T(8,128)S(1)} %copy-done, bf16[10,128,128]{2,1,0:T(8,128)(2,1)S(1)} %collective-permute-done.1.refs_2_, bf16[2,20,128,128]{3,2,1,0:T(8,128)(2,1)S(1)} %copy-done.1, ...), custom_call_target="tpu_custom_call" | custom-call | flops 3000000000 | bytes 5000000 | tf_op jit(solution)/shard_map/quotient/pallas_call | solution.py:225
  26.6 1.9 %collective-permute-start.4 = (bf16[10,128,128]{2,1,0:T(8,128)(2,1)S(1)}, bf16[10,128,128]{2,1,0:T(8,128)(2,1)S(1)}, u32[]{:S(2)}, u32[]{:S(2)}) collective-permute-start(bf16[10,128,128]{2,1,0:T(8,128)(2,1)S(1)} %get-tuple-element.19.refs_2_), channel_id=1, source_target_pairs={{0,4},{4,8},{8,12},{12,16},{16,20},{20,24},{24,28},{28,32},{32,36}... | collective-permute-start | bytes 983048 | tf_op jit(solution)/shard_map/ppermute | solution.py:235
  28.5 6.9 %collective-permute-start.5 = (bf16[10,128,128]{2,1,0:T(8,128)(2,1)S(1)}, bf16[10,128,128]{2,1,0:T(8,128)(2,1)S(1)}, u32[]{:S(2)}, u32[]{:S(2)}) collective-permute-start(bf16[10,128,128]{2,1,0:T(8,128)(2,1)S(1)} %get-tuple-element.20.refs_1_), channel_id=1, source_target_pairs={{4,0},{8,4},{12,8},{16,12},{20,16},{24,20},{28,24},{32,28},{36,32}... | collective-permute-start | bytes 983048 | tf_op jit(solution)/shard_map/ppermute | solution.py:235
  35.5 2.1 %quotient.2 = (bf16[10,128,128]{2,1,0:T(8,128)(2,1)S(1)}, bf16[10,128,128]{2,1,0:T(8,128)(2,1)S(1)}) custom-call(bf16[10,128,128]{2,1,0:T(8,128)(2,1)S(1)} %collective-permute-done.refs_0_, f32[20,128,128]{2,1,0:T(8,128)S(1)} %copy-done, bf16[10,128,128]{2,1,0:T(8,128)(2,1)S(1)} %collective-permute-done.1.refs_2_, bf16[2,20,128,128]{3,2,1,0:T(8,128)(2,1)S(1)} %copy-done.1, ...), custom_call_target="tpu_custom_call" | custom-call | flops 3000000000 | bytes 5000000 | tf_op jit(solution)/shard_map/quotient/pallas_call | solution.py:225
  37.6 1.9 %collective-permute-start.2 = (bf16[10,128,128]{2,1,0:T(8,128)(2,1)S(1)}, bf16[10,128,128]{2,1,0:T(8,128)(2,1)S(1)}, u32[]{:S(2)}, u32[]{:S(2)}) collective-permute-start(bf16[10,128,128]{2,1,0:T(8,128)(2,1)S(1)} %get-tuple-element.17.refs_2_), channel_id=1, source_target_pairs={{0,4},{4,8},{8,12},{12,16},{16,20},{20,24},{24,28},{28,32},{32,36}... | collective-permute-start | bytes 983048 | tf_op jit(solution)/shard_map/ppermute | solution.py:235
  39.5 7.1 %collective-permute-start.3 = (bf16[10,128,128]{2,1,0:T(8,128)(2,1)S(1)}, bf16[10,128,128]{2,1,0:T(8,128)(2,1)S(1)}, u32[]{:S(2)}, u32[]{:S(2)}) collective-permute-start(bf16[10,128,128]{2,1,0:T(8,128)(2,1)S(1)} %get-tuple-element.18.refs_1_), channel_id=1, source_target_pairs={{4,0},{8,4},{12,8},{16,12},{20,16},{24,20},{28,24},{32,28},{36,32}... | collective-permute-start | bytes 983048 | tf_op jit(solution)/shard_map/ppermute | solution.py:235
  46.7 0.0 collective-permute-done.4.refs_0_
  46.7 0.0 collective-permute-done.5.refs_3_
  46.7 3.5 %correction.1.refs_4_ = f32[20,128,128]{2,1,0:T(8,128)S(1)} custom-call(bf16[10,128,128]{2,1,0:T(8,128)(2,1)S(1)} %collective-permute-done.4.refs_0_, bf16[10,128,128]{2,1,0:T(8,128)(2,1)S(1)} %get-tuple-element.20.refs_1_, bf16[10,128,128]{2,1,0:T(8,128)(2,1)S(1)} %get-tuple-element.19.refs_2_, bf16[10,128,128]{2,1,0:T(8,128)(2,1)S(1)} %collective-permute-done.5.refs_3_, ...), custom_call_target="tpu_custom_call" | custom-call | flops 3000000000 | bytes 5000000 | tf_op jit(solution)/shard_map/correction/pallas_call | solution.py:236
  50.2 0.1 collective-permute-done.2.refs_0_
  50.2 1.2 %collective-permute-done.3.refs_3_ = bf16[10,128,128]{2,1,0:T(8,128)(2,1)S(1)} collective-permute-done((bf16[10,128,128]{2,1,0:T(8,128)(2,1)S(1)}, bf16[10,128,128]{2,1,0:T(8,128)(2,1)S(1)}, u32[]{:S(2)}, u32[]{:S(2)}) %collective-permute-start.3) | collective-permute-done | bytes 327712 | tf_op jit(solution)/shard_map/ppermute | solution.py:235
  51.4 3.5 %corrections.1 = (f32[2,20,32,128]{3,2,1,0:T(8,128)S(1)}, f32[2,20,32,128]{3,2,1,0:T(8,128)S(1)}) custom-call(bf16[10,128,128]{2,1,0:T(8,128)(2,1)S(1)} %collective-permute-done.2.refs_0_, bf16[10,128,128]{2,1,0:T(8,128)(2,1)S(1)} %get-tuple-element.18.refs_1_, bf16[10,128,128]{2,1,0:T(8,128)(2,1)S(1)} %get-tuple-element.17.refs_2_, ...), custom_call_target="tpu_custom_call" | custom-call | flops 3000000000 | bytes 5000000 | tf_op jit(solution)/shard_map/corrections/pallas_call | solution.py:246
  54.9 0.1 collective-permute-start.6
  55.0 2.1 %collective-permute-done.6 = f32[2,20,32,128]{3,2,1,0:T(8,128)S(1)} collective-permute-done((f32[2,20,32,128]{3,2,1,0:T(8,128)S(1)}, f32[2,20,32,128]{3,2,1,0:T(8,128)S(1)}, u32[]{:S(2)}, u32[]{:S(2)}) %collective-permute-start.6) | collective-permute-done | bytes 655392 | tf_op jit(solution)/shard_map/ppermute | solution.py:255
  57.1 2.8 %collective-permute-start.7 = (f32[20,32,128]{2,1,0:T(8,128)S(1)}, f32[20,32,128]{2,1,0:T(8,128)S(1)}, u32[]{:S(2)}, u32[]{:S(2)}) collective-permute-start(f32[20,32,128]{2,1,0:T(8,128)S(1)} %fusion), channel_id=1, source_target_pairs={{0,2},{1,3},{2,0},{3,1},{4,6},{5,7},{6,4},{7,5},{8,10},{9,11},{10,... | collective-permute-start | bytes 983048 | tf_op jit(solution)/shard_map/ppermute | solution.py:256
  59.9 8.5 %collective-permute-done.7 = f32[20,32,128]{2,1,0:T(8,128)S(1)} collective-permute-done((f32[20,32,128]{2,1,0:T(8,128)S(1)}, f32[20,32,128]{2,1,0:T(8,128)S(1)}, u32[]{:S(2)}, u32[]{:S(2)}) %collective-permute-start.7) | collective-permute-done | bytes 327712 | tf_op jit(solution)/shard_map/ppermute | solution.py:256
  68.5 0.8 %fusion.3 = f32[20,32,128]{2,1,0:T(8,128)} fusion(f32[20,32,128]{2,1,0:T(8,128)S(1)} %collective-permute-done.7, f32[2,20,32,128]{3,2,1,0:T(8,128)S(1)} %collective-permute-done.6, f32[2,20,32,128]{3,2,1,0:T(8,128)S(1)} %get-tuple-element.21, f32[20,128,128]{2,1,0:T(8,128)S(1)} %copy-done, s32[]{:T(128)S(6)} %select_n.3), kind=kLoop, calls=%fused_computation.5 | loop fusion | flops 245760 | bytes 1638404 | tf_op jit(solution)/shard_map/mul | solution.py:258
  (2 shorter events, 0.1 us)
Async XLA Ops:
  0.0 12.3 %copy-start.2 = (f32[2,3,2,21]{3,2,1,0:T(2,128)S(1)}, f32[2,3,2,21]{3,2,1,0:T(2,128)}, u32[]{:S(2)}) copy-start(f32[2,3,2,21]{3,2,1,0:T(2,128)} %taps_ref.1) | copy-start | bytes 3028
  1.5 15.8 %collective-permute-start.1 = (bf16[10,128,128]{2,1,0:T(8,128)(2,1)S(1)}, bf16[10,128,128]{2,1,0:T(8,128)(2,1)S(1)}, u32[]{:S(2)}, u32[]{:S(2)}) collective-permute-start(bf16[10,128,128]{2,1,0:T(8,128)(2,1)S(1)} %get-tuple-element.23), channel_id=1, source_target_pairs={{4,0},{8,4},{12,8},{16,12},{20,16},{24,20},{28,24},{32,28},{36,32}... | collective-permute-start | bytes 983048 | tf_op jit(solution)/shard_map/ppermute | solution.py:205
  10.4 14.1 %collective-permute-start = (bf16[10,128,128]{2,1,0:T(8,128)(2,1)S(1)}, bf16[10,128,128]{2,1,0:T(8,128)(2,1)S(1)}, u32[]{:S(2)}, u32[]{:S(2)}) collective-permute-start(bf16[10,128,128]{2,1,0:T(8,128)(2,1)S(1)} %get-tuple-element.24), channel_id=1, source_target_pairs={{0,4},{4,8},{8,12},{12,16},{16,20},{20,24},{24,28},{28,32},{32,36}... | collective-permute-start | bytes 983048 | tf_op jit(solution)/shard_map/ppermute | solution.py:204
  12.3 12.1 %copy-start = (f32[20,128,128]{2,1,0:T(8,128)S(1)}, f32[20,128,128]{2,1,0:T(8,128)}, u32[]{:S(2)}) copy-start(f32[20,128,128]{2,1,0:T(8,128)} %refs_1_.3) | copy-start | bytes 3932164
  12.3 12.1 %copy-start.1 = (bf16[2,20,128,128]{3,2,1,0:T(8,128)(2,1)S(1)}, bf16[2,20,128,128]{3,2,1,0:T(8,128)(2,1)}, u32[]{:S(2)}) copy-start(bf16[2,20,128,128]{3,2,1,0:T(8,128)(2,1)} %refs_3_.3) | copy-start | bytes 3932164
  26.6 20.1 %collective-permute-start.4 = (bf16[10,128,128]{2,1,0:T(8,128)(2,1)S(1)}, bf16[10,128,128]{2,1,0:T(8,128)(2,1)S(1)}, u32[]{:S(2)}, u32[]{:S(2)}) collective-permute-start(bf16[10,128,128]{2,1,0:T(8,128)(2,1)S(1)} %get-tuple-element.19.refs_2_), channel_id=1, source_target_pairs={{0,4},{4,8},{8,12},{12,16},{16,20},{20,24},{24,28},{28,32},{32,36}... | collective-permute-start | bytes 983048 | tf_op jit(solution)/shard_map/ppermute | solution.py:235
  28.5 18.1 %collective-permute-start.5 = (bf16[10,128,128]{2,1,0:T(8,128)(2,1)S(1)}, bf16[10,128,128]{2,1,0:T(8,128)(2,1)S(1)}, u32[]{:S(2)}, u32[]{:S(2)}) collective-permute-start(bf16[10,128,128]{2,1,0:T(8,128)(2,1)S(1)} %get-tuple-element.20.refs_1_), channel_id=1, source_target_pairs={{4,0},{8,4},{12,8},{16,12},{20,16},{24,20},{28,24},{32,28},{36,32}... | collective-permute-start | bytes 983048 | tf_op jit(solution)/shard_map/ppermute | solution.py:235
  37.6 12.6 %collective-permute-start.2 = (bf16[10,128,128]{2,1,0:T(8,128)(2,1)S(1)}, bf16[10,128,128]{2,1,0:T(8,128)(2,1)S(1)}, u32[]{:S(2)}, u32[]{:S(2)}) collective-permute-start(bf16[10,128,128]{2,1,0:T(8,128)(2,1)S(1)} %get-tuple-element.17.refs_2_), channel_id=1, source_target_pairs={{0,4},{4,8},{8,12},{12,16},{16,20},{20,24},{24,28},{28,32},{32,36}... | collective-permute-start | bytes 983048 | tf_op jit(solution)/shard_map/ppermute | solution.py:235
  39.5 11.9 %collective-permute-start.3 = (bf16[10,128,128]{2,1,0:T(8,128)(2,1)S(1)}, bf16[10,128,128]{2,1,0:T(8,128)(2,1)S(1)}, u32[]{:S(2)}, u32[]{:S(2)}) collective-permute-start(bf16[10,128,128]{2,1,0:T(8,128)(2,1)S(1)} %get-tuple-element.18.refs_1_), channel_id=1, source_target_pairs={{4,0},{8,4},{12,8},{16,12},{20,16},{24,20},{28,24},{32,28},{36,32}... | collective-permute-start | bytes 983048 | tf_op jit(solution)/shard_map/ppermute | solution.py:235
  54.9 2.2 %collective-permute-start.6 = (f32[2,20,32,128]{3,2,1,0:T(8,128)S(1)}, f32[2,20,32,128]{3,2,1,0:T(8,128)S(1)}, u32[]{:S(2)}, u32[]{:S(2)}) collective-permute-start(f32[2,20,32,128]{3,2,1,0:T(8,128)S(1)} %get-tuple-element.22), channel_id=1, source_target_pairs={{0,1},{1,0},{2,3},{3,2},{4,5},{5,4},{6,7},{7,6},{8,9},{9,8},{10,11... | collective-permute-start | bytes 1966088 | tf_op jit(solution)/shard_map/ppermute | solution.py:255
  57.1 11.3 %collective-permute-start.7 = (f32[20,32,128]{2,1,0:T(8,128)S(1)}, f32[20,32,128]{2,1,0:T(8,128)S(1)}, u32[]{:S(2)}, u32[]{:S(2)}) collective-permute-start(f32[20,32,128]{2,1,0:T(8,128)S(1)} %fusion), channel_id=1, source_target_pairs={{0,2},{1,3},{2,0},{3,1},{4,6},{5,7},{6,4},{7,5},{8,10},{9,11},{10,... | collective-permute-start | bytes 983048 | tf_op jit(solution)/shard_map/ppermute | solution.py:256
where the time goes:
time: 69.6 us; the launch traced here: 69.3 us
  starting transfers between devices  31.6 us (45%)
  waiting for transfers between devices  21.2 us (30%)
  Pallas kernels  14 us (20%)
  other arithmetic  2.32 us (3%)
    ppermute x2, starting transfers between devices, local(): lax.ppermute(low, 'gz', down)  14 us
    ppermute x1, starting transfers between devices, local(): after = lax.ppermute(estimate[:margin].astype(BF16), 'gz', down)  8.87 us
    ppermute x1, waiting for transfers between devices, local(): lax.ppermute(keep[1] * core[1], 'view', [(i, i ^ 2) for i in range(4)])  8.52 us
    ppermute x1, waiting for transfers between devices, local(): before = lax.ppermute(estimate[planes - margin:].astype(BF16), 'gz', up)  7.13 us
    pallas_call x2, Pallas kernels, local(): pl.pallas_call(lambda *refs, v=v: quotient_kernel(v, *refs), out_shape=[s...  4.28 us
    ppermute x2, starting transfers between devices, local(): lax.ppermute(high, 'gz', up)  3.84 us
    pallas_call x1, Pallas kernels, local(): pl.pallas_call(lambda *refs: last_correction_kernel(1, *refs), out_shape=...  3.48 us
    pallas_call x1, Pallas kernels, local(): pl.pallas_call(lambda *refs: first_correction_kernel(0, *refs), out_shape...  3.48 us
  transfers between devices with their start and end apart: 8, of which 6 were waited for; matrix products, arithmetic and copies ran while one was open for 0% of the time, Pallas kernels for 12%

commit v1 on v0

v1 whole, which is shorter than its diff:
```python
import jax
import jax.numpy as jnp
from jax import lax
from jax.experimental import pallas as pl
from jax.experimental.pallas import tpu as pltpu
from jax.sharding import PartitionSpec as P

F32 = jnp.float32
BF16 = jnp.bfloat16
VMEM = pl.BlockSpec(memory_space=pltpu.VMEM)
SMEM = pl.BlockSpec(memory_space=pltpu.SMEM)
LIMIT = 48 * 1024 * 1024


def split(value):
    high = value.astype(BF16)
    return high, (value - high.astype(F32)).astype(BF16)


def params(flops, nbytes):
    return dict(
        compiler_params=pltpu.CompilerParams(vmem_limit_bytes=LIMIT),
        cost_estimate=pl.CostEstimate(flops=flops, bytes_accessed=nbytes, transcendentals=0),
    )


def matrices_kernel(place_ref, taps_ref, z_ref, x_ref, y_ref):
    views, taps = taps_ref.shape[0], taps_ref.shape[3]
    half = (taps - 1) // 2
    rows = x_ref.shape[3] // 2
    place = place_ref[0]
    zeros = jnp.zeros((rows, rows), BF16)

    def inverse(values):
        total = values[0]
        for value in values[1:]:
            total = total + value
        return total

    for v in range(views):
        tap = {
            (d, r): [taps_ref[v, d, r, j] for j in range(taps)] for d in range(3) for r in range(2)
        }
        scale = {}
        for r in range(2):
            for d in range(2):
                scale[d, r] = 1.0 / jnp.full((8, 128), inverse(tap[d, r]), F32)[0:1]
            scale[2, r] = 1.0 / jnp.full((8, 128), inverse(tap[2, 0] + tap[2, 1]), F32)[0:1]
        for direction in range(2):
            for part in range(2):
                for r in range(2):
                    other = 1 - r
                    x_ref[direction, v, part, r * rows : (r + 1) * rows, other * rows : (other + 1) * rows] = zeros
        step = 32
        for first in range(0, rows, step):
            diff = (
                lax.broadcasted_iota(jnp.int32, (step, rows), 0)
                - lax.broadcasted_iota(jnp.int32, (step, rows), 1)
                + (first + half)
            )
            made = {(d, r, m): jnp.zeros((step, rows), F32) for d in range(2) for r in range(2) for m in range(2)}
            for j in range(taps):
                here = diff == j
                for d, r, m in made:
                    pick = tap[d, r][j] if m == 0 else tap[d, r][taps - 1 - j]
                    made[d, r, m] = jnp.where(here, pick, made[d, r, m])
            for (d, r, m), value in made.items():
                parts = split(value * scale[d, r])
                for part in range(2):
                    lanes = slice(r * rows, (r + 1) * rows)
                    if d == 0:
                        x_ref[m, v, part, r * rows + first : r * rows + first + step, lanes] = parts[part]
                    elif m == 1:
                        y_ref[0, v, part, first : first + step, lanes] = parts[part]
                    else:
                        target = pl.multiple_of(jnp.bitwise_xor(first // step, place) * step, step)
                        y_ref[1, v, part, pl.ds(target, step), lanes] = parts[part]
        tall = z_ref.shape[2] // (2 * views)
        wide = z_ref.shape[3]
        step = 16
        for first in range(0, tall, step):
            diff = (
                lax.broadcasted_iota(jnp.int32, (step, wide), 1)
                - lax.broadcasted_iota(jnp.int32, (step, wide), 0)
                - first
            )
            made = {(r, m): jnp.zeros((step, wide), F32) for r in range(2) for m in range(2)}
            for j in range(taps):
                here = diff == 8 * j
                for r, m in made:
                    pick = tap[2, r][j] if m == 0 else tap[2, r][taps - 1 - j]
                    made[r, m] = jnp.where(here, pick, made[r, m])
            for (r, m), value in made.items():
                parts = split(value * scale[2, r][0:1, 0:1])
                for part in range(2):
                    top = (2 * v + r) * tall + first
                    z_ref[m, part, top : top + step, :] = parts[part]


def dot(a, b):
    return jnp.dot(a, b, preferred_element_type=F32)


def filter_to(load, views, groups, z_ref, x_ref, y_ref, g_ref, exact, emit):
    tall = z_ref.shape[1] // (2 * views)
    z_out = tall // 8
    rows = y_ref.shape[2]
    for pair in range(rows // 16):
        block = load(slice(pair * 16, pair * 16 + 16))
        planes = block.shape[0]
        depth = (planes - (groups - 1) * z_out) * 8
        octets = [block[:, 8 * o : 8 * o + 8, :].reshape(planes * 8, rows).astype(BF16) for o in range(2)]
        octets = jnp.concatenate(octets, axis=1)
        for part in range(groups):
            data = octets[part * z_out * 8 : part * z_out * 8 + depth]
            all_e = dot(z_ref[0, :, :depth], data) + dot(z_ref[1, :, :depth], data)
            for v in range(views):
                e = all_e[v * 2 * tall : (v + 1) * 2 * tall]
                e = jnp.concatenate(
                    [
                        jnp.concatenate([e[:tall, o * rows : (o + 1) * rows], e[tall:, o * rows : (o + 1) * rows]], axis=1)
                        for o in range(2)
                    ],
                    axis=0,
                )
                if exact:
                    high, low = split(e)
                    g = dot(high, x_ref[v, 0]) + dot(high, x_ref[v, 1]) + dot(low, x_ref[v, 0])
                else:
                    high = e.astype(BF16)
                    g = dot(high, x_ref[v, 0]) + dot(high, x_ref[v, 1])
                for r in range(2):
                    lanes = slice(r * rows, (r + 1) * rows)
                    g_rows = jnp.concatenate(
                        [g[o * tall : (o + 1) * tall, lanes].reshape(z_out, 8, rows) for o in range(2)], axis=1
                    )
                    target = slice(r * rows + pair * 16, r * rows + pair * 16 + 16)
                    planes_at = slice(part * z_out, (part + 1) * z_out)
                    if exact:
                        high, low = split(g_rows)
                        g_ref[v, 0, planes_at, target, :] = high
                        g_ref[v, 1, planes_at, target, :] = low
                    else:
                        g_ref[v, 0, planes_at, target, :] = g_rows.astype(BF16)
    for v in range(views):
        for z in range(0, groups * z_out, 2):
            data = jnp.concatenate([g_ref[v, 0, z], g_ref[v, 0, z + 1]], axis=1)
            out = dot(y_ref[v, 0], data) + dot(y_ref[v, 1], data)
            if exact:
                data = jnp.concatenate([g_ref[v, 1, z], g_ref[v, 1, z + 1]], axis=1)
                out = out + dot(y_ref[v, 0], data)
            emit(v, z, out[:, :rows])
            emit(v, z + 1, out[:, rows:])


def quotient_kernel(place_ref, mine_ref, other_low_ref, other_high_ref, own_ref, rec_ref, z_ref, x_ref, y_ref, own_out, rim_out, g_ref):
    planes = own_ref.shape[0]
    margin = rim_out.shape[2]
    first_core = place_ref[0] % 2 == 0

    def load(at):
        mine = mine_ref[:, at, :].astype(F32)
        other = jnp.concatenate([ref[:, at, :].astype(F32) for ref in (other_low_ref, other_high_ref)], axis=0)
        before, after = jnp.where(first_core, mine, other), jnp.where(first_core, other, mine)
        return jnp.concatenate([before, own_ref[:, at, :], after], axis=0)

    def emit(v, z, blurred):
        if z < margin:
            rim_out[v, 0, z] = blurred
        elif z < margin + planes:
            own_out[v, z - margin] = (rec_ref[v, z - margin].astype(F32) / blurred).astype(BF16)
        else:
            rim_out[v, 1, z - margin - planes] = blurred

    groups = (planes + 2 * margin) // (planes // 2)
    filter_to(load, rec_ref.shape[0], groups, z_ref.at[0], x_ref.at[0], y_ref.at[0], g_ref, False, emit)


def correction(v, before_ref, own_ref, after_ref, rim_ref, z_ref, x_ref, y_ref, g_ref, emit):
    def load(at):
        before = before_ref[v, :, at, :].astype(F32) / rim_ref[v, 0, :, at, :]
        after = after_ref[v, :, at, :].astype(F32) / rim_ref[v, 1, :, at, :]
        return jnp.concatenate([before, own_ref[v, :, at, :].astype(F32), after], axis=0)

    tall = z_ref.shape[2] // own_ref.shape[0]
    filter_to(
        load,
        1,
        2,
        z_ref.at[1, :, v * tall : (v + 1) * tall],
        x_ref.at[1, v : v + 1],
        y_ref.at[1, v : v + 1],
        g_ref,
        True,
        emit,
    )


def first_correction_kernel(v, before_ref, own_ref, after_ref, rim_ref, z_ref, x_ref, y_ref, out_ref, g_ref):
    def emit(_, z, value):
        out_ref[z] = value

    correction(v, before_ref, own_ref, after_ref, rim_ref, z_ref, x_ref, y_ref, g_ref, emit)


def last_correction_kernel(
    v, before_ref, own_ref, after_ref, rim_ref, earlier_ref, z_ref, x_ref, y_ref, keep_ref, send_ref, g_ref
):
    part = keep_ref.shape[2]

    def emit(_, z, value):
        product = value * earlier_ref[z]
        for b in range(4):
            rows = product[b * part : (b + 1) * part]
            if b % 2 == 0:
                keep_ref[b // 2, z] = rows
            else:
                send_ref[b // 2, z] = rows

    correction(v, before_ref, own_ref, after_ref, rim_ref, z_ref, x_ref, y_ref, g_ref, emit)


def local(estimate, recordings, psf_taps):
    planes, rows, cols = estimate.shape
    taps = psf_taps.shape[-1]
    margin = (taps - 1) // 2
    views = recordings.shape[0]
    devices = lax.axis_size("gz")
    place = lax.axis_index("view")
    place_array = place.reshape(1).astype(jnp.int32)
    up = [(i, i + 1) for i in range(devices - 1)]
    down = [(i + 1, i) for i in range(devices - 1)]
    swap = [(i, i ^ 1) for i in range(4)]
    z_out = planes // 2

    both_ways = [(4 * i + w, 4 * j + w) for w in (0, 2) for i, j in up]
    both_ways += [(4 * i + w, 4 * j + w) for w in (1, 3) for i, j in down]
    mine = lax.ppermute(estimate.astype(BF16), ("gz", "view"), both_ways)
    shape = jax.ShapeDtypeStruct
    wide = -(-(z_out + taps - 1) * 8 // 128) * 128
    z_mat, x_mat, y_mat = pl.pallas_call(
        matrices_kernel,
        out_shape=[
            shape((2, 2, views * 2 * z_out * 8, wide), BF16),
            shape((2, views, 2, 2 * cols, 2 * cols), BF16),
            shape((2, views, 2, rows, 2 * rows), BF16),
        ],
        in_specs=[SMEM, SMEM],
        out_specs=[VMEM] * 3,
        name="matrices",
        **params(10**6, 10**4),
    )(place_array, psf_taps)

    before = lax.ppermute(recordings[:, planes - margin :], "gz", up)
    after = lax.ppermute(recordings[:, :margin], "gz", down)
    mine, z_mat = lax.optimization_barrier((mine, z_mat))
    other = [lax.ppermute(part, "view", swap) for part in (mine[:margin], mine[margin:])]

    own, rim = pl.pallas_call(
        quotient_kernel,
        out_shape=[shape((views, planes, rows, cols), BF16), shape((views, 2, margin, rows, cols), F32)],
        in_specs=[SMEM] + [VMEM] * 8,
        out_specs=[VMEM] * 2,
        scratch_shapes=[pltpu.VMEM((views, 1, planes + 2 * margin, 2 * rows, cols), BF16)],
        name="quotients",
        **params(10**6, 10**4),
    )(place_array, mine, *other, estimate, recordings, z_mat, x_mat, y_mat)
    product = pl.pallas_call(
        lambda *refs: first_correction_kernel(0, *refs),
        out_shape=shape((planes, rows, cols), F32),
        in_specs=[VMEM] * 7,
        out_specs=VMEM,
        scratch_shapes=[pltpu.VMEM((1, 2, planes, 2 * rows, cols), BF16)],
        name="correction",
        **params(4 * 10**9, 5 * 10**6),
    )(before, own, after, rim, z_mat, x_mat, y_mat)
    part = rows // 4
    keep, send = pl.pallas_call(
        lambda *refs: last_correction_kernel(1, *refs),
        out_shape=[shape((2, planes, part, cols), F32)] * 2,
        in_specs=[VMEM] * 8,
        out_specs=[VMEM] * 2,
        scratch_shapes=[pltpu.VMEM((1, 2, planes, 2 * rows, cols), BF16)],
        name="corrections",
        **params(4 * 10**9, 5 * 10**6),
    )(before, own, after, rim, product, z_mat, x_mat, y_mat)
    core = lax.ppermute(send, "view", swap)
    across = lax.ppermute(keep[1] * core[1], "view", [(i, i ^ 2) for i in range(4)])
    mine = lax.dynamic_slice_in_dim(estimate, place * part, part, 1)
    return mine * (keep[0] * core[0]) * across


def solution(mesh):
    in_specs = (P("gz", None, None), P("view", "gz", None, None), P("view", None, None, None))
    out_specs = P("gz", "view", None)
    return jax.shard_map(local, mesh=mesh, in_specs=in_specs, out_specs=out_specs, check_vma=False)
```

time: 69.6 us -> 63.4 us (0.911)
  starting transfers between devices: 31.6 us -> 17.4 us
  Pallas kernels: 14 us -> 23.9 us
  waiting for transfers between devices: 21.2 us -> 16.1 us
  local copies, waits for them, and re-layouts: 0.06 us -> 2.32 us
  other arithmetic: 2.32 us -> 3.26 us
    ppermute x7 -> x6, starting transfers between devices: 28.8 us -> 14.6 us  [the longest x1 7.09 us: local(): after = lax.ppermute(recordings[:, :margin], 'gz', down)]
    pallas_call x3 -> x2, Pallas kernels: 7.06 us -> 13 us  [the longest x1 10.3 us: local(): pl.pallas_call(quotient_kernel, out_shape=[shape((views, planes, rows, co...]
    ppermute x7 -> x6, waiting for transfers between devices: 12.7 us -> 7.54 us  [the longest x1 3.24 us: local(): before = lax.ppermute(recordings[:, planes - margin:], 'gz', up)]
    convert_element_type x0 -> x1, other arithmetic: none -> 2.37 us  [local(): mine = lax.ppermute(estimate.astype(BF16), ('gz', 'view'), both_ways)]
    pallas_call x1, Pallas kernels: 3.48 us -> 5.65 us  [local(): pl.pallas_call(lambda *refs: last_correction_kernel(1, *refs), out_shape=...]
    pallas_call x1, Pallas kernels: 3.48 us -> 5.27 us  [local(): pl.pallas_call(lambda *refs: first_correction_kernel(0, *refs), out_shape...]
    another operation x1 -> x0, other arithmetic: 1.43 us -> none
    slice x1 -> x2, local copies, waits for them, and re-layouts: 0.04 us -> 1.25 us  [the longest x1 1.21 us: local(): after = lax.ppermute(recordings[:, :margin], 'gz', down)]
  transfers between devices with their start and end apart: 8 -> 7, of which waited for: 6 -> 6; matrix products, arithmetic and copies ran while one was open for 0% -> 2% of each run, Pallas kernels for 12% -> 21%
where the time goes in v1:
time: 63.4 us; the launch traced here: 63.1 us
  Pallas kernels  23.9 us (38%)
  starting transfers between devices  17.4 us (27%)
  waiting for transfers between devices  16.1 us (25%)
  other arithmetic  3.26 us (5%)
  local copies, waits for them, and re-layouts  2.32 us (4%)
    pallas_call x1, Pallas kernels, local(): pl.pallas_call(quotient_kernel, out_shape=[shape((views, planes, rows, co...  10.3 us
    ppermute x1, waiting for transfers between devices, local(): lax.ppermute(keep[1] * core[1], 'view', [(i, i ^ 2) for i in range(4)])  8.52 us
    ppermute x1, starting transfers between devices, local(): after = lax.ppermute(recordings[:, :margin], 'gz', down)  7.09 us
    pallas_call x1, Pallas kernels, local(): pl.pallas_call(lambda *refs: last_correction_kernel(1, *refs), out_shape=...  5.65 us
    pallas_call x1, Pallas kernels, local(): pl.pallas_call(lambda *refs: first_correction_kernel(0, *refs), out_shape...  5.27 us
    ppermute x1, starting transfers between devices, local(): mine = lax.ppermute(estimate.astype(BF16), ('gz', 'view'), both_ways)  3.94 us
    ppermute x1, waiting for transfers between devices, local(): before = lax.ppermute(recordings[:, planes - margin:], 'gz', up)  3.24 us
    ppermute x1, starting transfers between devices, local(): lax.ppermute(keep[1] * core[1], 'view', [(i, i ^ 2) for i in range(4)])  2.82 us
  transfers between devices with their start and end apart: 7, of which 6 were waited for; matrix products, arithmetic and copies ran while one was open for 2% of the time, Pallas kernels for 21%

profile of v1, /device:TPU:24, one launch (start us, length us, event | category | flops | bytes accessed | tf_op | source)
XLA Modules:
  0.0 63.1 jit_solution(724779252401781210)
XLA Ops:
  0.0 0.0 copy-start.3
  0.0 2.4 %convert_element_type.3 = bf16[20,128,128]{2,1,0:T(8,128)(2,1)} convert(f32[20,128,128]{2,1,0:T(8,128)} %own_ref.1) | non-fusion elementwise | flops 327680 | bytes 1966080 | tf_op jit(solution)/shard_map/convert_element_type | solution.py:238
  2.4 0.0 copy-start.1
  2.4 3.9 %collective-permute-start.1 = (bf16[20,128,128]{2,1,0:T(8,128)(2,1)}, bf16[20,128,128]{2,1,0:T(8,128)(2,1)S(1)}, u32[]{:S(2)}, u32[]{:S(2)}) collective-permute-start(bf16[20,128,128]{2,1,0:T(8,128)(2,1)} %convert_element_type.3), channel_id=1, source_target_pairs={{0,4},{4,8},{8,12},{12,16},{16,20},{20,24},{24,28},{28,32},{32,36}... | collective-permute-start | bytes 1966088 | tf_op jit(solution)/shard_map/ppermute | solution.py:238
  6.3 0.0 copy-done.3
  6.3 1.2 %fusion.4 = (bf16[2,10,128,128]{3,2,1,0:T(8,128)(2,1)}, bf16[2,10,128,128]{3,2,1,0:T(8,128)(2,1)}) fusion(bf16[2,20,128,128]{3,2,1,0:T(8,128)(2,1)S(1)} %copy-done.3), kind=kLoop, calls=%fused_computation.6 | loop fusion | bytes 2621440 | tf_op jit(solution)/shard_map/slice | solution.py:255
  7.5 0.0 copy-start
  7.6 7.1 %collective-permute-start.4 = (bf16[2,10,128,128]{3,2,1,0:T(8,128)(2,1)}, bf16[2,10,128,128]{3,2,1,0:T(8,128)(2,1)S(1)}, u32[]{:S(2)}, u32[]{:S(2)}) collective-permute-start(bf16[2,10,128,128]{3,2,1,0:T(8,128)(2,1)} %get-tuple-element.23), channel_id=1, source_target_pairs={{4,0},{8,4},{12,8},{16,12},{20,16},{24,20},{28,24},{32,28},{36,32}... | collective-permute-start | bytes 1966088 | tf_op jit(solution)/shard_map/ppermute | solution.py:255
  14.6 1.9 %collective-permute-start = (bf16[2,10,128,128]{3,2,1,0:T(8,128)(2,1)}, bf16[2,10,128,128]{3,2,1,0:T(8,128)(2,1)S(1)}, u32[]{:S(2)}, u32[]{:S(2)}) collective-permute-start(bf16[2,10,128,128]{3,2,1,0:T(8,128)(2,1)} %get-tuple-element.24), channel_id=1, source_target_pairs={{0,4},{4,8},{8,12},{12,16},{16,20},{20,24},{24,28},{28,32},{32,36}... | collective-permute-start | bytes 1966088 | tf_op jit(solution)/shard_map/ppermute | solution.py:254
  16.6 0.0 copy-done.1
  16.6 2.8 %matrices.1 = (bf16[2,2,320,256]{3,2,1,0:T(8,128)(2,1)S(1)}, bf16[2,2,2,256,256]{4,3,2,1,0:T(8,128)(2,1)S(1)}, bf16[2,2,2,128,256]{4,3,2,1,0:T(8,128)(2,1)S(1)}) custom-call(s32[1]{0:T(128)} %bitcast.place_ref, f32[2,3,2,21]{3,2,1,0:T(2,128)S(1)} %copy-done.1), custom_call_target="tpu_custom_call" | custom-call | flops 1000000 | bytes 10000 | tf_op jit(solution)/shard_map/matrices/pallas_call | solution.py:241
  19.4 0.8 %collective-permute-done.1.mine_ref = bf16[20,128,128]{2,1,0:T(8,128)(2,1)S(1)} collective-permute-done((bf16[20,128,128]{2,1,0:T(8,128)(2,1)}, bf16[20,128,128]{2,1,0:T(8,128)(2,1)S(1)}, u32[]{:S(2)}, u32[]{:S(2)}) %collective-permute-start.1) | collective-permute-done | bytes 655392 | tf_op jit(solution)/shard_map/ppermute | solution.py:238
  20.2 1.3 %collective-permute-start.3 = (bf16[10,128,128]{2,1,0:T(8,128)(2,1)S(1)}, bf16[10,128,128]{2,1,0:T(8,128)(2,1)S(1)}, u32[]{:S(2)}, u32[]{:S(2)}) collective-permute-start(bf16[10,128,128]{2,1,0:T(8,128)(2,1)S(1)} %get-tuple-element.25), channel_id=1, source_target_pairs={{0,1},{1,0},{2,3},{3,2},{4,5},{5,4},{6,7},{7,6},{8,9},{9,8},{10,11... | collective-permute-start | bytes 983048 | tf_op jit(solution)/shard_map/ppermute | solution.py:257
  21.4 0.3 collective-permute-start.2
  21.7 1.0 %collective-permute-done.3.other_high_ref = bf16[10,128,128]{2,1,0:T(8,128)(2,1)S(1)} collective-permute-done((bf16[10,128,128]{2,1,0:T(8,128)(2,1)S(1)}, bf16[10,128,128]{2,1,0:T(8,128)(2,1)S(1)}, u32[]{:S(2)}, u32[]{:S(2)}) %collective-permute-start.3) | collective-permute-done | bytes 327712 | tf_op jit(solution)/shard_map/ppermute | solution.py:257
  22.7 0.5 collective-permute-done.2.other_low_ref
  23.2 0.0 copy-done
  23.2 10.3 %quotients.1 = (bf16[2,20,128,128]{3,2,1,0:T(8,128)(2,1)S(1)}, f32[2,2,10,128,128]{4,3,2,1,0:T(8,128)}) custom-call(s32[1]{0:T(128)} %bitcast.place_ref, bf16[20,128,128]{2,1,0:T(8,128)(2,1)S(1)} %collective-permute-done.1.mine_ref, bf16[10,128,128]{2,1,0:T(8,128)(2,1)S(1)} %collective-permute-done.2.other_low_ref, ...), custom_call_target="tpu_custom_call" | custom-call | flops 1000000 | bytes 10000 | tf_op jit(solution)/shard_map/quotients/pallas_call | solution.py:259
  33.4 0.0 collective-permute-done.4.refs_2_
  33.4 3.2 %collective-permute-done.refs_0_ = bf16[2,10,128,128]{3,2,1,0:T(8,128)(2,1)S(1)} collective-permute-done((bf16[2,10,128,128]{3,2,1,0:T(8,128)(2,1)}, bf16[2,10,128,128]{3,2,1,0:T(8,128)(2,1)S(1)}, u32[]{:S(2)}, u32[]{:S(2)}) %collective-permute-start) | collective-permute-done | bytes 655392 | tf_op jit(solution)/shard_map/ppermute | solution.py:254
  36.7 5.3 %correction.1.refs_4_ = f32[20,128,128]{2,1,0:T(8,128)S(1)} custom-call(bf16[2,10,128,128]{3,2,1,0:T(8,128)(2,1)S(1)} %collective-permute-done.refs_0_, bf16[2,20,128,128]{3,2,1,0:T(8,128)(2,1)S(1)} %get-tuple-element.19.refs_1_, bf16[2,10,128,128]{3,2,1,0:T(8,128)(2,1)S(1)} %collective-permute-done.4.refs_2_, ...), custom_call_target="tpu_custom_call" | custom-call | flops 4000000000 | bytes 5000000 | tf_op jit(solution)/shard_map/correction/pallas_call | solution.py:268
  41.9 0.0 copy-start.2
  42.0 1.1 %copy-done.2 = f32[20,128,128]{2,1,0:T(8,128)} copy-done((f32[20,128,128]{2,1,0:T(8,128)}, f32[20,128,128]{2,1,0:T(8,128)S(1)}, u32[]{:S(2)}) %copy-start.2) | copy-done | bytes 1310744
  43.0 5.6 %corrections.1 = (f32[2,20,32,128]{3,2,1,0:T(8,128)S(1)}, f32[2,20,32,128]{3,2,1,0:T(8,128)S(1)}) custom-call(bf16[2,10,128,128]{3,2,1,0:T(8,128)(2,1)S(1)} %collective-permute-done.refs_0_, bf16[2,20,128,128]{3,2,1,0:T(8,128)(2,1)S(1)} %get-tuple-element.19.refs_1_, bf16[2,10,128,128]{3,2,1,0:T(8,128)(2,1)S(1)} %collective-permute-done.4.refs_2_, ...), custom_call_target="tpu_custom_call" | custom-call | flops 4000000000 | bytes 5000000 | tf_op jit(solution)/shard_map/corrections/pallas_call | solution.py:278
  48.7 0.1 collective-permute-start.5
  48.8 2.1 %collective-permute-done.5 = f32[2,20,32,128]{3,2,1,0:T(8,128)S(1)} collective-permute-done((f32[2,20,32,128]{3,2,1,0:T(8,128)S(1)}, f32[2,20,32,128]{3,2,1,0:T(8,128)S(1)}, u32[]{:S(2)}, u32[]{:S(2)}) %collective-permute-start.5) | collective-permute-done | bytes 655392 | tf_op jit(solution)/shard_map/ppermute | solution.py:287
  50.9 2.8 %collective-permute-start.6 = (f32[20,32,128]{2,1,0:T(8,128)S(1)}, f32[20,32,128]{2,1,0:T(8,128)S(1)}, u32[]{:S(2)}, u32[]{:S(2)}) collective-permute-start(f32[20,32,128]{2,1,0:T(8,128)S(1)} %fusion), channel_id=1, source_target_pairs={{0,2},{1,3},{2,0},{3,1},{4,6},{5,7},{6,4},{7,5},{8,10},{9,11},{10,... | collective-permute-start | bytes 983048 | tf_op jit(solution)/shard_map/ppermute | solution.py:288
  53.7 8.5 %collective-permute-done.6 = f32[20,32,128]{2,1,0:T(8,128)S(1)} collective-permute-done((f32[20,32,128]{2,1,0:T(8,128)S(1)}, f32[20,32,128]{2,1,0:T(8,128)S(1)}, u32[]{:S(2)}, u32[]{:S(2)}) %collective-permute-start.6) | collective-permute-done | bytes 327712 | tf_op jit(solution)/shard_map/ppermute | solution.py:288
  62.2 0.8 %fusion.3 = f32[20,32,128]{2,1,0:T(8,128)} fusion(f32[20,32,128]{2,1,0:T(8,128)S(1)} %collective-permute-done.6, f32[2,20,32,128]{3,2,1,0:T(8,128)S(1)} %collective-permute-done.5, f32[2,20,32,128]{3,2,1,0:T(8,128)S(1)} %get-tuple-element.21, f32[20,128,128]{2,1,0:T(8,128)S(1)} %copy-done, s32[]{:T(128)S(6)} %select_n.3), kind=kLoop, calls=%fused_computation.5 | loop fusion | flops 245760 | bytes 1638404 | tf_op jit(solution)/shard_map/mul | solution.py:290
  (2 shorter events, 0.1 us)
Async XLA Ops:
  0.0 6.3 %copy-start.3 = (bf16[2,20,128,128]{3,2,1,0:T(8,128)(2,1)S(1)}, bf16[2,20,128,128]{3,2,1,0:T(8,128)(2,1)}, u32[]{:S(2)}) copy-start(bf16[2,20,128,128]{3,2,1,0:T(8,128)(2,1)} %rec_ref.1) | copy-start | bytes 3932164
  2.4 14.2 %copy-start.1 = (f32[2,3,2,21]{3,2,1,0:T(2,128)S(1)}, f32[2,3,2,21]{3,2,1,0:T(2,128)}, u32[]{:S(2)}) copy-start(f32[2,3,2,21]{3,2,1,0:T(2,128)} %taps_ref.1) | copy-start | bytes 3028
  2.4 17.8 %collective-permute-start.1 = (bf16[20,128,128]{2,1,0:T(8,128)(2,1)}, bf16[20,128,128]{2,1,0:T(8,128)(2,1)S(1)}, u32[]{:S(2)}, u32[]{:S(2)}) collective-permute-start(bf16[20,128,128]{2,1,0:T(8,128)(2,1)} %convert_element_type.3), channel_id=1, source_target_pairs={{0,4},{4,8},{8,12},{12,16},{16,20},{20,24},{24,28},{28,32},{32,36}... | collective-permute-start | bytes 1966088 | tf_op jit(solution)/shard_map/ppermute | solution.py:238
  7.5 15.6 %copy-start = (f32[20,128,128]{2,1,0:T(8,128)S(1)}, f32[20,128,128]{2,1,0:T(8,128)}, u32[]{:S(2)}) copy-start(f32[20,128,128]{2,1,0:T(8,128)} %own_ref.1) | copy-start | bytes 3932164
  7.6 25.9 %collective-permute-start.4 = (bf16[2,10,128,128]{3,2,1,0:T(8,128)(2,1)}, bf16[2,10,128,128]{3,2,1,0:T(8,128)(2,1)S(1)}, u32[]{:S(2)}, u32[]{:S(2)}) collective-permute-start(bf16[2,10,128,128]{3,2,1,0:T(8,128)(2,1)} %get-tuple-element.23), channel_id=1, source_target_pairs={{4,0},{8,4},{12,8},{16,12},{20,16},{24,20},{28,24},{32,28},{36,32}... | collective-permute-start | bytes 1966088 | tf_op jit(solution)/shard_map/ppermute | solution.py:255
  14.6 22.0 %collective-permute-start = (bf16[2,10,128,128]{3,2,1,0:T(8,128)(2,1)}, bf16[2,10,128,128]{3,2,1,0:T(8,128)(2,1)S(1)}, u32[]{:S(2)}, u32[]{:S(2)}) collective-permute-start(bf16[2,10,128,128]{3,2,1,0:T(8,128)(2,1)} %get-tuple-element.24), channel_id=1, source_target_pairs={{0,4},{4,8},{8,12},{12,16},{16,20},{20,24},{24,28},{28,32},{32,36}... | collective-permute-start | bytes 1966088 | tf_op jit(solution)/shard_map/ppermute | solution.py:254
  20.2 2.5 %collective-permute-start.3 = (bf16[10,128,128]{2,1,0:T(8,128)(2,1)S(1)}, bf16[10,128,128]{2,1,0:T(8,128)(2,1)S(1)}, u32[]{:S(2)}, u32[]{:S(2)}) collective-permute-start(bf16[10,128,128]{2,1,0:T(8,128)(2,1)S(1)} %get-tuple-element.25), channel_id=1, source_target_pairs={{0,1},{1,0},{2,3},{3,2},{4,5},{5,4},{6,7},{7,6},{8,9},{9,8},{10,11... | collective-permute-start | bytes 983048 | tf_op jit(solution)/shard_map/ppermute | solution.py:257
  21.4 1.7 %collective-permute-start.2 = (bf16[10,128,128]{2,1,0:T(8,128)(2,1)S(1)}, bf16[10,128,128]{2,1,0:T(8,128)(2,1)S(1)}, u32[]{:S(2)}, u32[]{:S(2)}) collective-permute-start(bf16[10,128,128]{2,1,0:T(8,128)(2,1)S(1)} %get-tuple-element.26), channel_id=1, source_target_pairs={{0,1},{1,0},{2,3},{3,2},{4,5},{5,4},{6,7},{7,6},{8,9},{9,8},{10,11... | collective-permute-start | bytes 983048 | tf_op jit(solution)/shard_map/ppermute | solution.py:257
  41.9 1.1 %copy-start.2 = (f32[20,128,128]{2,1,0:T(8,128)}, f32[20,128,128]{2,1,0:T(8,128)S(1)}, u32[]{:S(2)}) copy-start(f32[20,128,128]{2,1,0:T(8,128)S(1)} %correction.1.refs_4_) | copy-start | bytes 3932164
  48.7 2.2 %collective-permute-start.5 = (f32[2,20,32,128]{3,2,1,0:T(8,128)S(1)}, f32[2,20,32,128]{3,2,1,0:T(8,128)S(1)}, u32[]{:S(2)}, u32[]{:S(2)}) collective-permute-start(f32[2,20,32,128]{3,2,1,0:T(8,128)S(1)} %get-tuple-element.22), channel_id=1, source_target_pairs={{0,1},{1,0},{2,3},{3,2},{4,5},{5,4},{6,7},{7,6},{8,9},{9,8},{10,11... | collective-permute-start | bytes 1966088 | tf_op jit(solution)/shard_map/ppermute | solution.py:287
  50.9 11.3 %collective-permute-start.6 = (f32[20,32,128]{2,1,0:T(8,128)S(1)}, f32[20,32,128]{2,1,0:T(8,128)S(1)}, u32[]{:S(2)}, u32[]{:S(2)}) collective-permute-start(f32[20,32,128]{2,1,0:T(8,128)S(1)} %fusion), channel_id=1, source_target_pairs={{0,2},{1,3},{2,0},{3,1},{4,6},{5,7},{6,4},{7,5},{8,10},{9,11},{10,... | collective-permute-start | bytes 983048 | tf_op jit(solution)/shard_map/ppermute | solution.py:288

commit v2 on v1

--- a/solution.py
+++ b/solution.py
@@ -101,7 +101,23 @@
     return jnp.dot(a, b, preferred_element_type=F32)
 
 
-def filter_to(load, views, groups, z_ref, x_ref, y_ref, g_ref, exact, emit):
+STACK_Z, STACK_Y, CHUNK = True, True, 4
+
+
+def inverted(value):
+    guess = pl.reciprocal(value, approx=True)
+    return guess * (2.0 - value * guess)
+
+
+def both_halves(ref, depth, data, stacked):
+    if stacked:
+        rows = ref.shape[1]
+        out = dot(ref[:, :, :depth].reshape(2 * rows, depth), data)
+        return out[:rows] + out[rows:]
+    return dot(ref[0, :, :depth], data) + dot(ref[1, :, :depth], data)
+
+
+def filter_to(load, views, groups, z_ref, x_ref, y_ref, e_ref, g_ref, exact, emit):
     tall = z_ref.shape[1] // (2 * views)
     z_out = tall // 8
     rows = y_ref.shape[2]
@@ -113,22 +129,29 @@
         octets = jnp.concatenate(octets, axis=1)
         for part in range(groups):
             data = octets[part * z_out * 8 : part * z_out * 8 + depth]
-            all_e = dot(z_ref[0, :, :depth], data) + dot(z_ref[1, :, :depth], data)
+            all_e = both_halves(z_ref, depth, data, STACK_Z)
             for v in range(views):
-                e = all_e[v * 2 * tall : (v + 1) * 2 * tall]
-                e = jnp.concatenate(
-                    [
-                        jnp.concatenate([e[:tall, o * rows : (o + 1) * rows], e[tall:, o * rows : (o + 1) * rows]], axis=1)
-                        for o in range(2)
-                    ],
-                    axis=0,
-                )
-                if exact:
-                    high, low = split(e)
-                    g = dot(high, x_ref[v, 0]) + dot(high, x_ref[v, 1]) + dot(low, x_ref[v, 0])
-                else:
-                    high = e.astype(BF16)
-                    g = dot(high, x_ref[v, 0]) + dot(high, x_ref[v, 1])
+                for r in range(2):
+                    top = (2 * v + r) * tall
+                    e = all_e[top : top + tall]
+                    e = jnp.concatenate([e[:, :rows], e[:, rows:]], axis=0)
+                    lanes = slice(r * rows, (r + 1) * rows)
+                    if exact:
+                        high, low = split(e)
+                        e_ref[v, 0, pair * groups + part, :, lanes] = high
+                        e_ref[v, 1, pair * groups + part, :, lanes] = low
+                    else:
+                        e_ref[v, 0, pair * groups + part, :, lanes] = e.astype(BF16)
+    for v in range(views):
+        for first in range(0, rows // 16 * groups, CHUNK):
+            e = e_ref[v, 0, first : first + CHUNK].reshape(CHUNK * 2 * tall, 2 * rows)
+            all_g = dot(e, x_ref[v, 0]) + dot(e, x_ref[v, 1])
+            if exact:
+                e = e_ref[v, 1, first : first + CHUNK].reshape(CHUNK * 2 * tall, 2 * rows)
+                all_g = all_g + dot(e, x_ref[v, 0])
+            for index in range(first, first + CHUNK):
+                pair, part = index // groups, index % groups
+                g = all_g[(index - first) * 2 * tall : (index - first + 1) * 2 * tall]
                 for r in range(2):
                     lanes = slice(r * rows, (r + 1) * rows)
                     g_rows = jnp.concatenate(
@@ -145,7 +168,7 @@
     for v in range(views):
         for z in range(0, groups * z_out, 2):
             data = jnp.concatenate([g_ref[v, 0, z], g_ref[v, 0, z + 1]], axis=1)
-            out = dot(y_ref[v, 0], data) + dot(y_ref[v, 1], data)
+            out = both_halves(y_ref.at[v], 2 * rows, data, STACK_Y)
             if exact:
                 data = jnp.concatenate([g_ref[v, 1, z], g_ref[v, 1, z + 1]], axis=1)
                 out = out + dot(y_ref[v, 0], data)
@@ -153,7 +176,24 @@
             emit(v, z + 1, out[:, rows:])
 
 
-def quotient_kernel(place_ref, mine_ref, other_low_ref, other_high_ref, own_ref, rec_ref, z_ref, x_ref, y_ref, own_out, rim_out, g_ref):
+def scratch(views, groups, halves, z_out, rows, cols):
+    return [
+        pltpu.VMEM((views, halves, rows // 16 * groups, 2 * z_out * 8, 2 * cols), BF16),
+        pltpu.VMEM((views, halves, groups * z_out, 2 * rows, cols), BF16),
+    ]
+
+
+def prepare_kernel(est_ref, rec_ref, est_out, last_out, first_out):
+    margin = last_out.shape[1]
+    planes = est_ref.shape[0]
+    est_out[...] = est_ref[...].astype(BF16)
+    last_out[...] = rec_ref[:, planes - margin :]
+    first_out[...] = rec_ref[:, :margin]
+
+
+def quotient_kernel(
+    place_ref, mine_ref, other_low_ref, other_high_ref, own_ref, rec_ref, z_ref, x_ref, y_ref, own_out, rim_out, e_ref, g_ref
+):
     planes = own_ref.shape[0]
     margin = rim_out.shape[2]
     first_core = place_ref[0] % 2 == 0
@@ -162,62 +202,47 @@
         mine = mine_ref[:, at, :].astype(F32)
         other = jnp.concatenate([ref[:, at, :].astype(F32) for ref in (other_low_ref, other_high_ref)], axis=0)
         before, after = jnp.where(first_core, mine, other), jnp.where(first_core, other, mine)
-        return jnp.concatenate([before, own_ref[:, at, :], after], axis=0)
+        return jnp.concatenate([before, own_ref[:, at, :].astype(F32), after], axis=0)
 
     def emit(v, z, blurred):
+        inverse = inverted(blurred)
         if z < margin:
-            rim_out[v, 0, z] = blurred
+            rim_out[v, 0, z] = inverse
         elif z < margin + planes:
-            own_out[v, z - margin] = (rec_ref[v, z - margin].astype(F32) / blurred).astype(BF16)
+            own_out[v, z - margin] = (rec_ref[v, z - margin].astype(F32) * inverse).astype(BF16)
         else:
-            rim_out[v, 1, z - margin - planes] = blurred
+            rim_out[v, 1, z - margin - planes] = inverse
 
     groups = (planes + 2 * margin) // (planes // 2)
-    filter_to(load, rec_ref.shape[0], groups, z_ref.at[0], x_ref.at[0], y_ref.at[0], g_ref, False, emit)
-
-
-def correction(v, before_ref, own_ref, after_ref, rim_ref, z_ref, x_ref, y_ref, g_ref, emit):
-    def load(at):
-        before = before_ref[v, :, at, :].astype(F32) / rim_ref[v, 0, :, at, :]
-        after = after_ref[v, :, at, :].astype(F32) / rim_ref[v, 1, :, at, :]
-        return jnp.concatenate([before, own_ref[v, :, at, :].astype(F32), after], axis=0)
-
-    tall = z_ref.shape[2] // own_ref.shape[0]
-    filter_to(
-        load,
-        1,
-        2,
-        z_ref.at[1, :, v * tall : (v + 1) * tall],
-        x_ref.at[1, v : v + 1],
-        y_ref.at[1, v : v + 1],
-        g_ref,
-        True,
-        emit,
-    )
-
-
-def first_correction_kernel(v, before_ref, own_ref, after_ref, rim_ref, z_ref, x_ref, y_ref, out_ref, g_ref):
-    def emit(_, z, value):
-        out_ref[z] = value
-
-    correction(v, before_ref, own_ref, after_ref, rim_ref, z_ref, x_ref, y_ref, g_ref, emit)
-
-
-def last_correction_kernel(
-    v, before_ref, own_ref, after_ref, rim_ref, earlier_ref, z_ref, x_ref, y_ref, keep_ref, send_ref, g_ref
-):
+    filter_to(load, rec_ref.shape[0], groups, z_ref.at[0], x_ref.at[0], y_ref.at[0], e_ref, g_ref, False, emit)
+
+
+def correction_kernel(before_ref, own_ref, after_ref, rim_ref, z_ref, x_ref, y_ref, keep_ref, send_ref, e_ref, g_ref, earlier_ref):
+    views = own_ref.shape[0]
     part = keep_ref.shape[2]
-
-    def emit(_, z, value):
-        product = value * earlier_ref[z]
-        for b in range(4):
-            rows = product[b * part : (b + 1) * part]
-            if b % 2 == 0:
-                keep_ref[b // 2, z] = rows
-            else:
-                send_ref[b // 2, z] = rows
-
-    correction(v, before_ref, own_ref, after_ref, rim_ref, z_ref, x_ref, y_ref, g_ref, emit)
+    tall = z_ref.shape[2] // views
+    for v in range(views):
+
+        def load(at, v=v):
+            before = before_ref[v, :, at, :].astype(F32) * rim_ref[v, 0, :, at, :]
+            after = after_ref[v, :, at, :].astype(F32) * rim_ref[v, 1, :, at, :]
+            return jnp.concatenate([before, own_ref[v, :, at, :].astype(F32), after], axis=0)
+
+        def emit(_, z, value, v=v):
+            if v > 0:
+                value = value * earlier_ref[z]
+            if v < views - 1:
+                earlier_ref[z] = value
+                return
+            for b in range(4):
+                rows = value[b * part : (b + 1) * part]
+                if b % 2 == 0:
+                    keep_ref[b // 2, z] = rows
+                else:
+                    send_ref[b // 2, z] = rows
+
+        z_view = z_ref.at[1, :, v * tall : (v + 1) * tall]
+        filter_to(load, 1, 2, z_view, x_ref.at[1, v : v + 1], y_ref.at[1, v : v + 1], e_ref, g_ref, True, emit)
 
 
 def local(estimate, recordings, psf_taps):
@@ -232,11 +257,20 @@
     down = [(i + 1, i) for i in range(devices - 1)]
     swap = [(i, i ^ 1) for i in range(4)]
     z_out = planes // 2
-
+    shape = jax.ShapeDtypeStruct
+
+    rounded, last, first = pl.pallas_call(
+        prepare_kernel,
+        out_shape=[shape((planes, rows, cols), BF16)] + [shape((views, margin, rows, cols), BF16)] * 2,
+        in_specs=[VMEM] * 2,
+        out_specs=[VMEM] * 3,
+        name="prepare",
+        **params(10**6, 10**4),
+    )(estimate, recordings)
     both_ways = [(4 * i + w, 4 * j + w) for w in (0, 2) for i, j in up]
     both_ways += [(4 * i + w, 4 * j + w) for w in (1, 3) for i, j in down]
-    mine = lax.ppermute(estimate.astype(BF16), ("gz", "view"), both_ways)
-    shape = jax.ShapeDtypeStruct
+    mine = lax.ppermute(rounded, ("gz", "view"), both_ways)
+
     wide = -(-(z_out + taps - 1) * 8 // 128) * 128
     z_mat, x_mat, y_mat = pl.pallas_call(
         matrices_kernel,
@@ -251,8 +285,8 @@
         **params(10**6, 10**4),
     )(place_array, psf_taps)
 
-    before = lax.ppermute(recordings[:, planes - margin :], "gz", up)
-    after = lax.ppermute(recordings[:, :margin], "gz", down)
+    before = lax.ppermute(last, "gz", up)
+    after = lax.ppermute(first, "gz", down)
     mine, z_mat = lax.optimization_barrier((mine, z_mat))
     other = [lax.ppermute(part, "view", swap) for part in (mine[:margin], mine[margin:])]
 
@@ -261,33 +295,29 @@
         out_shape=[shape((views, planes, rows, cols), BF16), shape((views, 2, margin, rows, cols), F32)],
         in_specs=[SMEM] + [VMEM] * 8,
         out_specs=[VMEM] * 2,
-        scratch_shapes=[pltpu.VMEM((views, 1, planes + 2 * margin, 2 * rows, cols), BF16)],
+        scratch_shapes=scratch(views, 4, 1, z_out, rows, cols),
         name="quotients",
         **params(10**6, 10**4),
-    )(place_array, mine, *other, estimate, recordings, z_mat, x_mat, y_mat)
-    product = pl.pallas_call(
-        lambda *refs: first_correction_kernel(0, *refs),
-        out_shape=shape((planes, rows, cols), F32),
+    )(place_array, mine, *other, rounded, recordings, z_mat, x_mat, y_mat)
+    part = rows // 4
+    keep, send = pl.pallas_call(
+        correction_kernel,
+        out_shape=[shape((2, planes, part, cols), F32)] * 2,
         in_specs=[VMEM] * 7,
-        out_specs=VMEM,
-        scratch_shapes=[pltpu.VMEM((1, 2, planes, 2 * rows, cols), BF16)],
-        name="correction",
+        out_specs=[VMEM] * 2,
+        scratch_shapes=scratch(1, 2, 2, z_out, rows, cols) + [pltpu.VMEM((planes, rows, cols), F32)],
+        name="corrections",
         **params(4 * 10**9, 5 * 10**6),
     )(before, own, after, rim, z_mat, x_mat, y_mat)
-    part = rows // 4
-    keep, send = pl.pallas_call(
-        lambda *refs: last_correction_kernel(1, *refs),
-        out_shape=[shape((2, planes, part, cols), F32)] * 2,
-        in_specs=[VMEM] * 8,
-        out_specs=[VMEM] * 2,
-        scratch_shapes=[pltpu.VMEM((1, 2, planes, 2 * rows, cols), BF16)],
-        name="corrections",
-        **params(4 * 10**9, 5 * 10**6),
-    )(before, own, after, rim, product, z_mat, x_mat, y_mat)
     core = lax.ppermute(send, "view", swap)
-    across = lax.ppermute(keep[1] * core[1], "view", [(i, i ^ 2) for i in range(4)])
+    product = keep[1] * core[1]
+    most = jnp.maximum(jnp.max(product), 1e-30)
+    exponent = jnp.floor(jnp.log2(most)) - 14.0
+    coded = (product * jnp.exp2(-exponent)).astype(jnp.float16)
+    tail = jnp.broadcast_to(exponent.astype(jnp.float16), (1, part, cols))
+    across = lax.ppermute(jnp.concatenate([coded, tail]), "view", [(i, i ^ 2) for i in range(4)]).astype(F32)
     mine = lax.dynamic_slice_in_dim(estimate, place * part, part, 1)
-    return mine * (keep[0] * core[0]) * across
+    return mine * (keep[0] * core[0]) * (across[:planes] * jnp.exp2(across[planes:, :1, :1]))
 
 
 def solution(mesh):

time: 63.4 us -> 56.9 us (0.90)
  Pallas kernels: 23.9 us -> 19.7 us
  waiting for transfers between devices: 16.1 us -> 12.1 us
  between operations: 0.09 us -> 1.51 us
  local copies, waits for them, and re-layouts: 2.32 us -> 3.24 us
    pallas_call x2, Pallas kernels: 10.9 us -> 7.04 us  [the longest x1 6.89 us: local(): pl.pallas_call(correction_kernel, out_shape=[shape((2, planes, part, cols...]
    ppermute x4, waiting for transfers between devices: 12.5 us -> 8.76 us  [the longest x1 5.28 us: local(): lax.ppermute(jnp.concatenate([coded, tail]), 'view', [(i, i ^ 2) for i in...]
    convert_element_type x1 -> x2, other arithmetic: 2.37 us -> 0.09 us  [the longest x1 0.06 us: local(): coded = (product * jnp.exp2(-exponent)).astype(jnp.float16)]
    unnamed x8 -> x6, local copies, waits for them, and re-layouts: 1.06 us -> 2.64 us
    mul x2 -> x1, other arithmetic: 0.88 us -> 1.83 us  [local(): mine * (keep[0] * core[0])]
    reduce_max x0 -> x1, other arithmetic: none -> 0.71 us  [local(): most = jnp.maximum(jnp.max(product), 1e-30)]
    slice x1, local copies, waits for them, and re-layouts: 1.21 us -> 0.52 us  [local(): across[planes:, :1, :1]]
  transfers between devices with their start and end apart: 7 -> 7, of which waited for: 6 -> 6; matrix products, arithmetic and copies ran while one was open for 2% -> 0% of each run, Pallas kernels for 21% -> 23%
where the time goes in v2:
time: 56.9 us; the launch traced here: 56.1 us
  Pallas kernels  19.7 us (35%)
  starting transfers between devices  16.9 us (30%)
  waiting for transfers between devices  12.1 us (21%)
  local copies, waits for them, and re-layouts  3.24 us (6%)
  other arithmetic  2.63 us (5%)
  between operations  1.51 us (3%)
    pallas_call x1, Pallas kernels, local(): pl.pallas_call(quotient_kernel, out_shape=[shape((views, planes, rows, co...  9.91 us
    pallas_call x1, Pallas kernels, local(): pl.pallas_call(correction_kernel, out_shape=[shape((2, planes, part, cols...  6.89 us
    ppermute x1, waiting for transfers between devices, local(): lax.ppermute(jnp.concatenate([coded, tail]), 'view', [(i, i ^ 2) for i in...  5.28 us
    ppermute x1, starting transfers between devices, local(): after = lax.ppermute(first, 'gz', down)  5.06 us
    ppermute x1, starting transfers between devices, local(): before = lax.ppermute(last, 'gz', up)  3.83 us
    ppermute x1, starting transfers between devices, local(): mine = lax.ppermute(rounded, ('gz', 'view'), both_ways)  3.83 us
    ppermute x1, waiting for transfers between devices, local(): mine = lax.ppermute(rounded, ('gz', 'view'), both_ways)  3.33 us
    ppermute x1, starting transfers between devices, local(): lax.ppermute(jnp.concatenate([coded, tail]), 'view', [(i, i ^ 2) for i in...  2.81 us
  transfers between devices with their start and end apart: 7, of which 6 were waited for; matrix products, arithmetic and copies ran while one was open for 0% of the time, Pallas kernels for 23%

profile of v2, /device:TPU:24, one launch (start us, length us, event | category | flops | bytes accessed | tf_op | source)
XLA Modules:
  0.0 56.1 jit_solution(17021234752007382503)
XLA Ops:
  0.0 0.0 copy-start
  0.0 1.3 %copy-done = bf16[2,20,128,128]{3,2,1,0:T(8,128)(2,1)S(1)} copy-done((bf16[2,20,128,128]{3,2,1,0:T(8,128)(2,1)S(1)}, bf16[2,20,128,128]{3,2,1,0:T(8,128)(2,1)}, u32[]{:S(2)}) %copy-start) | copy-done | bytes 1310744
  1.3 0.0 copy-start.1
  1.3 1.3 %copy-done.1 = f32[20,128,128]{2,1,0:T(8,128)S(1)} copy-done((f32[20,128,128]{2,1,0:T(8,128)S(1)}, f32[20,128,128]{2,1,0:T(8,128)}, u32[]{:S(2)}) %copy-start.1) | copy-done | bytes 1310744
  2.6 0.0 copy-start.2
  2.6 0.1 prepare.1
  2.8 3.8 %collective-permute-start.1 = (bf16[20,128,128]{2,1,0:T(8,128)(2,1)S(1)}, bf16[20,128,128]{2,1,0:T(8,128)(2,1)S(1)}, u32[]{:S(2)}, u32[]{:S(2)}) collective-permute-start(bf16[20,128,128]{2,1,0:T(8,128)(2,1)S(1)} %get-tuple-element.18.own_ref), channel_id=1, source_target_pairs={{0,4},{4,8},{8,12},{12,16},{16,20},{20,24},{24,28},{28,32},{32,36}... | collective-permute-start | bytes 1966088 | tf_op jit(solution)/shard_map/ppermute | solution.py:272
  6.6 3.8 %collective-permute-start = (bf16[2,10,128,128]{3,2,1,0:T(8,128)(2,1)S(1)}, bf16[2,10,128,128]{3,2,1,0:T(8,128)(2,1)S(1)}, u32[]{:S(2)}, u32[]{:S(2)}) collective-permute-start(bf16[2,10,128,128]{3,2,1,0:T(8,128)(2,1)S(1)} %get-tuple-element.17), channel_id=1, source_target_pairs={{0,4},{4,8},{8,12},{12,16},{16,20},{20,24},{24,28},{28,32},{32,36}... | collective-permute-start | bytes 1966088 | tf_op jit(solution)/shard_map/ppermute | solution.py:288
  10.5 5.1 %collective-permute-start.4 = (bf16[2,10,128,128]{3,2,1,0:T(8,128)(2,1)S(1)}, bf16[2,10,128,128]{3,2,1,0:T(8,128)(2,1)}, u32[]{:S(2)}, u32[]{:S(2)}) collective-permute-start(bf16[2,10,128,128]{3,2,1,0:T(8,128)(2,1)S(1)} %get-tuple-element.25), channel_id=1, source_target_pairs={{4,0},{8,4},{12,8},{16,12},{20,16},{24,20},{28,24},{32,28},{36,32}... | collective-permute-start | bytes 1966088 | tf_op jit(solution)/shard_map/ppermute | solution.py:289
  15.5 0.0 copy-done.2
  15.5 2.8 %matrices.1 = (bf16[2,2,320,256]{3,2,1,0:T(8,128)(2,1)S(1)}, bf16[2,2,2,256,256]{4,3,2,1,0:T(8,128)(2,1)S(1)}, bf16[2,2,2,128,256]{4,3,2,1,0:T(8,128)(2,1)S(1)}) custom-call(s32[1]{0:T(128)} %bitcast.place_ref, f32[2,3,2,21]{3,2,1,0:T(2,128)S(1)} %copy-done.2), custom_call_target="tpu_custom_call" | custom-call | flops 1000000 | bytes 10000 | tf_op jit(solution)/shard_map/matrices/pallas_call | solution.py:275
  18.3 3.3 %collective-permute-done.1.mine_ref = bf16[20,128,128]{2,1,0:T(8,128)(2,1)S(1)} collective-permute-done((bf16[20,128,128]{2,1,0:T(8,128)(2,1)S(1)}, bf16[20,128,128]{2,1,0:T(8,128)(2,1)S(1)}, u32[]{:S(2)}, u32[]{:S(2)}) %collective-permute-start.1) | collective-permute-done | bytes 655392 | tf_op jit(solution)/shard_map/ppermute | solution.py:272
  21.7 0.8 %collective-permute-start.2 = (bf16[10,128,128]{2,1,0:T(8,128)(2,1)S(1)}, bf16[10,128,128]{2,1,0:T(8,128)(2,1)S(1)}, u32[]{:S(2)}, u32[]{:S(2)}) collective-permute-start(bf16[10,128,128]{2,1,0:T(8,128)(2,1)S(1)} %get-tuple-element.30), channel_id=1, source_target_pairs={{0,1},{1,0},{2,3},{3,2},{4,5},{5,4},{6,7},{7,6},{8,9},{9,8},{10,11... | collective-permute-start | bytes 983048 | tf_op jit(solution)/shard_map/ppermute | solution.py:291
  22.5 0.3 collective-permute-start.3
  22.8 1.0 %collective-permute-done.2.other_low_ref = bf16[10,128,128]{2,1,0:T(8,128)(2,1)S(1)} collective-permute-done((bf16[10,128,128]{2,1,0:T(8,128)(2,1)S(1)}, bf16[10,128,128]{2,1,0:T(8,128)(2,1)S(1)}, u32[]{:S(2)}, u32[]{:S(2)}) %collective-permute-start.2) | collective-permute-done | bytes 327712 | tf_op jit(solution)/shard_map/ppermute | solution.py:291
  23.7 0.5 collective-permute-done.3.other_high_ref
  24.2 9.9 %quotients.1 = (bf16[2,20,128,128]{3,2,1,0:T(8,128)(2,1)S(1)}, f32[2,2,10,128,128]{4,3,2,1,0:T(8,128)}) custom-call(s32[1]{0:T(128)} %bitcast.place_ref, bf16[20,128,128]{2,1,0:T(8,128)(2,1)S(1)} %collective-permute-done.1.mine_ref, bf16[10,128,128]{2,1,0:T(8,128)(2,1)S(1)} %collective-permute-done.2.other_low_ref, ...), custom_call_target="tpu_custom_call" | custom-call | flops 1000000 | bytes 10000 | tf_op jit(solution)/shard_map/quotients/pallas_call | solution.py:293
  34.1 0.2 collective-permute-done.before_ref
  34.3 0.0 collective-permute-done.4.after_ref
  34.3 6.9 %corrections.1 = (f32[2,20,32,128]{3,2,1,0:T(8,128)S(1)}, f32[2,20,32,128]{3,2,1,0:T(8,128)S(1)}) custom-call(bf16[2,10,128,128]{3,2,1,0:T(8,128)(2,1)S(1)} %collective-permute-done.before_ref, bf16[2,20,128,128]{3,2,1,0:T(8,128)(2,1)S(1)} %get-tuple-element.24.own_ref, bf16[2,10,128,128]{3,2,1,0:T(8,128)(2,1)} %collective-permute-done.4.after_ref, ...), custom_call_target="tpu_custom_call" | custom-call | flops 4000000000 | bytes 5000000 | tf_op jit(solution)/shard_map/corrections/pallas_call | solution.py:303
  41.2 0.3 collective-permute-start.5
  41.5 1.9 %collective-permute-done.5 = f32[2,20,32,128]{3,2,1,0:T(8,128)S(1)} collective-permute-done((f32[2,20,32,128]{3,2,1,0:T(8,128)S(1)}, f32[2,20,32,128]{3,2,1,0:T(8,128)S(1)}, u32[]{:S(2)}, u32[]{:S(2)}) %collective-permute-start.5) | collective-permute-done | bytes 655392 | tf_op jit(solution)/shard_map/ppermute | solution.py:312
  43.3 0.7 %fusion.4 = f32[]{:T(128)} fusion(f32[2,20,32,128]{3,2,1,0:T(8,128)S(1)} %collective-permute-done.5, f32[2,20,32,128]{3,2,1,0:T(8,128)S(1)} %get-tuple-element.27), kind=kLoop, calls=%fused_computation.8 | loop fusion | flops 163839 | bytes 655364 | tf_op jit(solution)/shard_map/reduce_max | solution.py:314
  44.8 0.1 fusion.3
  44.9 2.8 %collective-permute-start.6 = (f16[21,32,128]{2,1,0:T(8,128)(2,1)S(1)}, f16[21,32,128]{2,1,0:T(8,128)(2,1)S(1)}, u32[]{:S(2)}, u32[]{:S(2)}) collective-permute-start(f16[21,32,128]{2,1,0:T(8,128)(2,1)S(1)} %concatenate.3), channel_id=1, source_target_pairs={{0,2},{1,3},{2,0},{3,1},{4,6},{5,7},{6,4},{7,5},{8,10},{9,11},{10,... | collective-permute-start | bytes 516104 | tf_op jit(solution)/shard_map/ppermute | solution.py:318
  47.7 5.3 %collective-permute-done.6 = f16[21,32,128]{2,1,0:T(8,128)(2,1)S(1)} collective-permute-done((f16[21,32,128]{2,1,0:T(8,128)(2,1)S(1)}, f16[21,32,128]{2,1,0:T(8,128)(2,1)S(1)}, u32[]{:S(2)}, u32[]{:S(2)}) %collective-permute-start.6) | collective-permute-done | bytes 172064 | tf_op jit(solution)/shard_map/ppermute | solution.py:318
  53.0 0.5 slice.35
  54.2 1.8 %fusion = f32[20,32,128]{2,1,0:T(8,128)} fusion(f32[21,32,128]{2,1,0:T(8,128)S(1)} %convert_element_type.15, f32[2,20,32,128]{3,2,1,0:T(8,128)S(1)} %collective-permute-done.5, f32[2,20,32,128]{3,2,1,0:T(8,128)S(1)} %get-tuple-element.27, f32[20,128,128]{2,1,0:T(8,128)} %est_ref.1, s32[]{:T(128)S(6)} %select_n.3, f32[]{:T(128)} %bitcast.3), kind=kLoop, calls=%fused_computation.1 | loop fusion | flops 327680 | bytes 1638408 | tf_op jit(solution)/shard_map/mul | solution.py:320
  (3 shorter events, 0.1 us)
Async XLA Ops:
  0.0 1.3 %copy-start = (bf16[2,20,128,128]{3,2,1,0:T(8,128)(2,1)S(1)}, bf16[2,20,128,128]{3,2,1,0:T(8,128)(2,1)}, u32[]{:S(2)}) copy-start(bf16[2,20,128,128]{3,2,1,0:T(8,128)(2,1)} %rec_ref.3) | copy-start | bytes 3932164
  1.3 1.3 %copy-start.1 = (f32[20,128,128]{2,1,0:T(8,128)S(1)}, f32[20,128,128]{2,1,0:T(8,128)}, u32[]{:S(2)}) copy-start(f32[20,128,128]{2,1,0:T(8,128)} %est_ref.1) | copy-start | bytes 3932164
  2.6 12.9 %copy-start.2 = (f32[2,3,2,21]{3,2,1,0:T(2,128)S(1)}, f32[2,3,2,21]{3,2,1,0:T(2,128)}, u32[]{:S(2)}) copy-start(f32[2,3,2,21]{3,2,1,0:T(2,128)} %taps_ref.1) | copy-start | bytes 3028
  2.8 18.9 %collective-permute-start.1 = (bf16[20,128,128]{2,1,0:T(8,128)(2,1)S(1)}, bf16[20,128,128]{2,1,0:T(8,128)(2,1)S(1)}, u32[]{:S(2)}, u32[]{:S(2)}) collective-permute-start(bf16[20,128,128]{2,1,0:T(8,128)(2,1)S(1)} %get-tuple-element.18.own_ref), channel_id=1, source_target_pairs={{0,4},{4,8},{8,12},{12,16},{16,20},{20,24},{24,28},{28,32},{32,36}... | collective-permute-start | bytes 1966088 | tf_op jit(solution)/shard_map/ppermute | solution.py:272
  6.6 27.6 %collective-permute-start = (bf16[2,10,128,128]{3,2,1,0:T(8,128)(2,1)S(1)}, bf16[2,10,128,128]{3,2,1,0:T(8,128)(2,1)S(1)}, u32[]{:S(2)}, u32[]{:S(2)}) collective-permute-start(bf16[2,10,128,128]{3,2,1,0:T(8,128)(2,1)S(1)} %get-tuple-element.17), channel_id=1, source_target_pairs={{0,4},{4,8},{8,12},{12,16},{16,20},{20,24},{24,28},{28,32},{32,36}... | collective-permute-start | bytes 1966088 | tf_op jit(solution)/shard_map/ppermute | solution.py:288
  10.5 23.8 %collective-permute-start.4 = (bf16[2,10,128,128]{3,2,1,0:T(8,128)(2,1)S(1)}, bf16[2,10,128,128]{3,2,1,0:T(8,128)(2,1)}, u32[]{:S(2)}, u32[]{:S(2)}) collective-permute-start(bf16[2,10,128,128]{3,2,1,0:T(8,128)(2,1)S(1)} %get-tuple-element.25), channel_id=1, source_target_pairs={{4,0},{8,4},{12,8},{16,12},{20,16},{24,20},{28,24},{32,28},{36,32}... | collective-permute-start | bytes 1966088 | tf_op jit(solution)/shard_map/ppermute | solution.py:289
  21.7 2.0 %collective-permute-start.2 = (bf16[10,128,128]{2,1,0:T(8,128)(2,1)S(1)}, bf16[10,128,128]{2,1,0:T(8,128)(2,1)S(1)}, u32[]{:S(2)}, u32[]{:S(2)}) collective-permute-start(bf16[10,128,128]{2,1,0:T(8,128)(2,1)S(1)} %get-tuple-element.30), channel_id=1, source_target_pairs={{0,1},{1,0},{2,3},{3,2},{4,5},{5,4},{6,7},{7,6},{8,9},{9,8},{10,11... | collective-permute-start | bytes 983048 | tf_op jit(solution)/shard_map/ppermute | solution.py:291
  22.5 1.7 %collective-permute-start.3 = (bf16[10,128,128]{2,1,0:T(8,128)(2,1)S(1)}, bf16[10,128,128]{2,1,0:T(8,128)(2,1)S(1)}, u32[]{:S(2)}, u32[]{:S(2)}) collective-permute-start(bf16[10,128,128]{2,1,0:T(8,128)(2,1)S(1)} %get-tuple-element.29), channel_id=1, source_target_pairs={{0,1},{1,0},{2,3},{3,2},{4,5},{5,4},{6,7},{7,6},{8,9},{9,8},{10,11... | collective-permute-start | bytes 983048 | tf_op jit(solution)/shard_map/ppermute | solution.py:291
  41.2 2.2 %collective-permute-start.5 = (f32[2,20,32,128]{3,2,1,0:T(8,128)S(1)}, f32[2,20,32,128]{3,2,1,0:T(8,128)S(1)}, u32[]{:S(2)}, u32[]{:S(2)}) collective-permute-start(f32[2,20,32,128]{3,2,1,0:T(8,128)S(1)} %get-tuple-element.28), channel_id=1, source_target_pairs={{0,1},{1,0},{2,3},{3,2},{4,5},{5,4},{6,7},{7,6},{8,9},{9,8},{10,11... | collective-permute-start | bytes 1966088 | tf_op jit(solution)/shard_map/ppermute | solution.py:312
  44.9 8.1 %collective-permute-start.6 = (f16[21,32,128]{2,1,0:T(8,128)(2,1)S(1)}, f16[21,32,128]{2,1,0:T(8,128)(2,1)S(1)}, u32[]{:S(2)}, u32[]{:S(2)}) collective-permute-start(f16[21,32,128]{2,1,0:T(8,128)(2,1)S(1)} %concatenate.3), channel_id=1, source_target_pairs={{0,2},{1,3},{2,0},{3,1},{4,6},{5,7},{6,4},{7,5},{8,10},{9,11},{10,... | collective-permute-start | bytes 516104 | tf_op jit(solution)/shard_map/ppermute | solution.py:318

commit v3 on v2

v3 whole, which is shorter than its diff:
```python
import jax
import jax.numpy as jnp
from jax import lax
from jax.experimental import pallas as pl
from jax.experimental.pallas import tpu as pltpu
from jax.sharding import PartitionSpec as P

F32 = jnp.float32
BF16 = jnp.bfloat16
VMEM = pl.BlockSpec(memory_space=pltpu.VMEM)
HBM = pl.BlockSpec(memory_space=pltpu.HBM)
SMEM = pl.BlockSpec(memory_space=pltpu.SMEM)
LIMIT = 48 * 1024 * 1024


def split(value):
    high = value.astype(BF16)
    return high, (value - high.astype(F32)).astype(BF16)


def params(flops, nbytes, limit=LIMIT):
    return dict(
        compiler_params=pltpu.CompilerParams(vmem_limit_bytes=limit),
        cost_estimate=pl.CostEstimate(flops=flops, bytes_accessed=nbytes, transcendentals=0),
    )


def rounded_scale(tap, total):
    factor = jnp.exp2(lax.broadcasted_iota(jnp.int32, (1, 128), 1).astype(F32) * (1.0 / 128.0))
    scale = factor / jnp.full((1, 128), total, F32)
    sums, running = [], jnp.zeros((1, 128), F32)
    for value in tap:
        exact = value * scale
        running = running + (exact.astype(BF16).astype(F32) - exact)
        sums.append(running)
    error = jnp.zeros((1, 128), F32)
    for partial in sums:
        rest = running - partial
        error = error + partial * partial + rest * rest
    error = error / (factor * factor)
    best = error == jnp.min(error, axis=1, keepdims=True)
    factor = jnp.max(jnp.where(best, factor, 0.0), axis=1, keepdims=True)
    scale = jnp.max(jnp.where(best, scale, 0.0), axis=1, keepdims=True)
    return jnp.broadcast_to(scale, (1, 128)), jnp.broadcast_to(factor, (1, 128))


def matrices_kernel(place_ref, taps_ref, rec_ref, z_ref, x_ref, y_ref, scale_ref, last_out, first_out, sems):
    views, taps = taps_ref.shape[0], taps_ref.shape[3]
    margin = last_out.shape[1]
    copies = []
    for v in range(views):
        for out, begin in ((last_out, rec_ref.shape[1] - margin), (first_out, 0)):
            copies.append(
                pltpu.make_async_copy(rec_ref.at[v, pl.ds(begin, margin)], out.at[v], sems.at[len(copies)])
            )
    for copy in copies:
        copy.start()
    half = (taps - 1) // 2
    rows = x_ref.shape[2] // 2
    place = place_ref[0]
    zeros = jnp.zeros((rows, rows), BF16)

    for v in range(views):
        tap = {
            (d, r): [taps_ref[v, d, r, j] for j in range(taps)] for d in range(3) for r in range(2)
        }
        scale = {}
        for r in range(2):
            undo = jnp.ones((1, 128), F32)
            for d in range(3):
                values = tap[d, r] if d < 2 else tap[2, 0] + tap[2, 1]
                total = values[0]
                for value in values[1:]:
                    total = total + value
                scale[d, r], factor = rounded_scale(tap[d, r], total)
                undo = undo / factor
            scale_ref[v, r] = undo
        for direction in range(2):
            for r in range(2):
                other = 1 - r
                x_ref[direction, v, r * rows : (r + 1) * rows, other * rows : (other + 1) * rows] = zeros
        step = 32
        for first in range(0, rows, step):
            diff = (
                lax.broadcasted_iota(jnp.int32, (step, rows), 0)
                - lax.broadcasted_iota(jnp.int32, (step, rows), 1)
                + (first + half)
            )
            made = {(d, r, m): jnp.zeros((step, rows), F32) for d in range(2) for r in range(2) for m in range(2)}
            for j in range(taps):
                here = diff == j
                for d, r, m in made:
                    pick = tap[d, r][j] if m == 0 else tap[d, r][taps - 1 - j]
                    made[d, r, m] = jnp.where(here, pick, made[d, r, m])
            for (d, r, m), value in made.items():
                value = (value * scale[d, r]).astype(BF16)
                lanes = slice(r * rows, (r + 1) * rows)
                if d == 0:
                    x_ref[m, v, r * rows + first : r * rows + first + step, lanes] = value
                elif m == 1:
                    y_ref[0, v, first : first + step, lanes] = value
                else:
                    target = pl.multiple_of(jnp.bitwise_xor(first // step, place) * step, step)
                    y_ref[1, v, pl.ds(target, step), lanes] = value
        tall = z_ref.shape[1] // (2 * views)
        wide = z_ref.shape[2]
        step = 16
        for first in range(0, tall, step):
            diff = (
                lax.broadcasted_iota(jnp.int32, (step, wide), 1)
                - lax.broadcasted_iota(jnp.int32, (step, wide), 0)
                - first
            )
            made = {(r, m): jnp.zeros((step, wide), F32) for r in range(2) for m in range(2)}
            for j in range(taps):
                here = diff == 8 * j
                for r, m in made:
                    pick = tap[2, r][j] if m == 0 else tap[2, r][taps - 1 - j]
                    made[r, m] = jnp.where(here, pick, made[r, m])
            for (r, m), value in made.items():
                top = (2 * v + r) * tall + first
                z_ref[m, top : top + step, :] = (value * scale[2, r][0:1, 0:1]).astype(BF16)
    for copy in copies:
        copy.wait()


def dot(a, b):
    return jnp.dot(a, b, preferred_element_type=F32)


CHUNK = 4


def inverted(value):
    guess = pl.reciprocal(value, approx=True)
    return guess * (2.0 - value * guess)


def filter_to(load, views, groups, z_ref, x_ref, y_ref, scale_ref, e_ref, g_ref, exact, emit):
    tall = z_ref.shape[0] // (2 * views)
    z_out = tall // 8
    rows = y_ref.shape[1]
    for pair in range(rows // 16):
        block = load(slice(pair * 16, pair * 16 + 16))
        planes = block.shape[0]
        depth = (planes - (groups - 1) * z_out) * 8
        octets = [block[:, 8 * o : 8 * o + 8, :].reshape(planes * 8, rows).astype(BF16) for o in range(2)]
        octets = jnp.concatenate(octets, axis=1)
        for part in range(groups):
            data = octets[part * z_out * 8 : part * z_out * 8 + depth]
            all_e = dot(z_ref[:, :depth], data)
            for v in range(views):
                for r in range(2):
                    top = (2 * v + r) * tall
                    e = all_e[top : top + tall]
                    e = jnp.concatenate([e[:, :rows], e[:, rows:]], axis=0)
                    lanes = slice(r * rows, (r + 1) * rows)
                    if exact:
                        high, low = split(e)
                        e_ref[v, 0, pair * groups + part, :, lanes] = high
                        e_ref[v, 1, pair * groups + part, :, lanes] = low
                    else:
                        e_ref[v, 0, pair * groups + part, :, lanes] = e.astype(BF16)
    for v in range(views):
        for first in range(0, rows // 16 * groups, CHUNK):
            e = e_ref[v, 0, first : first + CHUNK].reshape(CHUNK * 2 * tall, 2 * rows)
            all_g = dot(e, x_ref[v])
            if exact:
                e = e_ref[v, 1, first : first + CHUNK].reshape(CHUNK * 2 * tall, 2 * rows)
                all_g = all_g + dot(e, x_ref[v])
            for index in range(first, first + CHUNK):
                pair, part = index // groups, index % groups
                g = all_g[(index - first) * 2 * tall : (index - first + 1) * 2 * tall]
                for r in range(2):
                    lanes = slice(r * rows, (r + 1) * rows)
                    g_rows = jnp.concatenate(
                        [g[o * tall : (o + 1) * tall, lanes].reshape(z_out, 8, rows) for o in range(2)], axis=1
                    )
                    g_rows = g_rows * scale_ref[v, r]
                    target = slice(r * rows + pair * 16, r * rows + pair * 16 + 16)
                    planes_at = slice(part * z_out, (part + 1) * z_out)
                    if exact:
                        high, low = split(g_rows)
                        g_ref[v, 0, planes_at, target, :] = high
                        g_ref[v, 1, planes_at, target, :] = low
                    else:
                        g_ref[v, 0, planes_at, target, :] = g_rows.astype(BF16)
    for v in range(views):
        for z in range(0, groups * z_out, 2):
            data = jnp.concatenate([g_ref[v, 0, z], g_ref[v, 0, z + 1]], axis=1)
            out = dot(y_ref[v], data)
            if exact:
                data = jnp.concatenate([g_ref[v, 1, z], g_ref[v, 1, z + 1]], axis=1)
                out = out + dot(y_ref[v], data)
            emit(v, z, out[:, :rows])
            emit(v, z + 1, out[:, rows:])


def scratch(views, groups, halves, z_out, rows, cols):
    return [
        pltpu.VMEM((views, halves, rows // 16 * groups, 2 * z_out * 8, 2 * cols), BF16),
        pltpu.VMEM((views, halves, groups * z_out, 2 * rows, cols), BF16),
    ]


def quotient_kernel(
    place_ref, mine_ref, other_ref, own_ref, rec_ref, z_ref, x_ref, y_ref, scale_ref, own_out, rim_out, e_ref, g_ref
):
    planes = own_ref.shape[0]
    margin = rim_out.shape[2]
    first_core = place_ref[0] % 2 == 0

    def load(at):
        mine = mine_ref[:, at, :].astype(F32)
        other = other_ref[:, at, :].astype(F32)
        before, after = jnp.where(first_core, mine, other), jnp.where(first_core, other, mine)
        return jnp.concatenate([before, own_ref[:, at, :].astype(F32), after], axis=0)

    def emit(v, z, blurred):
        inverse = inverted(blurred)
        if z < margin:
            rim_out[v, 0, z] = inverse
        elif z < margin + planes:
            own_out[v, z - margin] = (rec_ref[v, z - margin].astype(F32) * inverse).astype(BF16)
        else:
            rim_out[v, 1, z - margin - planes] = inverse

    groups = (planes + 2 * margin) // (planes // 2)
    filter_to(load, rec_ref.shape[0], groups, z_ref.at[0], x_ref.at[0], y_ref.at[0], scale_ref, e_ref, g_ref, False, emit)


def correction_kernel(before_ref, own_ref, after_ref, rim_ref, z_ref, x_ref, y_ref, scale_ref, keep_ref, send_ref, e_ref, g_ref, earlier_ref):
    views = own_ref.shape[0]
    part = keep_ref.shape[2]
    tall = z_ref.shape[1] // views
    for v in range(views):

        def load(at, v=v):
            before = before_ref[v, :, at, :].astype(F32) * rim_ref[v, 0, :, at, :]
            after = after_ref[v, :, at, :].astype(F32) * rim_ref[v, 1, :, at, :]
            return jnp.concatenate([before, own_ref[v, :, at, :].astype(F32), after], axis=0)

        def emit(_, z, value, v=v):
            if v > 0:
                value = value * earlier_ref[z]
            if v < views - 1:
                earlier_ref[z] = value
                return
            for b in range(4):
                rows = value[b * part : (b + 1) * part]
                if b % 2 == 0:
                    keep_ref[b // 2, z] = rows
                else:
                    send_ref[b // 2, z] = rows

        z_view = z_ref.at[1, v * tall : (v + 1) * tall]
        filter_to(load, 1, 2, z_view, x_ref.at[1, v : v + 1], y_ref.at[1, v : v + 1], scale_ref.at[v : v + 1], e_ref, g_ref, True, emit)


def local(estimate, recordings, psf_taps):
    planes, rows, cols = estimate.shape
    taps = psf_taps.shape[-1]
    margin = (taps - 1) // 2
    views = recordings.shape[0]
    devices = lax.axis_size("gz")
    place = lax.axis_index("view")
    place_array = place.reshape(1).astype(jnp.int32)
    up = [(i, i + 1) for i in range(devices - 1)]
    down = [(i + 1, i) for i in range(devices - 1)]
    swap = [(i, i ^ 1) for i in range(4)]
    z_out = planes // 2
    shape = jax.ShapeDtypeStruct

    rounded = estimate.astype(BF16)
    both_ways = [(4 * i + w, 4 * j + w) for w in (0, 2) for i, j in up]
    both_ways += [(4 * i + w, 4 * j + w) for w in (1, 3) for i, j in down]
    mine = lax.ppermute(rounded, ("gz", "view"), both_ways)

    wide = -(-(z_out + taps - 1) * 8 // 128) * 128
    z_mat, x_mat, y_mat, scales, last, first = pl.pallas_call(
        matrices_kernel,
        out_shape=[
            shape((2, views * 2 * z_out * 8, wide), BF16),
            shape((2, views, 2 * cols, 2 * cols), BF16),
            shape((2, views, rows, 2 * rows), BF16),
            shape((views, 2, 1, 128), F32),
            shape((views, margin, rows, cols), BF16),
            shape((views, margin, rows, cols), BF16),
        ],
        in_specs=[SMEM, SMEM, HBM],
        out_specs=[VMEM] * 6,
        scratch_shapes=[pltpu.SemaphoreType.DMA((2 * views,))],
        name="matrices",
        **params(10**6, 10**4),
    )(place_array, psf_taps, recordings)

    before = lax.ppermute(last, "gz", up)
    after = lax.ppermute(first, "gz", down)
    mine, z_mat = lax.optimization_barrier((mine, z_mat))
    other = lax.ppermute(mine, "view", swap)

    own, rim = pl.pallas_call(
        quotient_kernel,
        out_shape=[shape((views, planes, rows, cols), BF16), shape((views, 2, margin, rows, cols), F32)],
        in_specs=[SMEM] + [VMEM] * 8,
        out_specs=[VMEM] * 2,
        scratch_shapes=scratch(views, 4, 1, z_out, rows, cols),
        name="quotients",
        **params(10**6, 10**4),
    )(place_array, mine, other, rounded, recordings, z_mat, x_mat, y_mat, scales)
    part = rows // 4
    keep, send = pl.pallas_call(
        correction_kernel,
        out_shape=[shape((2, planes, part, cols), F32)] * 2,
        in_specs=[VMEM] * 8,
        out_specs=[VMEM] * 2,
        scratch_shapes=scratch(1, 2, 2, z_out, rows, cols) + [pltpu.VMEM((planes, rows, cols), F32)],
        name="corrections",
        **params(4 * 10**9, 5 * 10**6),
    )(before, own, after, rim, z_mat, x_mat, y_mat, scales)
    core = lax.ppermute(send, "view", swap)
    product = keep[1] * core[1]
    most = jnp.maximum(jnp.max(product), 1e-30)
    exponent = jnp.floor(jnp.log2(most)) - 14.0
    coded = (product * jnp.exp2(-exponent)).astype(jnp.float16)
    tail = jnp.broadcast_to(exponent.astype(jnp.float16), (1, part, cols))
    across = lax.ppermute(jnp.concatenate([coded, tail]), "view", [(i, i ^ 2) for i in range(4)])
    own_rows = lax.dynamic_slice_in_dim(estimate, place * part, part, 1)
    partial, across = lax.optimization_barrier((own_rows * (keep[0] * core[0]), across))
    return partial * (across[:planes].astype(F32) * jnp.exp2(across[planes:].astype(F32)))


def solution(mesh):
    in_specs = (P("gz", None, None), P("view", "gz", None, None), P("view", None, None, None))
    out_specs = P("gz", "view", None)
    return jax.shard_map(local, mesh=mesh, in_specs=in_specs, out_specs=out_specs, check_vma=False)
```

time: 56.9 us -> 60.3 us (1.060); the launches traced: 56.1 us -> 60.1 us
  waiting for transfers between devices: 12.1 us -> 25.6 us
  Pallas kernels: 19.7 us -> 13.9 us
  local copies, waits for them, and re-layouts: 3.24 us -> 0.05 us
  other arithmetic: 2.63 us -> 4.1 us
  starting transfers between devices: 16.9 us -> 15.6 us
  between operations: 1.51 us -> 0.85 us
    ppermute x1, waiting for transfers between devices: 0.15 us -> 7.68 us  [local(): before = lax.ppermute(last, 'gz', up)]
    ppermute x1, waiting for transfers between devices: 3.33 us -> 10.6 us  [local(): mine = lax.ppermute(rounded, ('gz', 'view'), both_ways)]
    pallas_call x1, Pallas kernels: 9.91 us -> 5.48 us  [local(): pl.pallas_call(quotient_kernel, out_shape=[shape((views, planes, rows, co...]
    unnamed x6 -> x4, local copies, waits for them, and re-layouts: 2.64 us -> 0.01 us
    ppermute x1, starting transfers between devices: 3.83 us -> 1.91 us  [local(): before = lax.ppermute(last, 'gz', up)]
    ppermute x1, starting transfers between devices: 5.06 us -> 6.93 us  [local(): after = lax.ppermute(first, 'gz', down)]
    pallas_call x1, Pallas kernels: 6.89 us -> 5.37 us  [local(): pl.pallas_call(correction_kernel, out_shape=[shape((2, planes, part, cols...]
    convert_element_type x1, other arithmetic: 0.03 us -> 1.52 us  [local(): rounded = estimate.astype(BF16)]
  transfers between devices with their start and end apart: 7 -> 6, of which waited for: 6 -> 5; matrix products, arithmetic and copies ran while one was open for 0% -> 2% of each run, Pallas kernels for 23% -> 14%
where the time goes in v3:
time: 60.3 us; the launch traced here: 60.1 us
  waiting for transfers between devices  25.6 us (42%)
  starting transfers between devices  15.6 us (26%)
  Pallas kernels  13.9 us (23%)
  other arithmetic  4.1 us (7%)
  between operations  0.85 us (1%)
    ppermute x1, waiting for transfers between devices, local(): mine = lax.ppermute(rounded, ('gz', 'view'), both_ways)  10.6 us
    ppermute x1, waiting for transfers between devices, local(): before = lax.ppermute(last, 'gz', up)  7.68 us
    ppermute x1, starting transfers between devices, local(): after = lax.ppermute(first, 'gz', down)  6.93 us
    pallas_call x1, Pallas kernels, local(): pl.pallas_call(quotient_kernel, out_shape=[shape((views, planes, rows, co...  5.48 us
    pallas_call x1, Pallas kernels, local(): pl.pallas_call(correction_kernel, out_shape=[shape((2, planes, part, cols...  5.37 us
    ppermute x1, waiting for transfers between devices, local(): lax.ppermute(jnp.concatenate([coded, tail]), 'view', [(i, i ^ 2) for i in...  4.13 us
    ppermute x1, starting transfers between devices, local(): mine = lax.ppermute(rounded, ('gz', 'view'), both_ways)  3.83 us
    pallas_call x1, Pallas kernels, local(): pl.pallas_call(matrices_kernel, out_shape=[shape((2, views * 2 * z_out *...  3 us
  transfers between devices with their start and end apart: 6, of which 5 were waited for; matrix products, arithmetic and copies ran while one was open for 2% of the time, Pallas kernels for 14%

profile of v3, /device:TPU:24, one launch (start us, length us, event | category | flops | bytes accessed | tf_op | source)
XLA Modules:
  0.0 60.1 jit_solution(767510020074948322)
XLA Ops:
  0.0 0.0 copy-start
  0.0 0.0 copy-start.1
  0.0 1.5 %convert_element_type.18.own_ref = bf16[20,128,128]{2,1,0:T(8,128)(2,1)S(1)} convert(f32[20,128,128]{2,1,0:T(8,128)} %param.3) | non-fusion elementwise | flops 327680 | bytes 1966080 | tf_op jit(solution)/shard_map/convert_element_type | solution.py:274
  1.5 3.8 %collective-permute-start.1 = (bf16[20,128,128]{2,1,0:T(8,128)(2,1)S(1)}, bf16[20,128,128]{2,1,0:T(8,128)(2,1)S(1)}, u32[]{:S(2)}, u32[]{:S(2)}) collective-permute-start(bf16[20,128,128]{2,1,0:T(8,128)(2,1)S(1)} %convert_element_type.18.own_ref), channel_id=1, source_target_pairs={{0,4},{4,8},{8,12},{12,16},{16,20},{20,24},{24,28},{28,32},{32,36}... | collective-permute-start | bytes 1966088 | tf_op jit(solution)/shard_map/ppermute | solution.py:277
  5.4 0.0 copy-done
  5.4 0.0 copy-done.1
  5.4 3.0 %matrices.1 = (bf16[2,320,256]{2,1,0:T(8,128)(2,1)S(1)}, bf16[2,2,256,256]{3,2,1,0:T(8,128)(2,1)S(1)}, bf16[2,2,128,256]{3,2,1,0:T(8,128)(2,1)S(1)}, f32[2,2,1,1...) custom-call(s32[1]{0:T(128)} %bitcast.place_ref, ...), custom_call_target="tpu_custom_call" | custom-call | flops 1000000 | bytes 10000 | tf_op jit(solution)/shard_map/matrices/pallas_call | solution.py:280
  8.4 10.6 %collective-permute-done.1.mine_ref = bf16[20,128,128]{2,1,0:T(8,128)(2,1)S(1)} collective-permute-done((bf16[20,128,128]{2,1,0:T(8,128)(2,1)S(1)}, bf16[20,128,128]{2,1,0:T(8,128)(2,1)S(1)}, u32[]{:S(2)}, u32[]{:S(2)}) %collective-permute-start.1) | collective-permute-done | bytes 655392 | tf_op jit(solution)/shard_map/ppermute | solution.py:277
  19.0 0.0 collective-permute-start.2
  19.0 1.9 %collective-permute-start = (bf16[2,10,128,128]{3,2,1,0:T(8,128)(2,1)S(1)}, bf16[2,10,128,128]{3,2,1,0:T(8,128)(2,1)S(1)}, u32[]{:S(2)}, u32[]{:S(2)}) collective-permute-start(bf16[2,10,128,128]{3,2,1,0:T(8,128)(2,1)S(1)} %get-tuple-element.19), channel_id=1, source_target_pairs={{0,4},{4,8},{8,12},{12,16},{16,20},{20,24},{24,28},{28,32},{32,36}... | collective-permute-start | bytes 1966088 | tf_op jit(solution)/shard_map/ppermute | solution.py:297
  20.9 6.9 %collective-permute-start.3 = (bf16[2,10,128,128]{3,2,1,0:T(8,128)(2,1)S(1)}, bf16[2,10,128,128]{3,2,1,0:T(8,128)(2,1)S(1)}, u32[]{:S(2)}, u32[]{:S(2)}) collective-permute-start(bf16[2,10,128,128]{3,2,1,0:T(8,128)(2,1)S(1)} %get-tuple-element.27), channel_id=1, source_target_pairs={{4,0},{8,4},{12,8},{16,12},{20,16},{24,20},{28,24},{32,28},{36,32}... | collective-permute-start | bytes 1966088 | tf_op jit(solution)/shard_map/ppermute | solution.py:298
  27.8 0.0 collective-permute-done.2.other_ref
  27.8 5.5 %quotients.1 = (bf16[2,20,128,128]{3,2,1,0:T(8,128)(2,1)S(1)}, f32[2,2,10,128,128]{4,3,2,1,0:T(8,128)}) custom-call(s32[1]{0:T(128)} %bitcast.place_ref, bf16[20,128,128]{2,1,0:T(8,128)(2,1)S(1)} %collective-permute-done.1.mine_ref, bf16[20,128,128]{2,1,0:T(8,128)(2,1)S(1)} %collective-permute-done.2.other_ref, ...), custom_call_target="tpu_custom_call" | custom-call | flops 1000000 | bytes 10000 | tf_op jit(solution)/shard_map/quotients/pallas_call | solution.py:302
  33.3 7.7 %collective-permute-done.before_ref = bf16[2,10,128,128]{3,2,1,0:T(8,128)(2,1)S(1)} collective-permute-done((bf16[2,10,128,128]{3,2,1,0:T(8,128)(2,1)S(1)}, bf16[2,10,128,128]{3,2,1,0:T(8,128)(2,1)S(1)}, u32[]{:S(2)}, u32[]{:S(2)}) %collective-permute-start) | collective-permute-done | bytes 655392 | tf_op jit(solution)/shard_map/ppermute | solution.py:297
  41.0 1.2 %collective-permute-done.3.after_ref = bf16[2,10,128,128]{3,2,1,0:T(8,128)(2,1)S(1)} collective-permute-done((bf16[2,10,128,128]{3,2,1,0:T(8,128)(2,1)S(1)}, bf16[2,10,128,128]{3,2,1,0:T(8,128)(2,1)S(1)}, u32[]{:S(2)}, u32[]{:S(2)}) %collective-permute-start.3) | collective-permute-done | bytes 655392 | tf_op jit(solution)/shard_map/ppermute | solution.py:298
  42.2 5.4 %corrections.1 = (f32[2,20,32,128]{3,2,1,0:T(8,128)S(1)}, f32[2,20,32,128]{3,2,1,0:T(8,128)S(1)}) custom-call(bf16[2,10,128,128]{3,2,1,0:T(8,128)(2,1)S(1)} %collective-permute-done.before_ref, bf16[2,20,128,128]{3,2,1,0:T(8,128)(2,1)S(1)} %get-tuple-element.26.own_ref, bf16[2,10,128,128]{3,2,1,0:T(8,128)(2,1)S(1)} %collective-permute-done.3.after_ref, ...), custom_call_target="tpu_custom_call" | custom-call | flops 4000000000 | bytes 5000000 | tf_op jit(solution)/shard_map/corrections/pallas_call | solution.py:312
  47.6 0.1 collective-permute-start.4
  47.7 2.1 %collective-permute-done.4 = f32[2,20,32,128]{3,2,1,0:T(8,128)S(1)} collective-permute-done((f32[2,20,32,128]{3,2,1,0:T(8,128)S(1)}, f32[2,20,32,128]{3,2,1,0:T(8,128)S(1)}, u32[]{:S(2)}, u32[]{:S(2)}) %collective-permute-start.4) | collective-permute-done | bytes 655392 | tf_op jit(solution)/shard_map/ppermute | solution.py:321
  49.8 0.7 %fusion.3 = f32[]{:T(128)} fusion(f32[2,20,32,128]{3,2,1,0:T(8,128)S(1)} %collective-permute-done.4, f32[2,20,32,128]{3,2,1,0:T(8,128)S(1)} %get-tuple-element.29), kind=kLoop, calls=%fused_computation.7 | loop fusion | flops 163839 | bytes 655364 | tf_op jit(solution)/shard_map/reduce_max | solution.py:323
  51.2 0.1 fusion.2
  51.3 2.8 %collective-permute-start.5 = (f16[21,32,128]{2,1,0:T(8,128)(2,1)S(1)}, f16[21,32,128]{2,1,0:T(8,128)(2,1)S(1)}, u32[]{:S(2)}, u32[]{:S(2)}) collective-permute-start(f16[21,32,128]{2,1,0:T(8,128)(2,1)S(1)} %concatenate.3), channel_id=1, source_target_pairs={{0,2},{1,3},{2,0},{3,1},{4,6},{5,7},{6,4},{7,5},{8,10},{9,11},{10,... | collective-permute-start | bytes 516104 | tf_op jit(solution)/shard_map/ppermute | solution.py:327
  54.1 1.1 %fusion.1 = f32[20,32,128]{2,1,0:T(8,128)S(1)} fusion(f32[2,20,32,128]{3,2,1,0:T(8,128)S(1)} %collective-permute-done.4, f32[2,20,32,128]{3,2,1,0:T(8,128)S(1)} %get-tuple-element.29, f32[20,128,128]{2,1,0:T(8,128)} %param.3, s32[]{:T(128)S(6)} %select_n.3), kind=kLoop, calls=%fused_computation.3 | loop fusion | flops 163840 | bytes 1310724 | tf_op jit(solution)/shard_map/mul | solution.py:329
  55.2 4.1 %collective-permute-done.5 = f16[21,32,128]{2,1,0:T(8,128)(2,1)S(1)} collective-permute-done((f16[21,32,128]{2,1,0:T(8,128)(2,1)S(1)}, f16[21,32,128]{2,1,0:T(8,128)(2,1)S(1)}, u32[]{:S(2)}, u32[]{:S(2)}) %collective-permute-start.5) | collective-permute-done | bytes 172064 | tf_op jit(solution)/shard_map/ppermute | solution.py:327
  59.3 0.8 %multiply_multiply_fusion = f32[20,32,128]{2,1,0:T(8,128)} fusion(f32[20,32,128]{2,1,0:T(8,128)S(1)} %fusion.1, f32[32,128]{1,0:T(8,128)S(1)} %exponential_bitcast_fusion, f16[21,32,128]{2,1,0:T(8,128)(2,1)S(1)} %collective-permute-done.5), kind=kLoop, calls=%fused_computation.4 | loop fusion | flops 245760 | bytes 835584 | tf_op jit(solution)/shard_map/mul | solution.py:330
  (2 shorter events, 0.1 us)
Async XLA Ops:
  0.0 5.4 %copy-start = (bf16[2,20,128,128]{3,2,1,0:T(8,128)(2,1)S(1)}, bf16[2,20,128,128]{3,2,1,0:T(8,128)(2,1)}, u32[]{:S(2)}) copy-start(bf16[2,20,128,128]{3,2,1,0:T(8,128)(2,1)} %rec_ref.3) | copy-start | bytes 3932164
  0.0 5.4 %copy-start.1 = (f32[2,3,2,21]{3,2,1,0:T(2,128)S(1)}, f32[2,3,2,21]{3,2,1,0:T(2,128)}, u32[]{:S(2)}) copy-start(f32[2,3,2,21]{3,2,1,0:T(2,128)} %taps_ref.1) | copy-start | bytes 3028
  1.5 17.4 %collective-permute-start.1 = (bf16[20,128,128]{2,1,0:T(8,128)(2,1)S(1)}, bf16[20,128,128]{2,1,0:T(8,128)(2,1)S(1)}, u32[]{:S(2)}, u32[]{:S(2)}) collective-permute-start(bf16[20,128,128]{2,1,0:T(8,128)(2,1)S(1)} %convert_element_type.18.own_ref), channel_id=1, source_target_pairs={{0,4},{4,8},{8,12},{12,16},{16,20},{20,24},{24,28},{28,32},{32,36}... | collective-permute-start | bytes 1966088 | tf_op jit(solution)/shard_map/ppermute | solution.py:277
  19.0 8.9 %collective-permute-start.2 = (bf16[20,128,128]{2,1,0:T(8,128)(2,1)S(1)}, bf16[20,128,128]{2,1,0:T(8,128)(2,1)S(1)}, u32[]{:S(2)}, u32[]{:S(2)}) collective-permute-start(bf16[20,128,128]{2,1,0:T(8,128)(2,1)S(1)} %collective-permute-done.1.mine_ref), channel_id=1, source_target_pairs={{0,1},{1,0},{2,3},{3,2},{4,5},{5,4},{6,7},{7,6},{8,9},{9,8},{10,11... | collective-permute-start | bytes 1966088 | tf_op jit(solution)/shard_map/ppermute | solution.py:300
  19.0 22.0 %collective-permute-start = (bf16[2,10,128,128]{3,2,1,0:T(8,128)(2,1)S(1)}, bf16[2,10,128,128]{3,2,1,0:T(8,128)(2,1)S(1)}, u32[]{:S(2)}, u32[]{:S(2)}) collective-permute-start(bf16[2,10,128,128]{3,2,1,0:T(8,128)(2,1)S(1)} %get-tuple-element.19), channel_id=1, source_target_pairs={{0,4},{4,8},{8,12},{12,16},{16,20},{20,24},{24,28},{28,32},{32,36}... | collective-permute-start | bytes 1966088 | tf_op jit(solution)/shard_map/ppermute | solution.py:297
  20.9 21.3 %collective-permute-start.3 = (bf16[2,10,128,128]{3,2,1,0:T(8,128)(2,1)S(1)}, bf16[2,10,128,128]{3,2,1,0:T(8,128)(2,1)S(1)}, u32[]{:S(2)}, u32[]{:S(2)}) collective-permute-start(bf16[2,10,128,128]{3,2,1,0:T(8,128)(2,1)S(1)} %get-tuple-element.27), channel_id=1, source_target_pairs={{4,0},{8,4},{12,8},{16,12},{20,16},{24,20},{28,24},{32,28},{36,32}... | collective-permute-start | bytes 1966088 | tf_op jit(solution)/shard_map/ppermute | solution.py:298
  47.6 2.2 %collective-permute-start.4 = (f32[2,20,32,128]{3,2,1,0:T(8,128)S(1)}, f32[2,20,32,128]{3,2,1,0:T(8,128)S(1)}, u32[]{:S(2)}, u32[]{:S(2)}) collective-permute-start(f32[2,20,32,128]{3,2,1,0:T(8,128)S(1)} %get-tuple-element.30), channel_id=1, source_target_pairs={{0,1},{1,0},{2,3},{3,2},{4,5},{5,4},{6,7},{7,6},{8,9},{9,8},{10,11... | collective-permute-start | bytes 1966088 | tf_op jit(solution)/shard_map/ppermute | solution.py:321
  51.3 8.0 %collective-permute-start.5 = (f16[21,32,128]{2,1,0:T(8,128)(2,1)S(1)}, f16[21,32,128]{2,1,0:T(8,128)(2,1)S(1)}, u32[]{:S(2)}, u32[]{:S(2)}) collective-permute-start(f16[21,32,128]{2,1,0:T(8,128)(2,1)S(1)} %concatenate.3), channel_id=1, source_target_pairs={{0,2},{1,3},{2,0},{3,1},{4,6},{5,7},{6,4},{7,5},{8,10},{9,11},{10,... | collective-permute-start | bytes 516104 | tf_op jit(solution)/shard_map/ppermute | solution.py:327

commit v4 on v3

--- a/solution.py
+++ b/solution.py
@@ -10,7 +10,7 @@
 VMEM = pl.BlockSpec(memory_space=pltpu.VMEM)
 HBM = pl.BlockSpec(memory_space=pltpu.HBM)
 SMEM = pl.BlockSpec(memory_space=pltpu.SMEM)
-LIMIT = 48 * 1024 * 1024
+LIMIT = 20 * 1024 * 1024
 
 
 def split(value):
@@ -23,6 +23,20 @@
         compiler_params=pltpu.CompilerParams(vmem_limit_bytes=limit),
         cost_estimate=pl.CostEstimate(flops=flops, bytes_accessed=nbytes, transcendentals=0),
     )
+
+
+def edges_kernel(rec_ref, last_out, first_out, sems):
+    margin = last_out.shape[1]
+    copies = []
+    for v in range(rec_ref.shape[0]):
+        for out, begin in ((last_out, rec_ref.shape[1] - margin), (first_out, 0)):
+            copies.append(
+                pltpu.make_async_copy(rec_ref.at[v, pl.ds(begin, margin)], out.at[v], sems.at[len(copies)])
+            )
+    for copy in copies:
+        copy.start()
+    for copy in copies:
+        copy.wait()
 
 
 def rounded_scale(tap, total):
@@ -44,17 +58,8 @@
     return jnp.broadcast_to(scale, (1, 128)), jnp.broadcast_to(factor, (1, 128))
 
 
-def matrices_kernel(place_ref, taps_ref, rec_ref, z_ref, x_ref, y_ref, scale_ref, last_out, first_out, sems):
+def matrices_kernel(place_ref, taps_ref, z_ref, x_ref, y_ref, scale_ref):
     views, taps = taps_ref.shape[0], taps_ref.shape[3]
-    margin = last_out.shape[1]
-    copies = []
-    for v in range(views):
-        for out, begin in ((last_out, rec_ref.shape[1] - margin), (first_out, 0)):
-            copies.append(
-                pltpu.make_async_copy(rec_ref.at[v, pl.ds(begin, margin)], out.at[v], sems.at[len(copies)])
-            )
-    for copy in copies:
-        copy.start()
     half = (taps - 1) // 2
     rows = x_ref.shape[2] // 2
     place = place_ref[0]
@@ -120,8 +125,6 @@
             for (r, m), value in made.items():
                 top = (2 * v + r) * tall + first
                 z_ref[m, top : top + step, :] = (value * scale[2, r][0:1, 0:1]).astype(BF16)
-    for copy in copies:
-        copy.wait()
 
 
 def dot(a, b):
@@ -203,58 +206,84 @@
     ]
 
 
-def quotient_kernel(
-    place_ref, mine_ref, other_ref, own_ref, rec_ref, z_ref, x_ref, y_ref, scale_ref, own_out, rim_out, e_ref, g_ref
+def inverse_kernel(early, place_ref, low_ref, high_ref, own_ref, z_ref, x_ref, y_ref, scale_ref, out_ref, e_ref, g_ref):
+    side_first = (place_ref[0] % 2 == 0) == early
+
+    def load(at):
+        side = jnp.concatenate([low_ref[:, at, :], high_ref[:, at, :]], axis=0).astype(F32)
+        own = own_ref[:, at, :].astype(F32)
+        return jnp.concatenate([jnp.where(side_first, side, own), jnp.where(side_first, own, side)], axis=0)
+
+    def emit(v, z, blurred):
+        out_ref[v, z] = inverted(blurred)
+
+    views = out_ref.shape[0]
+    filter_to(load, views, 2, z_ref.at[0], x_ref.at[0], y_ref.at[0], scale_ref, e_ref, g_ref, False, emit)
+
+
+def correction_kernel(
+    place_ref,
+    before_ref,
+    rec_ref,
+    after_ref,
+    early_ref,
+    late_ref,
+    z_ref,
+    x_ref,
+    y_ref,
+    scale_ref,
+    keep_ref,
+    send_ref,
+    e_ref,
+    g_ref,
+    product_ref,
 ):
-    planes = own_ref.shape[0]
-    margin = rim_out.shape[2]
-    first_core = place_ref[0] % 2 == 0
-
-    def load(at):
-        mine = mine_ref[:, at, :].astype(F32)
-        other = other_ref[:, at, :].astype(F32)
-        before, after = jnp.where(first_core, mine, other), jnp.where(first_core, other, mine)
-        return jnp.concatenate([before, own_ref[:, at, :].astype(F32), after], axis=0)
-
-    def emit(v, z, blurred):
-        inverse = inverted(blurred)
-        if z < margin:
-            rim_out[v, 0, z] = inverse
-        elif z < margin + planes:
-            own_out[v, z - margin] = (rec_ref[v, z - margin].astype(F32) * inverse).astype(BF16)
-        else:
-            rim_out[v, 1, z - margin - planes] = inverse
-
-    groups = (planes + 2 * margin) // (planes // 2)
-    filter_to(load, rec_ref.shape[0], groups, z_ref.at[0], x_ref.at[0], y_ref.at[0], scale_ref, e_ref, g_ref, False, emit)
-
-
-def correction_kernel(before_ref, own_ref, after_ref, rim_ref, z_ref, x_ref, y_ref, scale_ref, keep_ref, send_ref, e_ref, g_ref, earlier_ref):
-    views = own_ref.shape[0]
+    views, planes = rec_ref.shape[:2]
     part = keep_ref.shape[2]
     tall = z_ref.shape[1] // views
+    early_first = place_ref[0] % 2 == 0
+    most = [jnp.zeros((8, product_ref.shape[2]), F32)]
     for v in range(views):
 
         def load(at, v=v):
-            before = before_ref[v, :, at, :].astype(F32) * rim_ref[v, 0, :, at, :]
-            after = after_ref[v, :, at, :].astype(F32) * rim_ref[v, 1, :, at, :]
-            return jnp.concatenate([before, own_ref[v, :, at, :].astype(F32), after], axis=0)
+            rec = [ref[v, :, at, :].astype(F32) for ref in (before_ref, rec_ref, after_ref)]
+            early, late = early_ref[v, :, at, :], late_ref[v, :, at, :]
+            inverse = [jnp.where(early_first, early, late), jnp.where(early_first, late, early)]
+            return jnp.concatenate(rec, axis=0) * jnp.concatenate(inverse, axis=0)
 
         def emit(_, z, value, v=v):
             if v > 0:
-                value = value * earlier_ref[z]
-            if v < views - 1:
-                earlier_ref[z] = value
-                return
-            for b in range(4):
-                rows = value[b * part : (b + 1) * part]
-                if b % 2 == 0:
-                    keep_ref[b // 2, z] = rows
-                else:
-                    send_ref[b // 2, z] = rows
+                value = value * product_ref[z]
+            product_ref[z] = value
+            if v == views - 1:
+                for top in range(0, value.shape[0], 8):
+                    most[0] = jnp.maximum(most[0], value[top : top + 8])
 
         z_view = z_ref.at[1, v * tall : (v + 1) * tall]
-        filter_to(load, 1, 2, z_view, x_ref.at[1, v : v + 1], y_ref.at[1, v : v + 1], scale_ref.at[v : v + 1], e_ref, g_ref, True, emit)
+        filter_to(
+            load,
+            1,
+            2,
+            z_view,
+            x_ref.at[1, v : v + 1],
+            y_ref.at[1, v : v + 1],
+            scale_ref.at[v : v + 1],
+            e_ref,
+            g_ref,
+            True,
+            emit,
+        )
+    top = jnp.maximum(jnp.max(most[0], axis=(0, 1), keepdims=True), 1e-30)
+    quarter = jnp.ceil(jnp.log2(top) * 0.25)
+    scale = jnp.exp2(-4.0 * quarter)
+    root = jnp.broadcast_to(jnp.exp2(quarter), (part, product_ref.shape[2]))
+    for z in range(planes):
+        value = product_ref[z] * scale
+        for b in range(4):
+            (keep_ref, send_ref)[b % 2][b // 2, z] = value[b * part : (b + 1) * part]
+    for ref in (keep_ref, send_ref):
+        for b in range(2):
+            ref[b, planes] = root
 
 
 def local(estimate, recordings, psf_taps):
@@ -276,58 +305,67 @@
     both_ways += [(4 * i + w, 4 * j + w) for w in (1, 3) for i, j in down]
     mine = lax.ppermute(rounded, ("gz", "view"), both_ways)
 
+    last, first = pl.pallas_call(
+        edges_kernel,
+        out_shape=[shape((views, margin, rows, cols), BF16)] * 2,
+        in_specs=[HBM],
+        out_specs=[VMEM] * 2,
+        scratch_shapes=[pltpu.SemaphoreType.DMA((2 * views,))],
+        name="edges",
+        **params(10**4, 10**4),
+    )(recordings)
+    before = lax.ppermute(last, "gz", up)
+    after = lax.ppermute(first, "gz", down)
+
     wide = -(-(z_out + taps - 1) * 8 // 128) * 128
-    z_mat, x_mat, y_mat, scales, last, first = pl.pallas_call(
+    z_mat, x_mat, y_mat, scales = pl.pallas_call(
         matrices_kernel,
         out_shape=[
             shape((2, views * 2 * z_out * 8, wide), BF16),
             shape((2, views, 2 * cols, 2 * cols), BF16),
             shape((2, views, rows, 2 * rows), BF16),
             shape((views, 2, 1, 128), F32),
-            shape((views, margin, rows, cols), BF16),
-            shape((views, margin, rows, cols), BF16),
         ],
-        in_specs=[SMEM, SMEM, HBM],
-        out_specs=[VMEM] * 6,
-        scratch_shapes=[pltpu.SemaphoreType.DMA((2 * views,))],
+        in_specs=[SMEM, SMEM],
+        out_specs=[VMEM] * 4,
         name="matrices",
         **params(10**6, 10**4),
-    )(place_array, psf_taps, recordings)
-
-    before = lax.ppermute(last, "gz", up)
-    after = lax.ppermute(first, "gz", down)
+    )(place_array, psf_taps)
+
     mine, z_mat = lax.optimization_barrier((mine, z_mat))
-    other = lax.ppermute(mine, "view", swap)
-
-    own, rim = pl.pallas_call(
-        quotient_kernel,
-        out_shape=[shape((views, planes, rows, cols), BF16), shape((views, 2, margin, rows, cols), F32)],
-        in_specs=[SMEM] + [VMEM] * 8,
-        out_specs=[VMEM] * 2,
-        scratch_shapes=scratch(views, 4, 1, z_out, rows, cols),
-        name="quotients",
-        **params(10**6, 10**4),
-    )(place_array, mine, other, rounded, recordings, z_mat, x_mat, y_mat, scales)
+    mine = (mine[:margin], mine[margin:])
+    other = [lax.ppermute(piece, "view", swap) for piece in mine]
+    inverses = []
+    for early, side in ((True, mine), (False, other)):
+        inverses.append(
+            pl.pallas_call(
+                lambda *refs, early=early: inverse_kernel(early, *refs),
+                out_shape=shape((views, planes, rows, cols), F32),
+                in_specs=[SMEM] + [VMEM] * 7,
+                out_specs=VMEM,
+                scratch_shapes=scratch(views, 2, 1, z_out, rows, cols),
+                name="inverses",
+                **params(10**6, 10**4),
+            )(place_array, *side, rounded, z_mat, x_mat, y_mat, scales)
+        )
     part = rows // 4
     keep, send = pl.pallas_call(
         correction_kernel,
-        out_shape=[shape((2, planes, part, cols), F32)] * 2,
-        in_specs=[VMEM] * 8,
+        out_shape=[shape((2, planes + 1, part, cols), F32)] * 2,
+        in_specs=[SMEM] + [VMEM] * 9,
         out_specs=[VMEM] * 2,
         scratch_shapes=scratch(1, 2, 2, z_out, rows, cols) + [pltpu.VMEM((planes, rows, cols), F32)],
         name="corrections",
         **params(4 * 10**9, 5 * 10**6),
-    )(before, own, after, rim, z_mat, x_mat, y_mat, scales)
+    )(place_array, before, recordings, after, *inverses, z_mat, x_mat, y_mat, scales)
     core = lax.ppermute(send, "view", swap)
-    product = keep[1] * core[1]
-    most = jnp.maximum(jnp.max(product), 1e-30)
-    exponent = jnp.floor(jnp.log2(most)) - 14.0
-    coded = (product * jnp.exp2(-exponent)).astype(jnp.float16)
-    tail = jnp.broadcast_to(exponent.astype(jnp.float16), (1, part, cols))
-    across = lax.ppermute(jnp.concatenate([coded, tail]), "view", [(i, i ^ 2) for i in range(4)])
+    across = lax.ppermute((keep[1] * core[1]).astype(jnp.float16), "view", [(i, i ^ 2) for i in range(4)])
     own_rows = lax.dynamic_slice_in_dim(estimate, place * part, part, 1)
-    partial, across = lax.optimization_barrier((own_rows * (keep[0] * core[0]), across))
-    return partial * (across[:planes].astype(F32) * jnp.exp2(across[planes:].astype(F32)))
+    root = keep[0, planes] * core[0, planes]
+    partial = own_rows * (keep[0, :planes] * core[0, :planes])
+    partial, root, across = lax.optimization_barrier((partial, root, across))
+    root = root * across[planes].astype(F32)
+    return partial * (across[:planes].astype(F32) * (root * root * root * root))
 
 
 def solution(mesh):

time: 60.3 us -> 51.6 us (0.86)
  waiting for transfers between devices: 25.6 us -> 12.6 us
  starting transfers between devices: 15.6 us -> 19 us
  local copies, waits for them, and re-layouts: 0.05 us -> 3.07 us
  Pallas kernels: 13.9 us -> 13 us
  between operations: 0.85 us -> 0.14 us
  other arithmetic: 4.1 us -> 3.42 us
    ppermute x1, waiting for transfers between devices: 10.6 us -> 0.91 us  [local(): mine = lax.ppermute(rounded, ('gz', 'view'), both_ways)]
    ppermute x2 -> x3, starting transfers between devices: 2.83 us -> 6.11 us  [the longest x2 3.29 us: local(): other = [lax.ppermute(piece, 'view', swap) for piece in mine]]
    ppermute x1, waiting for transfers between devices: 7.68 us -> 5.51 us  [local(): before = lax.ppermute(last, 'gz', up)]
    unnamed x4 -> x8, local copies, waits for them, and re-layouts: 0.01 us -> 1.95 us
    ppermute x1, starting transfers between devices: 1.91 us -> 3.83 us  [local(): before = lax.ppermute(last, 'gz', up)]
    ppermute x1, starting transfers between devices: 6.93 us -> 5.06 us  [local(): after = lax.ppermute(first, 'gz', down)]
    ppermute x1, waiting for transfers between devices: 1.18 us -> 0.01 us  [local(): after = lax.ppermute(first, 'gz', down)]
    slice x0 -> x1, local copies, waits for them, and re-layouts: none -> 1.13 us  [local(): mine = (mine[:margin], mine[margin:])]
  transfers between devices with their start and end apart: 6 -> 7, of which waited for: 5 -> 4; matrix products, arithmetic and copies ran while one was open for 2% -> 4% of each run, Pallas kernels for 14% -> 15%
where the time goes in v4:
time: 51.6 us; the launch traced here: 51.2 us
  starting transfers between devices  19 us (37%)
  Pallas kernels  13 us (25%)
  waiting for transfers between devices  12.6 us (24%)
  other arithmetic  3.42 us (7%)
  local copies, waits for them, and re-layouts  3.07 us (6%)
    ppermute x1, waiting for transfers between devices, local(): before = lax.ppermute(last, 'gz', up)  5.51 us
    pallas_call x1, Pallas kernels, local(): pl.pallas_call(correction_kernel, out_shape=[shape((2, planes + 1, part,...  5.29 us
    ppermute x1, starting transfers between devices, local(): after = lax.ppermute(first, 'gz', down)  5.06 us
    ppermute x1, waiting for transfers between devices, local(): lax.ppermute((keep[1] * core[1]).astype(jnp.float16), 'view', [(i, i ^ 2)...  4.13 us
    pallas_call x2, Pallas kernels, local(): pl.pallas_call(lambda *refs, early=early: inverse_kernel(early, *refs), o...  3.86 us
    ppermute x1, starting transfers between devices, local(): mine = lax.ppermute(rounded, ('gz', 'view'), both_ways)  3.83 us
    ppermute x1, starting transfers between devices, local(): before = lax.ppermute(last, 'gz', up)  3.83 us
    ppermute x2, starting transfers between devices, local(): other = [lax.ppermute(piece, 'view', swap) for piece in mine]  3.29 us
  transfers between devices with their start and end apart: 7, of which 4 were waited for; matrix products, arithmetic and copies ran while one was open for 4% of the time, Pallas kernels for 15%

profile of v4, /device:TPU:24, one launch (start us, length us, event | category | flops | bytes accessed | tf_op | source)
XLA Modules:
  0.0 51.2 jit_solution(1779558560751544512)
XLA Ops:
  0.0 0.0 copy-start
  0.0 0.0 copy-start.1
  0.0 1.5 %convert_element_type.18.refs_3_ = bf16[20,128,128]{2,1,0:T(8,128)(2,1)S(1)} convert(f32[20,128,128]{2,1,0:T(8,128)} %param.3) | non-fusion elementwise | flops 327680 | bytes 1966080 | tf_op jit(solution)/shard_map/convert_element_type | solution.py:303
  1.5 3.8 %collective-permute-start.2 = (bf16[20,128,128]{2,1,0:T(8,128)(2,1)S(1)}, bf16[20,128,128]{2,1,0:T(8,128)(2,1)}, u32[]{:S(2)}, u32[]{:S(2)}) collective-permute-start(bf16[20,128,128]{2,1,0:T(8,128)(2,1)S(1)} %convert_element_type.18.refs_3_), channel_id=1, source_target_pairs={{0,4},{4,8},{8,12},{12,16},{16,20},{20,24},{24,28},{28,32},{32,36}... | collective-permute-start | bytes 1966088 | tf_op jit(solution)/shard_map/ppermute | solution.py:306
  5.4 0.0 copy-done
  5.4 1.3 %edges.1 = (bf16[2,10,128,128]{3,2,1,0:T(8,128)(2,1)}, bf16[2,10,128,128]{3,2,1,0:T(8,128)(2,1)S(1)}) custom-call(bf16[2,20,128,128]{3,2,1,0:T(8,128)(2,1)S(1)} %copy-done), custom_call_target="tpu_custom_call" | custom-call | flops 10000 | bytes 10000 | tf_op jit(solution)/shard_map/edges/pallas_call | solution.py:308
  6.7 3.8 %collective-permute-start = (bf16[2,10,128,128]{3,2,1,0:T(8,128)(2,1)}, bf16[2,10,128,128]{3,2,1,0:T(8,128)(2,1)S(1)}, u32[]{:S(2)}, u32[]{:S(2)}) collective-permute-start(bf16[2,10,128,128]{3,2,1,0:T(8,128)(2,1)} %get-tuple-element.18), channel_id=1, source_target_pairs={{0,4},{4,8},{8,12},{12,16},{16,20},{20,24},{24,28},{28,32},{32,36}... | collective-permute-start | bytes 1966088 | tf_op jit(solution)/shard_map/ppermute | solution.py:317
  10.5 5.1 %collective-permute-start.1 = (bf16[2,10,128,128]{3,2,1,0:T(8,128)(2,1)S(1)}, bf16[2,10,128,128]{3,2,1,0:T(8,128)(2,1)}, u32[]{:S(2)}, u32[]{:S(2)}) collective-permute-start(bf16[2,10,128,128]{3,2,1,0:T(8,128)(2,1)S(1)} %get-tuple-element.19), channel_id=1, source_target_pairs={{4,0},{8,4},{12,8},{16,12},{20,16},{24,20},{28,24},{32,28},{36,32}... | collective-permute-start | bytes 1966088 | tf_op jit(solution)/shard_map/ppermute | solution.py:318
  15.6 0.0 copy-done.1
  15.6 2.5 %matrices.1 = (bf16[2,320,256]{2,1,0:T(8,128)(2,1)S(1)}, bf16[2,2,256,256]{3,2,1,0:T(8,128)(2,1)S(1)}, bf16[2,2,128,256]{3,2,1,0:T(8,128)(2,1)S(1)}, f32[2,2,1,128]{3,2,1,0:T(1,128)S(1)}) custom-call(s32[1]{0:T(128)} %bitcast.place_ref.refs_0_, f32[2,3,2,21]{3,2,1,0:T(2,128)S(1)} %copy-done.1), custom_call_target="tpu_custom_call" | custom-call | flops 1000000 | bytes 10000 | tf_op jit(solution)/shard_map/matrices/pallas_call | solution.py:321
  18.2 0.9 %collective-permute-done.2 = bf16[20,128,128]{2,1,0:T(8,128)(2,1)} collective-permute-done((bf16[20,128,128]{2,1,0:T(8,128)(2,1)S(1)}, bf16[20,128,128]{2,1,0:T(8,128)(2,1)}, u32[]{:S(2)}, u32[]{:S(2)}) %collective-permute-start.2) | collective-permute-done | bytes 655392 | tf_op jit(solution)/shard_map/ppermute | solution.py:306
  19.1 1.1 %fusion.5 = (bf16[10,128,128]{2,1,0:T(8,128)(2,1)S(1)}, bf16[10,128,128]{2,1,0:T(8,128)(2,1)S(1)}) fusion(bf16[20,128,128]{2,1,0:T(8,128)(2,1)} %collective-permute-done.2), kind=kLoop, calls=%fused_computation.11 | loop fusion | bytes 1310720 | tf_op jit(solution)/shard_map/slice | solution.py:336
  20.2 3.2 %collective-permute-start.3 = (bf16[10,128,128]{2,1,0:T(8,128)(2,1)S(1)}, bf16[10,128,128]{2,1,0:T(8,128)(2,1)S(1)}, u32[]{:S(2)}, u32[]{:S(2)}) collective-permute-start(bf16[10,128,128]{2,1,0:T(8,128)(2,1)S(1)} %get-tuple-element.32.refs_1_), channel_id=1, source_target_pairs={{0,1},{1,0},{2,3},{3,2},{4,5},{5,4},{6,7},{7,6},{8,9},{9,8},{10,11... | collective-permute-start | bytes 983048 | tf_op jit(solution)/shard_map/ppermute | solution.py:337
  23.4 0.1 collective-permute-start.4
  23.5 1.9 %inverses.2.early_ref = f32[2,20,128,128]{3,2,1,0:T(8,128)S(1)} custom-call(s32[1]{0:T(128)} %bitcast.place_ref.refs_0_, bf16[10,128,128]{2,1,0:T(8,128)(2,1)S(1)} %get-tuple-element.32.refs_1_, bf16[10,128,128]{2,1,0:T(8,128)(2,1)S(1)} %get-tuple-element.31.refs_2_, bf16[20,128,128]{2,1,0:T(8,128)(2,1)S(1)} %convert_element_type.18.refs_3_, ...), custom_call_target="tpu_custom_call" | custom-call | flops 1000000 | bytes 10000 | tf_op jit(solution)/shard_map/inverses/pallas_call | solution.py:341
  25.4 0.0 collective-permute-done.3.refs_1_
  25.4 0.0 collective-permute-done.4.refs_2_
  25.5 1.9 %inverses.3.late_ref = f32[2,20,128,128]{3,2,1,0:T(8,128)S(1)} custom-call(s32[1]{0:T(128)} %bitcast.place_ref.refs_0_, bf16[10,128,128]{2,1,0:T(8,128)(2,1)S(1)} %collective-permute-done.3.refs_1_, bf16[10,128,128]{2,1,0:T(8,128)(2,1)S(1)} %collective-permute-done.4.refs_2_, bf16[20,128,128]{2,1,0:T(8,128)(2,1)S(1)} %convert_element_type.18.refs_3_, ...), custom_call_target="tpu_custom_call" | custom-call | flops 1000000 | bytes 10000 | tf_op jit(solution)/shard_map/inverses/pallas_call | solution.py:341
  27.4 5.5 %collective-permute-done.before_ref = bf16[2,10,128,128]{3,2,1,0:T(8,128)(2,1)S(1)} collective-permute-done((bf16[2,10,128,128]{3,2,1,0:T(8,128)(2,1)}, bf16[2,10,128,128]{3,2,1,0:T(8,128)(2,1)S(1)}, u32[]{:S(2)}, u32[]{:S(2)}) %collective-permute-start) | collective-permute-done | bytes 655392 | tf_op jit(solution)/shard_map/ppermute | solution.py:317
  32.9 0.0 copy-start.2
  32.9 0.9 %copy-done.2 = bf16[2,10,128,128]{3,2,1,0:T(8,128)(2,1)} copy-done((bf16[2,10,128,128]{3,2,1,0:T(8,128)(2,1)}, bf16[2,10,128,128]{3,2,1,0:T(8,128)(2,1)S(1)}, u32[]{:S(2)}) %copy-start.2) | copy-done | bytes 655384
  33.8 0.0 collective-permute-done.1.after_ref
  33.8 0.0 copy-start.3
  33.8 1.1 %copy-done.3 = bf16[2,10,128,128]{3,2,1,0:T(8,128)(2,1)S(1)} copy-done((bf16[2,10,128,128]{3,2,1,0:T(8,128)(2,1)S(1)}, bf16[2,10,128,128]{3,2,1,0:T(8,128)(2,1)}, u32[]{:S(2)}) %copy-start.3) | copy-done | bytes 655384
  34.9 5.3 %corrections.1 = (f32[2,21,32,128]{3,2,1,0:T(8,128)S(1)}, f32[2,21,32,128]{3,2,1,0:T(8,128)S(1)}) custom-call(s32[1]{0:T(128)} %bitcast.place_ref.refs_0_, bf16[2,10,128,128]{3,2,1,0:T(8,128)(2,1)S(1)} %copy-done.3, bf16[2,20,128,128]{3,2,1,0:T(8,128)(2,1)S(1)} %copy-done, bf16[2,10,128,128]{3,2,1,0:T(8,128)(2,1)} %collective-permute-done.1.after_ref, ...), custom_call_target="tpu_custom_call" | custom-call | flops 4000000000 | bytes 5000000 | tf_op jit(solution)/shard_map/corrections/pallas_call | solution.py:352
  40.2 0.2 collective-permute-start.5
  40.4 2.0 %collective-permute-done.5 = f32[2,21,32,128]{3,2,1,0:T(8,128)S(1)} collective-permute-done((f32[2,21,32,128]{3,2,1,0:T(8,128)S(1)}, f32[2,21,32,128]{3,2,1,0:T(8,128)S(1)}, u32[]{:S(2)}, u32[]{:S(2)}) %collective-permute-start.5) | collective-permute-done | bytes 688160 | tf_op jit(solution)/shard_map/ppermute | solution.py:361
  42.4 0.1 fusion.3
  42.4 2.8 %collective-permute-start.6 = (f16[21,32,128]{2,1,0:T(8,128)(2,1)S(1)}, f16[21,32,128]{2,1,0:T(8,128)(2,1)S(1)}, u32[]{:S(2)}, u32[]{:S(2)}) collective-permute-start(f16[21,32,128]{2,1,0:T(8,128)(2,1)S(1)} %fusion.3), channel_id=1, source_target_pairs={{0,2},{1,3},{2,0},{3,1},{4,6},{5,7},{6,4},{7,5},{8,10},{9,11},{10,... | collective-permute-start | bytes 516104 | tf_op jit(solution)/shard_map/ppermute | solution.py:362
  45.3 1.1 %fusion.2 = f32[20,32,128]{2,1,0:T(8,128)S(1)} fusion(f32[2,21,32,128]{3,2,1,0:T(8,128)S(1)} %collective-permute-done.5, f32[2,21,32,128]{3,2,1,0:T(8,128)S(1)} %get-tuple-element.26, f32[20,128,128]{2,1,0:T(8,128)} %param.3, s32[]{:T(128)S(6)} %select_n.3), kind=kLoop, calls=%fused_computation.4 | loop fusion | flops 163840 | bytes 1310724 | tf_op jit(solution)/shard_map/mul | solution.py:365
  46.3 4.1 %collective-permute-done.6 = f16[21,32,128]{2,1,0:T(8,128)(2,1)S(1)} collective-permute-done((f16[21,32,128]{2,1,0:T(8,128)(2,1)S(1)}, f16[21,32,128]{2,1,0:T(8,128)(2,1)S(1)}, u32[]{:S(2)}, u32[]{:S(2)}) %collective-permute-start.6) | collective-permute-done | bytes 172064 | tf_op jit(solution)/shard_map/ppermute | solution.py:362
  50.5 0.8 %multiply_multiply_fusion = f32[20,32,128]{2,1,0:T(8,128)} fusion(f32[20,32,128]{2,1,0:T(8,128)S(1)} %fusion.2, f32[32,128]{1,0:T(8,128)S(1)} %multiply_multiply_fusion.1, f16[21,32,128]{2,1,0:T(8,128)(2,1)S(1)} %collective-permute-done.6), kind=kLoop, calls=%fused_computation.5 | loop fusion | flops 245760 | bytes 835584 | tf_op jit(solution)/shard_map/mul | solution.py:368
  (2 shorter events, 0.0 us)
Async XLA Ops:
  0.0 5.4 %copy-start = (bf16[2,20,128,128]{3,2,1,0:T(8,128)(2,1)S(1)}, bf16[2,20,128,128]{3,2,1,0:T(8,128)(2,1)}, u32[]{:S(2)}) copy-start(bf16[2,20,128,128]{3,2,1,0:T(8,128)(2,1)} %rec_ref.3) | copy-start | bytes 3932164
  0.0 15.6 %copy-start.1 = (f32[2,3,2,21]{3,2,1,0:T(2,128)S(1)}, f32[2,3,2,21]{3,2,1,0:T(2,128)}, u32[]{:S(2)}) copy-start(f32[2,3,2,21]{3,2,1,0:T(2,128)} %taps_ref.1) | copy-start | bytes 3028
  1.5 17.5 %collective-permute-start.2 = (bf16[20,128,128]{2,1,0:T(8,128)(2,1)S(1)}, bf16[20,128,128]{2,1,0:T(8,128)(2,1)}, u32[]{:S(2)}, u32[]{:S(2)}) collective-permute-start(bf16[20,128,128]{2,1,0:T(8,128)(2,1)S(1)} %convert_element_type.18.refs_3_), channel_id=1, source_target_pairs={{0,4},{4,8},{8,12},{12,16},{16,20},{20,24},{24,28},{28,32},{32,36}... | collective-permute-start | bytes 1966088 | tf_op jit(solution)/shard_map/ppermute | solution.py:306
  6.7 26.2 %collective-permute-start = (bf16[2,10,128,128]{3,2,1,0:T(8,128)(2,1)}, bf16[2,10,128,128]{3,2,1,0:T(8,128)(2,1)S(1)}, u32[]{:S(2)}, u32[]{:S(2)}) collective-permute-start(bf16[2,10,128,128]{3,2,1,0:T(8,128)(2,1)} %get-tuple-element.18), channel_id=1, source_target_pairs={{0,4},{4,8},{8,12},{12,16},{16,20},{20,24},{24,28},{28,32},{32,36}... | collective-permute-start | bytes 1966088 | tf_op jit(solution)/shard_map/ppermute | solution.py:317
  10.5 23.2 %collective-permute-start.1 = (bf16[2,10,128,128]{3,2,1,0:T(8,128)(2,1)S(1)}, bf16[2,10,128,128]{3,2,1,0:T(8,128)(2,1)}, u32[]{:S(2)}, u32[]{:S(2)}) collective-permute-start(bf16[2,10,128,128]{3,2,1,0:T(8,128)(2,1)S(1)} %get-tuple-element.19), channel_id=1, source_target_pairs={{4,0},{8,4},{12,8},{16,12},{20,16},{24,20},{28,24},{32,28},{36,32}... | collective-permute-start | bytes 1966088 | tf_op jit(solution)/shard_map/ppermute | solution.py:318
  20.2 5.2 %collective-permute-start.3 = (bf16[10,128,128]{2,1,0:T(8,128)(2,1)S(1)}, bf16[10,128,128]{2,1,0:T(8,128)(2,1)S(1)}, u32[]{:S(2)}, u32[]{:S(2)}) collective-permute-start(bf16[10,128,128]{2,1,0:T(8,128)(2,1)S(1)} %get-tuple-element.32.refs_1_), channel_id=1, source_target_pairs={{0,1},{1,0},{2,3},{3,2},{4,5},{5,4},{6,7},{7,6},{8,9},{9,8},{10,11... | collective-permute-start | bytes 983048 | tf_op jit(solution)/shard_map/ppermute | solution.py:337
  23.4 2.0 %collective-permute-start.4 = (bf16[10,128,128]{2,1,0:T(8,128)(2,1)S(1)}, bf16[10,128,128]{2,1,0:T(8,128)(2,1)S(1)}, u32[]{:S(2)}, u32[]{:S(2)}) collective-permute-start(bf16[10,128,128]{2,1,0:T(8,128)(2,1)S(1)} %get-tuple-element.31.refs_2_), channel_id=1, source_target_pairs={{0,1},{1,0},{2,3},{3,2},{4,5},{5,4},{6,7},{7,6},{8,9},{9,8},{10,11... | collective-permute-start | bytes 983048 | tf_op jit(solution)/shard_map/ppermute | solution.py:337
  32.9 0.9 %copy-start.2 = (bf16[2,10,128,128]{3,2,1,0:T(8,128)(2,1)}, bf16[2,10,128,128]{3,2,1,0:T(8,128)(2,1)S(1)}, u32[]{:S(2)}) copy-start(bf16[2,10,128,128]{3,2,1,0:T(8,128)(2,1)S(1)} %collective-permute-done.before_ref) | copy-start | bytes 1966084
  33.8 1.1 %copy-start.3 = (bf16[2,10,128,128]{3,2,1,0:T(8,128)(2,1)S(1)}, bf16[2,10,128,128]{3,2,1,0:T(8,128)(2,1)}, u32[]{:S(2)}) copy-start(bf16[2,10,128,128]{3,2,1,0:T(8,128)(2,1)} %copy-done.2) | copy-start | bytes 1966084
  40.2 2.2 %collective-permute-start.5 = (f32[2,21,32,128]{3,2,1,0:T(8,128)S(1)}, f32[2,21,32,128]{3,2,1,0:T(8,128)S(1)}, u32[]{:S(2)}, u32[]{:S(2)}) collective-permute-start(f32[2,21,32,128]{3,2,1,0:T(8,128)S(1)} %get-tuple-element.27), channel_id=1, source_target_pairs={{0,1},{1,0},{2,3},{3,2},{4,5},{5,4},{6,7},{7,6},{8,9},{9,8},{10,11... | collective-permute-start | bytes 2064392 | tf_op jit(solution)/shard_map/ppermute | solution.py:361
  42.4 8.0 %collective-permute-start.6 = (f16[21,32,128]{2,1,0:T(8,128)(2,1)S(1)}, f16[21,32,128]{2,1,0:T(8,128)(2,1)S(1)}, u32[]{:S(2)}, u32[]{:S(2)}) collective-permute-start(f16[21,32,128]{2,1,0:T(8,128)(2,1)S(1)} %fusion.3), channel_id=1, source_target_pairs={{0,2},{1,3},{2,0},{3,1},{4,6},{5,7},{6,4},{7,5},{8,10},{9,11},{10,... | collective-permute-start | bytes 516104 | tf_op jit(solution)/shard_map/ppermute | solution.py:362

commit v5 on v4

--- a/solution.py
+++ b/solution.py
@@ -37,6 +37,22 @@
         copy.start()
     for copy in copies:
         copy.wait()
+
+
+def prepare_kernel(est_ref, est_out, held, rounded, sems):
+    pieces = sems.shape[1]
+    step = est_ref.shape[0] // pieces
+    at = [slice(i * step, (i + 1) * step) for i in range(pieces)]
+    copies = [pltpu.make_async_copy(est_ref.at[at[i]], held.at[at[i]], sems.at[0, i]) for i in range(pieces)]
+    outs = [pltpu.make_async_copy(rounded.at[at[i]], est_out.at[at[i]], sems.at[1, i]) for i in range(pieces)]
+    for copy in copies:
+        copy.start()
+    for i in range(pieces):
+        copies[i].wait()
+        rounded[at[i]] = held[at[i]].astype(BF16)
+        outs[i].start()
+    for out in outs:
+        out.wait()
 
 
 def rounded_scale(tap, total):
@@ -300,7 +316,19 @@
     z_out = planes // 2
     shape = jax.ShapeDtypeStruct
 
-    rounded = estimate.astype(BF16)
+    rounded = pl.pallas_call(
+        prepare_kernel,
+        out_shape=shape((planes, rows, cols), BF16),
+        in_specs=[HBM],
+        out_specs=HBM,
+        scratch_shapes=[
+            pltpu.VMEM((planes, rows, cols), F32),
+            pltpu.VMEM((planes, rows, cols), BF16),
+            pltpu.SemaphoreType.DMA((2, 5)),
+        ],
+        name="prepare",
+        **params(10**6, 10**4, 58 * 1024 * 1024),
+    )(estimate)
     both_ways = [(4 * i + w, 4 * j + w) for w in (0, 2) for i, j in up]
     both_ways += [(4 * i + w, 4 * j + w) for w in (1, 3) for i, j in down]
     mine = lax.ppermute(rounded, ("gz", "view"), both_ways)
@@ -309,10 +337,10 @@
         edges_kernel,
         out_shape=[shape((views, margin, rows, cols), BF16)] * 2,
         in_specs=[HBM],
-        out_specs=[VMEM] * 2,
+        out_specs=[HBM] * 2,
         scratch_shapes=[pltpu.SemaphoreType.DMA((2 * views,))],
         name="edges",
-        **params(10**4, 10**4),
+        **params(10**4, 10**4, 58 * 1024 * 1024),
     )(recordings)
     before = lax.ppermute(last, "gz", up)
     after = lax.ppermute(first, "gz", down)

time: 51.6 us -> 86.7 us (1.68)
  Pallas kernels: 13 us -> 53.5 us
  waiting for transfers between devices: 12.6 us -> 7.96 us
  starting transfers between devices: 19 us -> 22.9 us
  local copies, waits for them, and re-layouts: 3.07 us -> 0.06 us
  other arithmetic: 3.42 us -> 1.9 us
    pallas_call x1, Pallas kernels: 1.3 us -> 40.8 us  [local(): pl.pallas_call(edges_kernel, out_shape=[shape((views, margin, rows, cols)...]
    ppermute x1, waiting for transfers between devices: 5.51 us -> 0.01 us  [local(): before = lax.ppermute(last, 'gz', up)]
    ppermute x1, starting transfers between devices: 0.2 us -> 2.77 us  [local(): core = lax.ppermute(send, 'view', swap)]
    ppermute x1, waiting for transfers between devices: 0.01 us -> 2.09 us  [local(): after = lax.ppermute(first, 'gz', down)]
    pallas_call x0 -> x1, Pallas kernels: none -> 2.03 us  [local(): pl.pallas_call(prepare_kernel, out_shape=shape((planes, rows, cols), BF16...]
    unnamed x8 -> x6, local copies, waits for them, and re-layouts: 1.95 us -> 0.01 us
    convert_element_type x1 -> x0, other arithmetic: 1.52 us -> none  [local(): rounded = estimate.astype(BF16)]
    slice x1, local copies, waits for them, and re-layouts: 1.13 us -> 0.04 us  [local(): mine = (mine[:margin], mine[margin:])]
  transfers between devices with their start and end apart: 7 -> 7, of which waited for: 4 -> 3; matrix products, arithmetic and copies ran while one was open for 4% -> 1% of each run, Pallas kernels for 15% -> 55%
where the time goes in v5:
time: 86.7 us; the launch traced here: 86.5 us
  Pallas kernels  53.5 us (62%)
  starting transfers between devices  22.9 us (26%)
  waiting for transfers between devices  7.96 us (9%)
  other arithmetic  1.9 us (2%)
    pallas_call x1, Pallas kernels, local(): pl.pallas_call(edges_kernel, out_shape=[shape((views, margin, rows, cols)...  40.8 us
    ppermute x1, starting transfers between devices, local(): after = lax.ppermute(first, 'gz', down)  5.06 us
    pallas_call x1, Pallas kernels, local(): pl.pallas_call(correction_kernel, out_shape=[shape((2, planes + 1, part,...  4.22 us
    ppermute x2, starting transfers between devices, local(): other = [lax.ppermute(piece, 'view', swap) for piece in mine]  4.19 us
    ppermute x1, waiting for transfers between devices, local(): lax.ppermute((keep[1] * core[1]).astype(jnp.float16), 'view', [(i, i ^ 2)...  4.09 us
    ppermute x1, starting transfers between devices, local(): mine = lax.ppermute(rounded, ('gz', 'view'), both_ways)  3.96 us
    pallas_call x2, Pallas kernels, local(): pl.pallas_call(lambda *refs, early=early: inverse_kernel(early, *refs), o...  3.87 us
    ppermute x1, starting transfers between devices, local(): before = lax.ppermute(last, 'gz', up)  3.83 us
  transfers between devices with their start and end apart: 7, of which 3 were waited for; matrix products, arithmetic and copies ran while one was open for 1% of the time, Pallas kernels for 55%

profile of v5, /device:TPU:24, one launch (start us, length us, event | category | flops | bytes accessed | tf_op | source)
XLA Modules:
  0.0 86.5 jit_solution(17804098473873979523)
XLA Ops:
  0.0 0.0 copy-start.2
  0.0 2.0 %prepare.1.refs_3_ = bf16[20,128,128]{2,1,0:T(8,128)(2,1)} custom-call(f32[20,128,128]{2,1,0:T(8,128)} %est_ref.1), custom_call_target="tpu_custom_call" | custom-call | flops 1000000 | bytes 10000 | tf_op jit(solution)/shard_map/prepare/pallas_call | solution.py:319
  2.0 0.0 copy-start
  2.0 4.0 %collective-permute-start.2 = (bf16[20,128,128]{2,1,0:T(8,128)(2,1)}, bf16[20,128,128]{2,1,0:T(8,128)(2,1)S(1)}, u32[]{:S(2)}, u32[]{:S(2)}) collective-permute-start(bf16[20,128,128]{2,1,0:T(8,128)(2,1)} %prepare.1.refs_3_), channel_id=1, source_target_pairs={{0,4},{4,8},{8,12},{12,16},{16,20},{20,24},{24,28},{28,32},{32,36}... | collective-permute-start | bytes 1966088 | tf_op jit(solution)/shard_map/ppermute | solution.py:334
  6.0 40.8 %edges.1 = (bf16[2,10,128,128]{3,2,1,0:T(8,128)(2,1)}, bf16[2,10,128,128]{3,2,1,0:T(8,128)(2,1)}) custom-call(bf16[2,20,128,128]{3,2,1,0:T(8,128)(2,1)} %rec_ref.3), custom_call_target="tpu_custom_call" | custom-call | flops 10000 | bytes 10000 | tf_op jit(solution)/shard_map/edges/pallas_call | solution.py:336
  46.9 3.8 %collective-permute-start = (bf16[2,10,128,128]{3,2,1,0:T(8,128)(2,1)}, bf16[2,10,128,128]{3,2,1,0:T(8,128)(2,1)S(1)}, u32[]{:S(2)}, u32[]{:S(2)}) collective-permute-start(bf16[2,10,128,128]{3,2,1,0:T(8,128)(2,1)} %get-tuple-element.18), channel_id=1, source_target_pairs={{0,4},{4,8},{8,12},{12,16},{16,20},{20,24},{24,28},{28,32},{32,36}... | collective-permute-start | bytes 1966088 | tf_op jit(solution)/shard_map/ppermute | solution.py:345
  50.7 5.1 %collective-permute-start.1 = (bf16[2,10,128,128]{3,2,1,0:T(8,128)(2,1)}, bf16[2,10,128,128]{3,2,1,0:T(8,128)(2,1)S(1)}, u32[]{:S(2)}, u32[]{:S(2)}) collective-permute-start(bf16[2,10,128,128]{3,2,1,0:T(8,128)(2,1)} %get-tuple-element.19), channel_id=1, source_target_pairs={{4,0},{8,4},{12,8},{16,12},{20,16},{24,20},{28,24},{32,28},{36,32}... | collective-permute-start | bytes 1966088 | tf_op jit(solution)/shard_map/ppermute | solution.py:346
  55.8 0.0 copy-done.2
  55.8 2.5 %matrices.1 = (bf16[2,320,256]{2,1,0:T(8,128)(2,1)S(1)}, bf16[2,2,256,256]{3,2,1,0:T(8,128)(2,1)S(1)}, bf16[2,2,128,256]{3,2,1,0:T(8,128)(2,1)S(1)}, f32[2,2,1,128]{3,2,1,0:T(1,128)S(1)}) custom-call(s32[1]{0:T(128)} %bitcast.place_ref.refs_0_, f32[2,3,2,21]{3,2,1,0:T(2,128)S(1)} %copy-done.2), custom_call_target="tpu_custom_call" | custom-call | flops 1000000 | bytes 10000 | tf_op jit(solution)/shard_map/matrices/pallas_call | solution.py:349
  58.3 0.0 collective-permute-done.2
  58.4 4.1 %collective-permute-start.3 = (bf16[10,128,128]{2,1,0:T(8,128)(2,1)S(1)}, bf16[10,128,128]{2,1,0:T(8,128)(2,1)S(1)}, u32[]{:S(2)}, u32[]{:S(2)}) collective-permute-start(bf16[10,128,128]{2,1,0:T(8,128)(2,1)S(1)} %get-tuple-element.32.refs_1_), channel_id=1, source_target_pairs={{0,1},{1,0},{2,3},{3,2},{4,5},{5,4},{6,7},{7,6},{8,9},{9,8},{10,11... | collective-permute-start | bytes 983048 | tf_op jit(solution)/shard_map/ppermute | solution.py:365
  62.5 0.1 collective-permute-start.4
  62.6 0.0 copy-done
  62.6 1.9 %inverses.2.early_ref = f32[2,20,128,128]{3,2,1,0:T(8,128)S(1)} custom-call(s32[1]{0:T(128)} %bitcast.place_ref.refs_0_, bf16[10,128,128]{2,1,0:T(8,128)(2,1)S(1)} %get-tuple-element.32.refs_1_, bf16[10,128,128]{2,1,0:T(8,128)(2,1)S(1)} %get-tuple-element.31.refs_2_, bf16[20,128,128]{2,1,0:T(8,128)(2,1)S(1)} %copy-done, ...), custom_call_target="tpu_custom_call" | custom-call | flops 1000000 | bytes 10000 | tf_op jit(solution)/shard_map/inverses/pallas_call | solution.py:369
  64.5 0.0 copy-start.1
  64.5 0.0 collective-permute-done.3.refs_1_
  64.6 0.0 collective-permute-done.4.refs_2_
  64.6 1.9 %inverses.3.late_ref = f32[2,20,128,128]{3,2,1,0:T(8,128)S(1)} custom-call(s32[1]{0:T(128)} %bitcast.place_ref.refs_0_, bf16[10,128,128]{2,1,0:T(8,128)(2,1)S(1)} %collective-permute-done.3.refs_1_, bf16[10,128,128]{2,1,0:T(8,128)(2,1)S(1)} %collective-permute-done.4.refs_2_, bf16[20,128,128]{2,1,0:T(8,128)(2,1)S(1)} %copy-done, ...), custom_call_target="tpu_custom_call" | custom-call | flops 1000000 | bytes 10000 | tf_op jit(solution)/shard_map/inverses/pallas_call | solution.py:369
  66.5 0.0 collective-permute-done.before_ref
  66.5 2.1 %collective-permute-done.1.after_ref = bf16[2,10,128,128]{3,2,1,0:T(8,128)(2,1)S(1)} collective-permute-done((bf16[2,10,128,128]{3,2,1,0:T(8,128)(2,1)}, bf16[2,10,128,128]{3,2,1,0:T(8,128)(2,1)S(1)}, u32[]{:S(2)}, u32[]{:S(2)}) %collective-permute-start.1) | collective-permute-done | bytes 655392 | tf_op jit(solution)/shard_map/ppermute | solution.py:346
  68.6 0.0 copy-done.1
  68.6 4.2 %corrections.1 = (f32[2,21,32,128]{3,2,1,0:T(8,128)S(1)}, f32[2,21,32,128]{3,2,1,0:T(8,128)S(1)}) custom-call(s32[1]{0:T(128)} %bitcast.place_ref.refs_0_, bf16[2,10,128,128]{3,2,1,0:T(8,128)(2,1)S(1)} %collective-permute-done.before_ref, bf16[2,20,128,128]{3,2,1,0:T(8,128)(2,1)S(1)} %copy-done.1, ...), custom_call_target="tpu_custom_call" | custom-call | flops 4000000000 | bytes 5000000 | tf_op jit(solution)/shard_map/corrections/pallas_call | solution.py:380
  72.8 2.8 %collective-permute-start.5 = (f32[2,21,32,128]{3,2,1,0:T(8,128)S(1)}, f32[2,21,32,128]{3,2,1,0:T(8,128)S(1)}, u32[]{:S(2)}, u32[]{:S(2)}) collective-permute-start(f32[2,21,32,128]{3,2,1,0:T(8,128)S(1)} %get-tuple-element.27), channel_id=1, source_target_pairs={{0,1},{1,0},{2,3},{3,2},{4,5},{5,4},{6,7},{7,6},{8,9},{9,8},{10,11... | collective-permute-start | bytes 2064392 | tf_op jit(solution)/shard_map/ppermute | solution.py:389
  75.6 1.8 %collective-permute-done.5 = f32[2,21,32,128]{3,2,1,0:T(8,128)S(1)} collective-permute-done((f32[2,21,32,128]{3,2,1,0:T(8,128)S(1)}, f32[2,21,32,128]{3,2,1,0:T(8,128)S(1)}, u32[]{:S(2)}, u32[]{:S(2)}) %collective-permute-start.5) | collective-permute-done | bytes 688160 | tf_op jit(solution)/shard_map/ppermute | solution.py:389
  77.4 0.1 fusion.3
  77.4 3.1 %collective-permute-start.6 = (f16[21,32,128]{2,1,0:T(8,128)(2,1)S(1)}, f16[21,32,128]{2,1,0:T(8,128)(2,1)S(1)}, u32[]{:S(2)}, u32[]{:S(2)}) collective-permute-start(f16[21,32,128]{2,1,0:T(8,128)(2,1)S(1)} %fusion.3), channel_id=1, source_target_pairs={{0,2},{1,3},{2,0},{3,1},{4,6},{5,7},{6,4},{7,5},{8,10},{9,11},{10,... | collective-permute-start | bytes 516104 | tf_op jit(solution)/shard_map/ppermute | solution.py:390
  80.5 1.1 %fusion.2 = f32[20,32,128]{2,1,0:T(8,128)S(1)} fusion(f32[2,21,32,128]{3,2,1,0:T(8,128)S(1)} %collective-permute-done.5, f32[2,21,32,128]{3,2,1,0:T(8,128)S(1)} %get-tuple-element.26, f32[20,128,128]{2,1,0:T(8,128)} %est_ref.1, s32[]{:T(128)S(6)} %select_n.3), kind=kLoop, calls=%fused_computation.4 | loop fusion | flops 163840 | bytes 1310724 | tf_op jit(solution)/shard_map/mul | solution.py:393
  81.6 4.1 %collective-permute-done.6 = f16[21,32,128]{2,1,0:T(8,128)(2,1)S(1)} collective-permute-done((f16[21,32,128]{2,1,0:T(8,128)(2,1)S(1)}, f16[21,32,128]{2,1,0:T(8,128)(2,1)S(1)}, u32[]{:S(2)}, u32[]{:S(2)}) %collective-permute-start.6) | collective-permute-done | bytes 172064 | tf_op jit(solution)/shard_map/ppermute | solution.py:390
  85.7 0.8 multiply_multiply_fusion
  (3 shorter events, 0.1 us)
Async XLA Ops:
  0.0 55.8 %copy-start.2 = (f32[2,3,2,21]{3,2,1,0:T(2,128)S(1)}, f32[2,3,2,21]{3,2,1,0:T(2,128)}, u32[]{:S(2)}) copy-start(f32[2,3,2,21]{3,2,1,0:T(2,128)} %taps_ref.1) | copy-start | bytes 3028
  2.0 60.6 %copy-start = (bf16[20,128,128]{2,1,0:T(8,128)(2,1)S(1)}, bf16[20,128,128]{2,1,0:T(8,128)(2,1)}, u32[]{:S(2)}) copy-start(bf16[20,128,128]{2,1,0:T(8,128)(2,1)} %prepare.1.refs_3_) | copy-start | bytes 1966084
  2.0 56.3 %collective-permute-start.2 = (bf16[20,128,128]{2,1,0:T(8,128)(2,1)}, bf16[20,128,128]{2,1,0:T(8,128)(2,1)S(1)}, u32[]{:S(2)}, u32[]{:S(2)}) collective-permute-start(bf16[20,128,128]{2,1,0:T(8,128)(2,1)} %prepare.1.refs_3_), channel_id=1, source_target_pairs={{0,4},{4,8},{8,12},{12,16},{16,20},{20,24},{24,28},{28,32},{32,36}... | collective-permute-start | bytes 1966088 | tf_op jit(solution)/shard_map/ppermute | solution.py:334
  46.9 19.6 %collective-permute-start = (bf16[2,10,128,128]{3,2,1,0:T(8,128)(2,1)}, bf16[2,10,128,128]{3,2,1,0:T(8,128)(2,1)S(1)}, u32[]{:S(2)}, u32[]{:S(2)}) collective-permute-start(bf16[2,10,128,128]{3,2,1,0:T(8,128)(2,1)} %get-tuple-element.18), channel_id=1, source_target_pairs={{0,4},{4,8},{8,12},{12,16},{16,20},{20,24},{24,28},{28,32},{32,36}... | collective-permute-start | bytes 1966088 | tf_op jit(solution)/shard_map/ppermute | solution.py:345
  50.7 17.9 %collective-permute-start.1 = (bf16[2,10,128,128]{3,2,1,0:T(8,128)(2,1)}, bf16[2,10,128,128]{3,2,1,0:T(8,128)(2,1)S(1)}, u32[]{:S(2)}, u32[]{:S(2)}) collective-permute-start(bf16[2,10,128,128]{3,2,1,0:T(8,128)(2,1)} %get-tuple-element.19), channel_id=1, source_target_pairs={{4,0},{8,4},{12,8},{16,12},{20,16},{24,20},{28,24},{32,28},{36,32}... | collective-permute-start | bytes 1966088 | tf_op jit(solution)/shard_map/ppermute | solution.py:346
  58.4 6.2 %collective-permute-start.3 = (bf16[10,128,128]{2,1,0:T(8,128)(2,1)S(1)}, bf16[10,128,128]{2,1,0:T(8,128)(2,1)S(1)}, u32[]{:S(2)}, u32[]{:S(2)}) collective-permute-start(bf16[10,128,128]{2,1,0:T(8,128)(2,1)S(1)} %get-tuple-element.32.refs_1_), channel_id=1, source_target_pairs={{0,1},{1,0},{2,3},{3,2},{4,5},{5,4},{6,7},{7,6},{8,9},{9,8},{10,11... | collective-permute-start | bytes 983048 | tf_op jit(solution)/shard_map/ppermute | solution.py:365
  62.5 2.1 %collective-permute-start.4 = (bf16[10,128,128]{2,1,0:T(8,128)(2,1)S(1)}, bf16[10,128,128]{2,1,0:T(8,128)(2,1)S(1)}, u32[]{:S(2)}, u32[]{:S(2)}) collective-permute-start(bf16[10,128,128]{2,1,0:T(8,128)(2,1)S(1)} %get-tuple-element.31.refs_2_), channel_id=1, source_target_pairs={{0,1},{1,0},{2,3},{3,2},{4,5},{5,4},{6,7},{7,6},{8,9},{9,8},{10,11... | collective-permute-start | bytes 983048 | tf_op jit(solution)/shard_map/ppermute | solution.py:365
  64.5 4.1 %copy-start.1 = (bf16[2,20,128,128]{3,2,1,0:T(8,128)(2,1)S(1)}, bf16[2,20,128,128]{3,2,1,0:T(8,128)(2,1)}, u32[]{:S(2)}) copy-start(bf16[2,20,128,128]{3,2,1,0:T(8,128)(2,1)} %rec_ref.3) | copy-start | bytes 3932164
  72.8 4.5 %collective-permute-start.5 = (f32[2,21,32,128]{3,2,1,0:T(8,128)S(1)}, f32[2,21,32,128]{3,2,1,0:T(8,128)S(1)}, u32[]{:S(2)}, u32[]{:S(2)}) collective-permute-start(f32[2,21,32,128]{3,2,1,0:T(8,128)S(1)} %get-tuple-element.27), channel_id=1, source_target_pairs={{0,1},{1,0},{2,3},{3,2},{4,5},{5,4},{6,7},{7,6},{8,9},{9,8},{10,11... | collective-permute-start | bytes 2064392 | tf_op jit(solution)/shard_map/ppermute | solution.py:389
  77.4 8.2 %collective-permute-start.6 = (f16[21,32,128]{2,1,0:T(8,128)(2,1)S(1)}, f16[21,32,128]{2,1,0:T(8,128)(2,1)S(1)}, u32[]{:S(2)}, u32[]{:S(2)}) collective-permute-start(f16[21,32,128]{2,1,0:T(8,128)(2,1)S(1)} %fusion.3), channel_id=1, source_target_pairs={{0,2},{1,3},{2,0},{3,1},{4,6},{5,7},{6,4},{7,5},{8,10},{9,11},{10,... | collective-permute-start | bytes 516104 | tf_op jit(solution)/shard_map/ppermute | solution.py:390

commit v6 on v4

--- a/solution.py
+++ b/solution.py
@@ -25,18 +25,22 @@
     )
 
 
-def edges_kernel(rec_ref, last_out, first_out, sems):
+def edges_kernel(rec_ref, last_out, first_out, held, sems):
+    views, planes = rec_ref.shape[:2]
     margin = last_out.shape[1]
-    copies = []
-    for v in range(rec_ref.shape[0]):
-        for out, begin in ((last_out, rec_ref.shape[1] - margin), (first_out, 0)):
-            copies.append(
-                pltpu.make_async_copy(rec_ref.at[v, pl.ds(begin, margin)], out.at[v], sems.at[len(copies)])
-            )
+    copies, outs = [], []
+    for v in range(views):
+        for out, begin in ((last_out, planes - margin), (first_out, 0)):
+            i = len(copies)
+            copies.append(pltpu.make_async_copy(rec_ref.at[v, pl.ds(begin, margin)], held.at[i], sems.at[0, i]))
+            outs.append(pltpu.make_async_copy(held.at[i], out.at[v], sems.at[1, i]))
     for copy in copies:
         copy.start()
-    for copy in copies:
+    for copy, out in zip(copies, outs):
         copy.wait()
+        out.start()
+    for out in outs:
+        out.wait()
 
 
 def rounded_scale(tap, total):
@@ -309,10 +313,13 @@
         edges_kernel,
         out_shape=[shape((views, margin, rows, cols), BF16)] * 2,
         in_specs=[HBM],
-        out_specs=[VMEM] * 2,
-        scratch_shapes=[pltpu.SemaphoreType.DMA((2 * views,))],
+        out_specs=[HBM] * 2,
+        scratch_shapes=[
+            pltpu.VMEM((2 * views, margin, rows, cols), BF16),
+            pltpu.SemaphoreType.DMA((2, 2 * views)),
+        ],
         name="edges",
-        **params(10**4, 10**4),
+        **params(10**4, 10**4, 58 * 1024 * 1024),
     )(recordings)
     before = lax.ppermute(last, "gz", up)
     after = lax.ppermute(first, "gz", down)

time: 51.6 us -> 48.1 us (0.932)
  local copies, waits for them, and re-layouts: 3.07 us -> 0.05 us
  starting transfers between devices: 19 us -> 20.6 us
  waiting for transfers between devices: 12.6 us -> 11.1 us
    unnamed x8 -> x4, local copies, waits for them, and re-layouts: 1.95 us -> 0.01 us
    slice x1, local copies, waits for them, and re-layouts: 1.13 us -> 0.04 us  [local(): mine = (mine[:margin], mine[margin:])]
    pallas_call x1, Pallas kernels: 5.29 us -> 4.21 us  [local(): pl.pallas_call(correction_kernel, out_shape=[shape((2, planes + 1, part,...]
    ppermute x1, waiting for transfers between devices: 0.91 us -> 0.01 us  [local(): mine = lax.ppermute(rounded, ('gz', 'view'), both_ways)]
    ppermute x2, starting transfers between devices: 3.29 us -> 4.19 us  [local(): other = [lax.ppermute(piece, 'view', swap) for piece in mine]]
    pallas_call x1, Pallas kernels: 1.3 us -> 2.13 us  [local(): pl.pallas_call(edges_kernel, out_shape=[shape((views, margin, rows, cols)...]
    ppermute x1, starting transfers between devices: 0.2 us -> 0.83 us  [local(): core = lax.ppermute(send, 'view', swap)]
    ppermute x1, waiting for transfers between devices: 5.51 us -> 4.94 us  [local(): before = lax.ppermute(last, 'gz', up)]
  transfers between devices with their start and end apart: 7 -> 7, of which waited for: 4 -> 3; matrix products, arithmetic and copies ran while one was open for 4% -> 2% of each run, Pallas kernels for 15% -> 18%
where the time goes in v6:
time: 48.1 us; the launch traced here: 47.9 us
  starting transfers between devices  20.6 us (43%)
  Pallas kernels  12.8 us (27%)
  waiting for transfers between devices  11.1 us (23%)
  other arithmetic  3.33 us (7%)
    ppermute x1, starting transfers between devices, local(): after = lax.ppermute(first, 'gz', down)  5.06 us
    ppermute x1, waiting for transfers between devices, local(): before = lax.ppermute(last, 'gz', up)  4.94 us
    ppermute x1, waiting for transfers between devices, local(): lax.ppermute((keep[1] * core[1]).astype(jnp.float16), 'view', [(i, i ^ 2)...  4.34 us
    pallas_call x1, Pallas kernels, local(): pl.pallas_call(correction_kernel, out_shape=[shape((2, planes + 1, part,...  4.21 us
    ppermute x2, starting transfers between devices, local(): other = [lax.ppermute(piece, 'view', swap) for piece in mine]  4.19 us
    pallas_call x2, Pallas kernels, local(): pl.pallas_call(lambda *refs, early=early: inverse_kernel(early, *refs), o...  3.87 us
    ppermute x1, starting transfers between devices, local(): mine = lax.ppermute(rounded, ('gz', 'view'), both_ways)  3.83 us
    ppermute x1, starting transfers between devices, local(): before = lax.ppermute(last, 'gz', up)  3.83 us
  transfers between devices with their start and end apart: 7, of which 3 were waited for; matrix products, arithmetic and copies ran while one was open for 2% of the time, Pallas kernels for 18%

profile of v6, /device:TPU:24, one launch (start us, length us, event | category | flops | bytes accessed | tf_op | source)
XLA Modules:
  0.0 47.9 jit_solution(5690911119310671399)
XLA Ops:
  0.0 0.0 copy-start.1
  0.0 1.4 %convert_element_type.18.refs_3_ = bf16[20,128,128]{2,1,0:T(8,128)(2,1)S(1)} convert(f32[20,128,128]{2,1,0:T(8,128)} %param.3) | non-fusion elementwise | flops 327680 | bytes 1966080 | tf_op jit(solution)/shard_map/convert_element_type | solution.py:307
  1.4 3.8 %collective-permute-start.2 = (bf16[20,128,128]{2,1,0:T(8,128)(2,1)S(1)}, bf16[20,128,128]{2,1,0:T(8,128)(2,1)S(1)}, u32[]{:S(2)}, u32[]{:S(2)}) collective-permute-start(bf16[20,128,128]{2,1,0:T(8,128)(2,1)S(1)} %convert_element_type.18.refs_3_), channel_id=1, source_target_pairs={{0,4},{4,8},{8,12},{12,16},{16,20},{20,24},{24,28},{28,32},{32,36}... | collective-permute-start | bytes 1966088 | tf_op jit(solution)/shard_map/ppermute | solution.py:310
  5.3 2.1 %edges.1 = (bf16[2,10,128,128]{3,2,1,0:T(8,128)(2,1)}, bf16[2,10,128,128]{3,2,1,0:T(8,128)(2,1)}) custom-call(bf16[2,20,128,128]{3,2,1,0:T(8,128)(2,1)} %rec_ref.3), custom_call_target="tpu_custom_call" | custom-call | flops 10000 | bytes 10000 | tf_op jit(solution)/shard_map/edges/pallas_call | solution.py:312
  7.4 3.8 %collective-permute-start = (bf16[2,10,128,128]{3,2,1,0:T(8,128)(2,1)}, bf16[2,10,128,128]{3,2,1,0:T(8,128)(2,1)S(1)}, u32[]{:S(2)}, u32[]{:S(2)}) collective-permute-start(bf16[2,10,128,128]{3,2,1,0:T(8,128)(2,1)} %get-tuple-element.18), channel_id=1, source_target_pairs={{0,4},{4,8},{8,12},{12,16},{16,20},{20,24},{24,28},{28,32},{32,36}... | collective-permute-start | bytes 1966088 | tf_op jit(solution)/shard_map/ppermute | solution.py:324
  11.2 5.1 %collective-permute-start.1 = (bf16[2,10,128,128]{3,2,1,0:T(8,128)(2,1)}, bf16[2,10,128,128]{3,2,1,0:T(8,128)(2,1)S(1)}, u32[]{:S(2)}, u32[]{:S(2)}) collective-permute-start(bf16[2,10,128,128]{3,2,1,0:T(8,128)(2,1)} %get-tuple-element.19), channel_id=1, source_target_pairs={{4,0},{8,4},{12,8},{16,12},{20,16},{24,20},{28,24},{32,28},{36,32}... | collective-permute-start | bytes 1966088 | tf_op jit(solution)/shard_map/ppermute | solution.py:325
  16.3 0.0 copy-done.1
  16.3 2.5 %matrices.1 = (bf16[2,320,256]{2,1,0:T(8,128)(2,1)S(1)}, bf16[2,2,256,256]{3,2,1,0:T(8,128)(2,1)S(1)}, bf16[2,2,128,256]{3,2,1,0:T(8,128)(2,1)S(1)}, f32[2,2,1,128]{3,2,1,0:T(1,128)S(1)}) custom-call(s32[1]{0:T(128)} %bitcast.place_ref.refs_0_, f32[2,3,2,21]{3,2,1,0:T(2,128)S(1)} %copy-done.1), custom_call_target="tpu_custom_call" | custom-call | flops 1000000 | bytes 10000 | tf_op jit(solution)/shard_map/matrices/pallas_call | solution.py:328
  18.9 0.0 collective-permute-done.2
  18.9 4.1 %collective-permute-start.3 = (bf16[10,128,128]{2,1,0:T(8,128)(2,1)S(1)}, bf16[10,128,128]{2,1,0:T(8,128)(2,1)S(1)}, u32[]{:S(2)}, u32[]{:S(2)}) collective-permute-start(bf16[10,128,128]{2,1,0:T(8,128)(2,1)S(1)} %get-tuple-element.32.refs_1_), channel_id=1, source_target_pairs={{0,1},{1,0},{2,3},{3,2},{4,5},{5,4},{6,7},{7,6},{8,9},{9,8},{10,11... | collective-permute-start | bytes 983048 | tf_op jit(solution)/shard_map/ppermute | solution.py:344
  23.0 0.1 collective-permute-start.4
  23.1 1.9 %inverses.2.early_ref = f32[2,20,128,128]{3,2,1,0:T(8,128)S(1)} custom-call(s32[1]{0:T(128)} %bitcast.place_ref.refs_0_, bf16[10,128,128]{2,1,0:T(8,128)(2,1)S(1)} %get-tuple-element.32.refs_1_, bf16[10,128,128]{2,1,0:T(8,128)(2,1)S(1)} %get-tuple-element.31.refs_2_, bf16[20,128,128]{2,1,0:T(8,128)(2,1)S(1)} %convert_element_type.18.refs_3_, ...), custom_call_target="tpu_custom_call" | custom-call | flops 1000000 | bytes 10000 | tf_op jit(solution)/shard_map/inverses/pallas_call | solution.py:348
  25.1 0.0 copy-start
  25.1 0.0 collective-permute-done.3.refs_1_
  25.1 0.0 collective-permute-done.4.refs_2_
  25.1 1.9 %inverses.3.late_ref = f32[2,20,128,128]{3,2,1,0:T(8,128)S(1)} custom-call(s32[1]{0:T(128)} %bitcast.place_ref.refs_0_, bf16[10,128,128]{2,1,0:T(8,128)(2,1)S(1)} %collective-permute-done.3.refs_1_, bf16[10,128,128]{2,1,0:T(8,128)(2,1)S(1)} %collective-permute-done.4.refs_2_, bf16[20,128,128]{2,1,0:T(8,128)(2,1)S(1)} %convert_element_type.18.refs_3_, ...), custom_call_target="tpu_custom_call" | custom-call | flops 1000000 | bytes 10000 | tf_op jit(solution)/shard_map/inverses/pallas_call | solution.py:348
  27.1 4.9 %collective-permute-done.before_ref = bf16[2,10,128,128]{3,2,1,0:T(8,128)(2,1)S(1)} collective-permute-done((bf16[2,10,128,128]{3,2,1,0:T(8,128)(2,1)}, bf16[2,10,128,128]{3,2,1,0:T(8,128)(2,1)S(1)}, u32[]{:S(2)}, u32[]{:S(2)}) %collective-permute-start) | collective-permute-done | bytes 655392 | tf_op jit(solution)/shard_map/ppermute | solution.py:324
  32.0 0.0 collective-permute-done.1.after_ref
  32.0 0.0 copy-done
  32.0 4.2 %corrections.1 = (f32[2,21,32,128]{3,2,1,0:T(8,128)S(1)}, f32[2,21,32,128]{3,2,1,0:T(8,128)S(1)}) custom-call(s32[1]{0:T(128)} %bitcast.place_ref.refs_0_, bf16[2,10,128,128]{3,2,1,0:T(8,128)(2,1)S(1)} %collective-permute-done.before_ref, bf16[2,20,128,128]{3,2,1,0:T(8,128)(2,1)S(1)} %copy-done, ...), custom_call_target="tpu_custom_call" | custom-call | flops 4000000000 | bytes 5000000 | tf_op jit(solution)/shard_map/corrections/pallas_call | solution.py:359
  36.2 0.8 %collective-permute-start.5 = (f32[2,21,32,128]{3,2,1,0:T(8,128)S(1)}, f32[2,21,32,128]{3,2,1,0:T(8,128)S(1)}, u32[]{:S(2)}, u32[]{:S(2)}) collective-permute-start(f32[2,21,32,128]{3,2,1,0:T(8,128)S(1)} %get-tuple-element.27), channel_id=1, source_target_pairs={{0,1},{1,0},{2,3},{3,2},{4,5},{5,4},{6,7},{7,6},{8,9},{9,8},{10,11... | collective-permute-start | bytes 2064392 | tf_op jit(solution)/shard_map/ppermute | solution.py:368
  37.1 1.8 %collective-permute-done.5 = f32[2,21,32,128]{3,2,1,0:T(8,128)S(1)} collective-permute-done((f32[2,21,32,128]{3,2,1,0:T(8,128)S(1)}, f32[2,21,32,128]{3,2,1,0:T(8,128)S(1)}, u32[]{:S(2)}, u32[]{:S(2)}) %collective-permute-start.5) | collective-permute-done | bytes 688160 | tf_op jit(solution)/shard_map/ppermute | solution.py:368
  38.8 0.1 fusion.3
  38.9 2.8 %collective-permute-start.6 = (f16[21,32,128]{2,1,0:T(8,128)(2,1)S(1)}, f16[21,32,128]{2,1,0:T(8,128)(2,1)S(1)}, u32[]{:S(2)}, u32[]{:S(2)}) collective-permute-start(f16[21,32,128]{2,1,0:T(8,128)(2,1)S(1)} %fusion.3), channel_id=1, source_target_pairs={{0,2},{1,3},{2,0},{3,1},{4,6},{5,7},{6,4},{7,5},{8,10},{9,11},{10,... | collective-permute-start | bytes 516104 | tf_op jit(solution)/shard_map/ppermute | solution.py:369
  41.7 1.1 %fusion.2 = f32[20,32,128]{2,1,0:T(8,128)S(1)} fusion(f32[2,21,32,128]{3,2,1,0:T(8,128)S(1)} %collective-permute-done.5, f32[2,21,32,128]{3,2,1,0:T(8,128)S(1)} %get-tuple-element.26, f32[20,128,128]{2,1,0:T(8,128)} %param.3, s32[]{:T(128)S(6)} %select_n.3), kind=kLoop, calls=%fused_computation.4 | loop fusion | flops 163840 | bytes 1310724 | tf_op jit(solution)/shard_map/mul | solution.py:372
  42.8 4.3 %collective-permute-done.6 = f16[21,32,128]{2,1,0:T(8,128)(2,1)S(1)} collective-permute-done((f16[21,32,128]{2,1,0:T(8,128)(2,1)S(1)}, f16[21,32,128]{2,1,0:T(8,128)(2,1)S(1)}, u32[]{:S(2)}, u32[]{:S(2)}) %collective-permute-start.6) | collective-permute-done | bytes 172064 | tf_op jit(solution)/shard_map/ppermute | solution.py:369
  47.1 0.8 %multiply_multiply_fusion = f32[20,32,128]{2,1,0:T(8,128)} fusion(f32[20,32,128]{2,1,0:T(8,128)S(1)} %fusion.2, f32[32,128]{1,0:T(8,128)S(1)} %multiply_multiply_fusion.1, f16[21,32,128]{2,1,0:T(8,128)(2,1)S(1)} %collective-permute-done.6), kind=kLoop, calls=%fused_computation.5 | loop fusion | flops 245760 | bytes 835584 | tf_op jit(solution)/shard_map/mul | solution.py:375
  (3 shorter events, 0.1 us)
Async XLA Ops:
  0.0 16.3 %copy-start.1 = (f32[2,3,2,21]{3,2,1,0:T(2,128)S(1)}, f32[2,3,2,21]{3,2,1,0:T(2,128)}, u32[]{:S(2)}) copy-start(f32[2,3,2,21]{3,2,1,0:T(2,128)} %taps_ref.1) | copy-start | bytes 3028
  1.4 17.4 %collective-permute-start.2 = (bf16[20,128,128]{2,1,0:T(8,128)(2,1)S(1)}, bf16[20,128,128]{2,1,0:T(8,128)(2,1)S(1)}, u32[]{:S(2)}, u32[]{:S(2)}) collective-permute-start(bf16[20,128,128]{2,1,0:T(8,128)(2,1)S(1)} %convert_element_type.18.refs_3_), channel_id=1, source_target_pairs={{0,4},{4,8},{8,12},{12,16},{16,20},{20,24},{24,28},{28,32},{32,36}... | collective-permute-start | bytes 1966088 | tf_op jit(solution)/shard_map/ppermute | solution.py:310
  7.4 24.6 %collective-permute-start = (bf16[2,10,128,128]{3,2,1,0:T(8,128)(2,1)}, bf16[2,10,128,128]{3,2,1,0:T(8,128)(2,1)S(1)}, u32[]{:S(2)}, u32[]{:S(2)}) collective-permute-start(bf16[2,10,128,128]{3,2,1,0:T(8,128)(2,1)} %get-tuple-element.18), channel_id=1, source_target_pairs={{0,4},{4,8},{8,12},{12,16},{16,20},{20,24},{24,28},{28,32},{32,36}... | collective-permute-start | bytes 1966088 | tf_op jit(solution)/shard_map/ppermute | solution.py:324
  11.2 20.7 %collective-permute-start.1 = (bf16[2,10,128,128]{3,2,1,0:T(8,128)(2,1)}, bf16[2,10,128,128]{3,2,1,0:T(8,128)(2,1)S(1)}, u32[]{:S(2)}, u32[]{:S(2)}) collective-permute-start(bf16[2,10,128,128]{3,2,1,0:T(8,128)(2,1)} %get-tuple-element.19), channel_id=1, source_target_pairs={{4,0},{8,4},{12,8},{16,12},{20,16},{24,20},{28,24},{32,28},{36,32}... | collective-permute-start | bytes 1966088 | tf_op jit(solution)/shard_map/ppermute | solution.py:325
  18.9 6.1 %collective-permute-start.3 = (bf16[10,128,128]{2,1,0:T(8,128)(2,1)S(1)}, bf16[10,128,128]{2,1,0:T(8,128)(2,1)S(1)}, u32[]{:S(2)}, u32[]{:S(2)}) collective-permute-start(bf16[10,128,128]{2,1,0:T(8,128)(2,1)S(1)} %get-tuple-element.32.refs_1_), channel_id=1, source_target_pairs={{0,1},{1,0},{2,3},{3,2},{4,5},{5,4},{6,7},{7,6},{8,9},{9,8},{10,11... | collective-permute-start | bytes 983048 | tf_op jit(solution)/shard_map/ppermute | solution.py:344
  23.0 2.1 %collective-permute-start.4 = (bf16[10,128,128]{2,1,0:T(8,128)(2,1)S(1)}, bf16[10,128,128]{2,1,0:T(8,128)(2,1)S(1)}, u32[]{:S(2)}, u32[]{:S(2)}) collective-permute-start(bf16[10,128,128]{2,1,0:T(8,128)(2,1)S(1)} %get-tuple-element.31.refs_2_), channel_id=1, source_target_pairs={{0,1},{1,0},{2,3},{3,2},{4,5},{5,4},{6,7},{7,6},{8,9},{9,8},{10,11... | collective-permute-start | bytes 983048 | tf_op jit(solution)/shard_map/ppermute | solution.py:344
  25.1 6.9 %copy-start = (bf16[2,20,128,128]{3,2,1,0:T(8,128)(2,1)S(1)}, bf16[2,20,128,128]{3,2,1,0:T(8,128)(2,1)}, u32[]{:S(2)}) copy-start(bf16[2,20,128,128]{3,2,1,0:T(8,128)(2,1)} %rec_ref.3) | copy-start | bytes 3932164
  36.2 2.6 %collective-permute-start.5 = (f32[2,21,32,128]{3,2,1,0:T(8,128)S(1)}, f32[2,21,32,128]{3,2,1,0:T(8,128)S(1)}, u32[]{:S(2)}, u32[]{:S(2)}) collective-permute-start(f32[2,21,32,128]{3,2,1,0:T(8,128)S(1)} %get-tuple-element.27), channel_id=1, source_target_pairs={{0,1},{1,0},{2,3},{3,2},{4,5},{5,4},{6,7},{7,6},{8,9},{9,8},{10,11... | collective-permute-start | bytes 2064392 | tf_op jit(solution)/shard_map/ppermute | solution.py:368
  38.9 8.2 %collective-permute-start.6 = (f16[21,32,128]{2,1,0:T(8,128)(2,1)S(1)}, f16[21,32,128]{2,1,0:T(8,128)(2,1)S(1)}, u32[]{:S(2)}, u32[]{:S(2)}) collective-permute-start(f16[21,32,128]{2,1,0:T(8,128)(2,1)S(1)} %fusion.3), channel_id=1, source_target_pairs={{0,2},{1,3},{2,0},{3,1},{4,6},{5,7},{6,4},{7,5},{8,10},{9,11},{10,... | collective-permute-start | bytes 516104 | tf_op jit(solution)/shard_map/ppermute | solution.py:369

commit v7 on v6

--- a/solution.py
+++ b/solution.py
@@ -226,10 +226,10 @@
 
 
 def correction_kernel(
+    upper,
     place_ref,
-    before_ref,
+    halo_ref,
     rec_ref,
-    after_ref,
     early_ref,
     late_ref,
     z_ref,
@@ -242,18 +242,22 @@
     g_ref,
     product_ref,
 ):
-    views, planes = rec_ref.shape[:2]
-    part = keep_ref.shape[2]
+    views = rec_ref.shape[0]
+    planes, part = product_ref.shape[0], keep_ref.shape[2]
+    margin = halo_ref.shape[1]
     tall = z_ref.shape[1] // views
     early_first = place_ref[0] % 2 == 0
     most = [jnp.zeros((8, product_ref.shape[2]), F32)]
     for v in range(views):
 
         def load(at, v=v):
-            rec = [ref[v, :, at, :].astype(F32) for ref in (before_ref, rec_ref, after_ref)]
+            halo, own = halo_ref[v, :, at, :].astype(F32), rec_ref[v, :, at, :].astype(F32)
             early, late = early_ref[v, :, at, :], late_ref[v, :, at, :]
             inverse = [jnp.where(early_first, early, late), jnp.where(early_first, late, early)]
-            return jnp.concatenate(rec, axis=0) * jnp.concatenate(inverse, axis=0)
+            inverse = jnp.concatenate(inverse, axis=0)
+            if upper:
+                return jnp.concatenate([own, halo], axis=0) * inverse[margin:]
+            return jnp.concatenate([halo, own], axis=0) * inverse[: inverse.shape[0] - margin]
 
         def emit(_, z, value, v=v):
             if v > 0:
@@ -267,7 +271,7 @@
         filter_to(
             load,
             1,
-            2,
+            1,
             z_view,
             x_ref.at[1, v : v + 1],
             y_ref.at[1, v : v + 1],
@@ -356,23 +360,33 @@
             )(place_array, *side, rounded, z_mat, x_mat, y_mat, scales)
         )
     part = rows // 4
-    keep, send = pl.pallas_call(
-        correction_kernel,
-        out_shape=[shape((2, planes + 1, part, cols), F32)] * 2,
-        in_specs=[SMEM] + [VMEM] * 9,
-        out_specs=[VMEM] * 2,
-        scratch_shapes=scratch(1, 2, 2, z_out, rows, cols) + [pltpu.VMEM((planes, rows, cols), F32)],
-        name="corrections",
-        **params(4 * 10**9, 5 * 10**6),
-    )(place_array, before, recordings, after, *inverses, z_mat, x_mat, y_mat, scales)
-    core = lax.ppermute(send, "view", swap)
-    across = lax.ppermute((keep[1] * core[1]).astype(jnp.float16), "view", [(i, i ^ 2) for i in range(4)])
+    halves = []
+    for upper, halo in ((False, before), (True, after)):
+        halves.append(
+            pl.pallas_call(
+                lambda *refs, upper=upper: correction_kernel(upper, *refs),
+                out_shape=[shape((2, z_out + 1, part, cols), F32)] * 2,
+                in_specs=[SMEM] + [VMEM] * 8,
+                out_specs=[VMEM] * 2,
+                scratch_shapes=scratch(1, 1, 2, z_out, rows, cols) + [pltpu.VMEM((z_out, rows, cols), F32)],
+                name="corrections",
+                **params(2 * 10**9, 2 * 10**6),
+            )(place_array, halo, recordings, *inverses, z_mat, x_mat, y_mat, scales)
+        )
     own_rows = lax.dynamic_slice_in_dim(estimate, place * part, part, 1)
-    root = keep[0, planes] * core[0, planes]
-    partial = own_rows * (keep[0, :planes] * core[0, :planes])
-    partial, root, across = lax.optimization_barrier((partial, root, across))
-    root = root * across[planes].astype(F32)
-    return partial * (across[:planes].astype(F32) * (root * root * root * root))
+    cores = [lax.ppermute(send, "view", swap) for _, send in halves]
+    outs = []
+    for half, ((keep, _), core) in enumerate(zip(halves, cores)):
+        across = lax.ppermute((keep[1] * core[1]).astype(jnp.float16), "view", [(i, i ^ 2) for i in range(4)])
+        root = keep[0, z_out] * core[0, z_out]
+        partial = own_rows[half * z_out : (half + 1) * z_out] * (keep[0, :z_out] * core[0, :z_out])
+        outs.append((partial, root, across))
+    outs = lax.optimization_barrier(outs)
+    results = []
+    for partial, root, across in outs:
+        root = root * across[z_out].astype(F32)
+        results.append(partial * (across[:z_out].astype(F32) * (root * root * root * root)))
+    return jnp.concatenate(results, axis=0)
 
 
 def solution(mesh):

time: 48.1 us -> 49.5 us (1.029)
  Pallas kernels: 12.8 us -> 13.9 us
    ppermute x1, waiting for transfers between devices: 0.01 us -> 5.82 us  [local(): after = lax.ppermute(first, 'gz', down)]
    ppermute x1, waiting for transfers between devices: 4.94 us -> 1.91 us  [local(): before = lax.ppermute(last, 'gz', up)]
    ppermute x2, starting transfers between devices: 4.19 us -> 1.18 us  [local(): other = [lax.ppermute(piece, 'view', swap) for piece in mine]]
    ppermute x1, starting transfers between devices: 3.83 us -> 1.92 us  [local(): before = lax.ppermute(last, 'gz', up)]
    ppermute x1, starting transfers between devices: 5.06 us -> 6.97 us  [local(): after = lax.ppermute(first, 'gz', down)]
    ppermute x1 -> x2, waiting for transfers between devices: 1.77 us -> 0.01 us  [local(): cores = [lax.ppermute(send, 'view', swap) for _, send in halves]]
    ppermute x1 -> x2, starting transfers between devices: 2.84 us -> 4.43 us  [local(): lax.ppermute((keep[1] * core[1]).astype(jnp.float16), 'view', [(i, i ^ 2)...]
    ppermute x1 -> x2, starting transfers between devices: 0.83 us -> 2.02 us  [local(): cores = [lax.ppermute(send, 'view', swap) for _, send in halves]]
  transfers between devices with their start and end apart: 7 -> 9, of which waited for: 3 -> 4; matrix products, arithmetic and copies ran while one was open for 2% -> 2% of each run, Pallas kernels for 18% -> 28%
where the time goes in v7:
time: 49.5 us; the launch traced here: 49.3 us
  starting transfers between devices  20.3 us (41%)
  Pallas kernels  13.9 us (28%)
  waiting for transfers between devices  11.4 us (23%)
  other arithmetic  3.39 us (7%)
    ppermute x1, starting transfers between devices, local(): after = lax.ppermute(first, 'gz', down)  6.97 us
    ppermute x1, waiting for transfers between devices, local(): after = lax.ppermute(first, 'gz', down)  5.82 us
    pallas_call x2, Pallas kernels, local(): pl.pallas_call(lambda *refs, upper=upper: correction_kernel(upper, *refs)...  5.39 us
    ppermute x2, starting transfers between devices, local(): lax.ppermute((keep[1] * core[1]).astype(jnp.float16), 'view', [(i, i ^ 2)...  4.43 us
    pallas_call x2, Pallas kernels, local(): pl.pallas_call(lambda *refs, early=early: inverse_kernel(early, *refs), o...  3.87 us
    ppermute x1, starting transfers between devices, local(): mine = lax.ppermute(rounded, ('gz', 'view'), both_ways)  3.83 us
    ppermute x2, waiting for transfers between devices, local(): lax.ppermute((keep[1] * core[1]).astype(jnp.float16), 'view', [(i, i ^ 2)...  3.61 us
    pallas_call x1, Pallas kernels, local(): pl.pallas_call(matrices_kernel, out_shape=[shape((2, views * 2 * z_out *...  2.54 us
  transfers between devices with their start and end apart: 9, of which 4 were waited for; matrix products, arithmetic and copies ran while one was open for 2% of the time, Pallas kernels for 28%

profile of v7, /device:TPU:24, one launch (start us, length us, event | category | flops | bytes accessed | tf_op | source)
XLA Modules:
  0.0 49.3 jit_solution(17387017659077110565)
XLA Ops:
  0.0 0.0 copy-start.1
  0.0 1.4 %convert_element_type.33.refs_3_ = bf16[20,128,128]{2,1,0:T(8,128)(2,1)S(1)} convert(f32[20,128,128]{2,1,0:T(8,128)} %param.3) | non-fusion elementwise | flops 327680 | bytes 1966080 | tf_op jit(solution)/shard_map/convert_element_type | solution.py:311
  1.4 3.8 %collective-permute-start.1 = (bf16[20,128,128]{2,1,0:T(8,128)(2,1)S(1)}, bf16[20,128,128]{2,1,0:T(8,128)(2,1)S(1)}, u32[]{:S(2)}, u32[]{:S(2)}) collective-permute-start(bf16[20,128,128]{2,1,0:T(8,128)(2,1)S(1)} %convert_element_type.33.refs_3_), channel_id=1, source_target_pairs={{0,4},{4,8},{8,12},{12,16},{16,20},{20,24},{24,28},{28,32},{32,36}... | collective-permute-start | bytes 1966088 | tf_op jit(solution)/shard_map/ppermute | solution.py:314
  5.3 2.1 %edges.1 = (bf16[2,10,128,128]{3,2,1,0:T(8,128)(2,1)}, bf16[2,10,128,128]{3,2,1,0:T(8,128)(2,1)}) custom-call(bf16[2,20,128,128]{3,2,1,0:T(8,128)(2,1)} %refs_2_.3), custom_call_target="tpu_custom_call" | custom-call | flops 10000 | bytes 10000 | tf_op jit(solution)/shard_map/edges/pallas_call | solution.py:316
  7.4 7.0 %collective-permute-start.6 = (bf16[2,10,128,128]{3,2,1,0:T(8,128)(2,1)}, bf16[2,10,128,128]{3,2,1,0:T(8,128)(2,1)S(1)}, u32[]{:S(2)}, u32[]{:S(2)}) collective-permute-start(bf16[2,10,128,128]{3,2,1,0:T(8,128)(2,1)} %get-tuple-element.32), channel_id=1, source_target_pairs={{4,0},{8,4},{12,8},{16,12},{20,16},{24,20},{28,24},{32,28},{36,32}... | collective-permute-start | bytes 1966088 | tf_op jit(solution)/shard_map/ppermute | solution.py:329
  14.4 1.9 %collective-permute-start = (bf16[2,10,128,128]{3,2,1,0:T(8,128)(2,1)}, bf16[2,10,128,128]{3,2,1,0:T(8,128)(2,1)S(1)}, u32[]{:S(2)}, u32[]{:S(2)}) collective-permute-start(bf16[2,10,128,128]{3,2,1,0:T(8,128)(2,1)} %get-tuple-element.23), channel_id=1, source_target_pairs={{0,4},{4,8},{8,12},{12,16},{16,20},{20,24},{24,28},{28,32},{32,36}... | collective-permute-start | bytes 1966088 | tf_op jit(solution)/shard_map/ppermute | solution.py:328
  16.3 0.0 copy-done.1
  16.3 2.5 %matrices.1 = (bf16[2,320,256]{2,1,0:T(8,128)(2,1)S(1)}, bf16[2,2,256,256]{3,2,1,0:T(8,128)(2,1)S(1)}, bf16[2,2,128,256]{3,2,1,0:T(8,128)(2,1)S(1)}, f32[2,2,1,128]{3,2,1,0:T(1,128)S(1)}) custom-call(s32[1]{0:T(128)} %bitcast.place_ref.refs_0_, f32[2,3,2,21]{3,2,1,0:T(2,128)S(1)} %copy-done.1), custom_call_target="tpu_custom_call" | custom-call | flops 1000000 | bytes 10000 | tf_op jit(solution)/shard_map/matrices/pallas_call | solution.py:332
  18.9 0.0 collective-permute-done.1
  18.9 1.1 %collective-permute-start.2 = (bf16[10,128,128]{2,1,0:T(8,128)(2,1)S(1)}, bf16[10,128,128]{2,1,0:T(8,128)(2,1)S(1)}, u32[]{:S(2)}, u32[]{:S(2)}) collective-permute-start(bf16[10,128,128]{2,1,0:T(8,128)(2,1)S(1)} %get-tuple-element.44.refs_1_), channel_id=1, source_target_pairs={{0,1},{1,0},{2,3},{3,2},{4,5},{5,4},{6,7},{7,6},{8,9},{9,8},{10,11... | collective-permute-start | bytes 983048 | tf_op jit(solution)/shard_map/ppermute | solution.py:348
  20.0 0.1 collective-permute-start.3
  20.1 1.9 %inverses.2.refs_3_ = f32[2,20,128,128]{3,2,1,0:T(8,128)S(1)} custom-call(s32[1]{0:T(128)} %bitcast.place_ref.refs_0_, bf16[10,128,128]{2,1,0:T(8,128)(2,1)S(1)} %get-tuple-element.44.refs_1_, bf16[10,128,128]{2,1,0:T(8,128)(2,1)S(1)} %get-tuple-element.43.refs_2_, bf16[20,128,128]{2,1,0:T(8,128)(2,1)S(1)} %convert_element_type.33.refs_3_, ...), custom_call_target="tpu_custom_call" | custom-call | flops 1000000 | bytes 10000 | tf_op jit(solution)/shard_map/inverses/pallas_call | solution.py:352
  22.1 0.0 copy-start
  22.1 0.0 collective-permute-done.2.refs_1_
  22.1 0.0 collective-permute-done.3.refs_2_
  22.1 1.9 %inverses.3.refs_4_ = f32[2,20,128,128]{3,2,1,0:T(8,128)S(1)} custom-call(s32[1]{0:T(128)} %bitcast.place_ref.refs_0_, bf16[10,128,128]{2,1,0:T(8,128)(2,1)S(1)} %collective-permute-done.2.refs_1_, bf16[10,128,128]{2,1,0:T(8,128)(2,1)S(1)} %collective-permute-done.3.refs_2_, bf16[20,128,128]{2,1,0:T(8,128)(2,1)S(1)} %convert_element_type.33.refs_3_, ...), custom_call_target="tpu_custom_call" | custom-call | flops 1000000 | bytes 10000 | tf_op jit(solution)/shard_map/inverses/pallas_call | solution.py:352
  24.0 5.8 %collective-permute-done.6.refs_1_ = bf16[2,10,128,128]{3,2,1,0:T(8,128)(2,1)S(1)} collective-permute-done((bf16[2,10,128,128]{3,2,1,0:T(8,128)(2,1)}, bf16[2,10,128,128]{3,2,1,0:T(8,128)(2,1)S(1)}, u32[]{:S(2)}, u32[]{:S(2)}) %collective-permute-start.6) | collective-permute-done | bytes 655392 | tf_op jit(solution)/shard_map/ppermute | solution.py:329
  29.9 0.0 copy-done
  29.9 2.7 %corrections.3 = (f32[2,11,32,128]{3,2,1,0:T(8,128)S(1)}, f32[2,11,32,128]{3,2,1,0:T(8,128)S(1)}) custom-call(s32[1]{0:T(128)} %bitcast.place_ref.refs_0_, bf16[2,10,128,128]{3,2,1,0:T(8,128)(2,1)S(1)} %collective-permute-done.6.refs_1_, bf16[2,20,128,128]{3,2,1,0:T(8,128)(2,1)S(1)} %copy-done, f32[2,20,128,128]{3,2,1,0:T(8,128)S(1)} %inverses.2.refs_3_, ...), custom_call_target="tpu_custom_call" | custom-call | flops 2000000000 | bytes 2000000 | tf_op jit(solution)/shard_map/corrections/pallas_call | solution.py:366
  32.6 1.9 %collective-permute-start.7 = (f32[2,11,32,128]{3,2,1,0:T(8,128)S(1)}, f32[2,11,32,128]{3,2,1,0:T(8,128)S(1)}, u32[]{:S(2)}, u32[]{:S(2)}) collective-permute-start(f32[2,11,32,128]{3,2,1,0:T(8,128)S(1)} %get-tuple-element.34), channel_id=1, source_target_pairs={{0,1},{1,0},{2,3},{3,2},{4,5},{5,4},{6,7},{7,6},{8,9},{9,8},{10,11... | collective-permute-start | bytes 1081352 | tf_op jit(solution)/shard_map/ppermute | solution.py:377
  34.5 1.9 %collective-permute-done.refs_1_ = bf16[2,10,128,128]{3,2,1,0:T(8,128)(2,1)S(1)} collective-permute-done((bf16[2,10,128,128]{3,2,1,0:T(8,128)(2,1)}, bf16[2,10,128,128]{3,2,1,0:T(8,128)(2,1)S(1)}, u32[]{:S(2)}, u32[]{:S(2)}) %collective-permute-start) | collective-permute-done | bytes 655392 | tf_op jit(solution)/shard_map/ppermute | solution.py:328
  36.4 2.7 %corrections.2 = (f32[2,11,32,128]{3,2,1,0:T(8,128)S(1)}, f32[2,11,32,128]{3,2,1,0:T(8,128)S(1)}) custom-call(s32[1]{0:T(128)} %bitcast.place_ref.refs_0_, bf16[2,10,128,128]{3,2,1,0:T(8,128)(2,1)S(1)} %collective-permute-done.refs_1_, bf16[2,20,128,128]{3,2,1,0:T(8,128)(2,1)S(1)} %copy-done, f32[2,20,128,128]{3,2,1,0:T(8,128)S(1)} %inverses.2.refs_3_, ...), custom_call_target="tpu_custom_call" | custom-call | flops 2000000000 | bytes 2000000 | tf_op jit(solution)/shard_map/corrections/pallas_call | solution.py:366
  39.1 0.1 collective-permute-start.4
  39.2 0.0 collective-permute-done.7
  39.3 2.8 %collective-permute-start.8 = (f16[11,32,128]{2,1,0:T(8,128)(2,1)S(1)}, f16[11,32,128]{2,1,0:T(8,128)(2,1)S(1)}, u32[]{:S(2)}, u32[]{:S(2)}) collective-permute-start(f16[11,32,128]{2,1,0:T(8,128)(2,1)S(1)} %fusion.7), channel_id=1, source_target_pairs={{0,2},{1,3},{2,0},{3,1},{4,6},{5,7},{6,4},{7,5},{8,10},{9,11},{10,... | collective-permute-start | bytes 270344 | tf_op jit(solution)/shard_map/ppermute | solution.py:380
  42.1 0.0 collective-permute-done.4
  42.1 1.6 %collective-permute-start.5 = (f16[11,32,128]{2,1,0:T(8,128)(2,1)S(1)}, f16[11,32,128]{2,1,0:T(8,128)(2,1)S(1)}, u32[]{:S(2)}, u32[]{:S(2)}) collective-permute-start(f16[11,32,128]{2,1,0:T(8,128)(2,1)S(1)} %fusion.6), channel_id=1, source_target_pairs={{0,2},{1,3},{2,0},{3,1},{4,6},{5,7},{6,4},{7,5},{8,10},{9,11},{10,... | collective-permute-start | bytes 270344 | tf_op jit(solution)/shard_map/ppermute | solution.py:380
  43.7 1.1 %fusion.3 = (f32[10,32,128]{2,1,0:T(8,128)S(1)}, f32[10,32,128]{2,1,0:T(8,128)S(1)}) fusion(f32[2,11,32,128]{3,2,1,0:T(8,128)S(1)} %collective-permute-done.7, f32[20,128,128]{2,1,0:T(8,128)} %param.3, s32[]{:T(128)S(6)} %add.4, s32[]{:T(128)S(6)} %select_n.3, f32[2,11,32,128]{3,2,1,0:T(8,128)S(1)} %get-tuple-element.33, ...), kind=kLoop, calls=%fused_computation.7 | loop fusion | flops 163840 | bytes 1310728 | tf_op jit(solution)/shard_map/mul | solution.py:382
  44.8 1.0 %collective-permute-done.8 = f16[11,32,128]{2,1,0:T(8,128)(2,1)S(1)} collective-permute-done((f16[11,32,128]{2,1,0:T(8,128)(2,1)S(1)}, f16[11,32,128]{2,1,0:T(8,128)(2,1)S(1)}, u32[]{:S(2)}, u32[]{:S(2)}) %collective-permute-start.8) | collective-permute-done | bytes 90144 | tf_op jit(solution)/shard_map/ppermute | solution.py:380
  45.9 2.6 %collective-permute-done.5 = f16[11,32,128]{2,1,0:T(8,128)(2,1)S(1)} collective-permute-done((f16[11,32,128]{2,1,0:T(8,128)(2,1)S(1)}, f16[11,32,128]{2,1,0:T(8,128)(2,1)S(1)}, u32[]{:S(2)}, u32[]{:S(2)}) %collective-permute-start.5) | collective-permute-done | bytes 90144 | tf_op jit(solution)/shard_map/ppermute | solution.py:380
  48.5 0.1 multiply_multiply_fusion
  48.5 0.7 %pad_maximum_fusion = f32[20,32,128]{2,1,0:T(8,128)} fusion(f32[10,32,128]{2,1,0:T(8,128)S(1)} %get-tuple-element.45, f32[10,32,128]{2,1,0:T(8,128)S(1)} %get-tuple-element.46), kind=kLoop, calls=%fused_computation | loop fusion | flops 81920 | bytes 655360 | tf_op jit(solution)/shard_map/concatenate | solution.py:389
  (7 shorter events, 0.1 us)
Async XLA Ops:
  0.0 16.3 %copy-start.1 = (f32[2,3,2,21]{3,2,1,0:T(2,128)S(1)}, f32[2,3,2,21]{3,2,1,0:T(2,128)}, u32[]{:S(2)}) copy-start(f32[2,3,2,21]{3,2,1,0:T(2,128)} %taps_ref.1) | copy-start | bytes 3028
  1.4 17.4 %collective-permute-start.1 = (bf16[20,128,128]{2,1,0:T(8,128)(2,1)S(1)}, bf16[20,128,128]{2,1,0:T(8,128)(2,1)S(1)}, u32[]{:S(2)}, u32[]{:S(2)}) collective-permute-start(bf16[20,128,128]{2,1,0:T(8,128)(2,1)S(1)} %convert_element_type.33.refs_3_), channel_id=1, source_target_pairs={{0,4},{4,8},{8,12},{12,16},{16,20},{20,24},{24,28},{28,32},{32,36}... | collective-permute-start | bytes 1966088 | tf_op jit(solution)/shard_map/ppermute | solution.py:314
  7.4 22.5 %collective-permute-start.6 = (bf16[2,10,128,128]{3,2,1,0:T(8,128)(2,1)}, bf16[2,10,128,128]{3,2,1,0:T(8,128)(2,1)S(1)}, u32[]{:S(2)}, u32[]{:S(2)}) collective-permute-start(bf16[2,10,128,128]{3,2,1,0:T(8,128)(2,1)} %get-tuple-element.32), channel_id=1, source_target_pairs={{4,0},{8,4},{12,8},{16,12},{20,16},{24,20},{28,24},{32,28},{36,32}... | collective-permute-start | bytes 1966088 | tf_op jit(solution)/shard_map/ppermute | solution.py:329
  14.4 22.0 %collective-permute-start = (bf16[2,10,128,128]{3,2,1,0:T(8,128)(2,1)}, bf16[2,10,128,128]{3,2,1,0:T(8,128)(2,1)S(1)}, u32[]{:S(2)}, u32[]{:S(2)}) collective-permute-start(bf16[2,10,128,128]{3,2,1,0:T(8,128)(2,1)} %get-tuple-element.23), channel_id=1, source_target_pairs={{0,4},{4,8},{8,12},{12,16},{16,20},{20,24},{24,28},{28,32},{32,36}... | collective-permute-start | bytes 1966088 | tf_op jit(solution)/shard_map/ppermute | solution.py:328
  18.9 3.1 %collective-permute-start.2 = (bf16[10,128,128]{2,1,0:T(8,128)(2,1)S(1)}, bf16[10,128,128]{2,1,0:T(8,128)(2,1)S(1)}, u32[]{:S(2)}, u32[]{:S(2)}) collective-permute-start(bf16[10,128,128]{2,1,0:T(8,128)(2,1)S(1)} %get-tuple-element.44.refs_1_), channel_id=1, source_target_pairs={{0,1},{1,0},{2,3},{3,2},{4,5},{5,4},{6,7},{7,6},{8,9},{9,8},{10,11... | collective-permute-start | bytes 983048 | tf_op jit(solution)/shard_map/ppermute | solution.py:348
  20.0 2.1 %collective-permute-start.3 = (bf16[10,128,128]{2,1,0:T(8,128)(2,1)S(1)}, bf16[10,128,128]{2,1,0:T(8,128)(2,1)S(1)}, u32[]{:S(2)}, u32[]{:S(2)}) collective-permute-start(bf16[10,128,128]{2,1,0:T(8,128)(2,1)S(1)} %get-tuple-element.43.refs_2_), channel_id=1, source_target_pairs={{0,1},{1,0},{2,3},{3,2},{4,5},{5,4},{6,7},{7,6},{8,9},{9,8},{10,11... | collective-permute-start | bytes 983048 | tf_op jit(solution)/shard_map/ppermute | solution.py:348
  22.1 7.8 %copy-start = (bf16[2,20,128,128]{3,2,1,0:T(8,128)(2,1)S(1)}, bf16[2,20,128,128]{3,2,1,0:T(8,128)(2,1)}, u32[]{:S(2)}) copy-start(bf16[2,20,128,128]{3,2,1,0:T(8,128)(2,1)} %refs_2_.3) | copy-start | bytes 3932164
  32.6 6.7 %collective-permute-start.7 = (f32[2,11,32,128]{3,2,1,0:T(8,128)S(1)}, f32[2,11,32,128]{3,2,1,0:T(8,128)S(1)}, u32[]{:S(2)}, u32[]{:S(2)}) collective-permute-start(f32[2,11,32,128]{3,2,1,0:T(8,128)S(1)} %get-tuple-element.34), channel_id=1, source_target_pairs={{0,1},{1,0},{2,3},{3,2},{4,5},{5,4},{6,7},{7,6},{8,9},{9,8},{10,11... | collective-permute-start | bytes 1081352 | tf_op jit(solution)/shard_map/ppermute | solution.py:377
  39.1 3.0 %collective-permute-start.4 = (f32[2,11,32,128]{3,2,1,0:T(8,128)S(1)}, f32[2,11,32,128]{3,2,1,0:T(8,128)S(1)}, u32[]{:S(2)}, u32[]{:S(2)}) collective-permute-start(f32[2,11,32,128]{3,2,1,0:T(8,128)S(1)} %get-tuple-element.31), channel_id=1, source_target_pairs={{0,1},{1,0},{2,3},{3,2},{4,5},{5,4},{6,7},{7,6},{8,9},{9,8},{10,11... | collective-permute-start | bytes 1081352 | tf_op jit(solution)/shard_map/ppermute | solution.py:377
  39.3 6.6 %collective-permute-start.8 = (f16[11,32,128]{2,1,0:T(8,128)(2,1)S(1)}, f16[11,32,128]{2,1,0:T(8,128)(2,1)S(1)}, u32[]{:S(2)}, u32[]{:S(2)}) collective-permute-start(f16[11,32,128]{2,1,0:T(8,128)(2,1)S(1)} %fusion.7), channel_id=1, source_target_pairs={{0,2},{1,3},{2,0},{3,1},{4,6},{5,7},{6,4},{7,5},{8,10},{9,11},{10,... | collective-permute-start | bytes 270344 | tf_op jit(solution)/shard_map/ppermute | solution.py:380
  42.1 6.3 %collective-permute-start.5 = (f16[11,32,128]{2,1,0:T(8,128)(2,1)S(1)}, f16[11,32,128]{2,1,0:T(8,128)(2,1)S(1)}, u32[]{:S(2)}, u32[]{:S(2)}) collective-permute-start(f16[11,32,128]{2,1,0:T(8,128)(2,1)S(1)} %fusion.6), channel_id=1, source_target_pairs={{0,2},{1,3},{2,0},{3,1},{4,6},{5,7},{6,4},{7,5},{8,10},{9,11},{10,... | collective-permute-start | bytes 270344 | tf_op jit(solution)/shard_map/ppermute | solution.py:380

commit v8 on v7

--- a/solution.py
+++ b/solution.py
@@ -361,7 +361,7 @@
         )
     part = rows // 4
     halves = []
-    for upper, halo in ((False, before), (True, after)):
+    for upper, halo in ((True, after), (False, before)):
         halves.append(
             pl.pallas_call(
                 lambda *refs, upper=upper: correction_kernel(upper, *refs),
@@ -379,14 +379,14 @@
     for half, ((keep, _), core) in enumerate(zip(halves, cores)):
         across = lax.ppermute((keep[1] * core[1]).astype(jnp.float16), "view", [(i, i ^ 2) for i in range(4)])
         root = keep[0, z_out] * core[0, z_out]
-        partial = own_rows[half * z_out : (half + 1) * z_out] * (keep[0, :z_out] * core[0, :z_out])
+        partial = own_rows[(1 - half) * z_out : (2 - half) * z_out] * (keep[0, :z_out] * core[0, :z_out])
         outs.append((partial, root, across))
     outs = lax.optimization_barrier(outs)
     results = []
     for partial, root, across in outs:
         root = root * across[z_out].astype(F32)
         results.append(partial * (across[:z_out].astype(F32) * (root * root * root * root)))
-    return jnp.concatenate(results, axis=0)
+    return jnp.concatenate(results[::-1], axis=0)
 
 
 def solution(mesh):

time: 49.5 us -> 48.8 us (0.986)
  waiting for transfers between devices: 11.4 us -> 8.59 us
  starting transfers between devices: 20.3 us -> 22.4 us
    ppermute x1, waiting for transfers between devices: 5.82 us -> 0.01 us  [local(): after = lax.ppermute(first, 'gz', down)]
    ppermute x1, waiting for transfers between devices: 1.91 us -> 4.96 us  [local(): before = lax.ppermute(last, 'gz', up)]
    ppermute x2, starting transfers between devices: 1.18 us -> 4.19 us  [local(): other = [lax.ppermute(piece, 'view', swap) for piece in mine]]
    ppermute x1, starting transfers between devices: 1.92 us -> 3.83 us  [local(): before = lax.ppermute(last, 'gz', up)]
    ppermute x1, starting transfers between devices: 6.97 us -> 5.06 us  [local(): after = lax.ppermute(first, 'gz', down)]
    ppermute x2, starting transfers between devices: 2.02 us -> 1.11 us  [local(): cores = [lax.ppermute(send, 'view', swap) for _, send in halves]]
  transfers between devices with their start and end apart: 9 -> 9, of which waited for: 4 -> 3; matrix products, arithmetic and copies ran while one was open for 2% -> 2% of each run, Pallas kernels for 28% -> 29%
where the time goes in v8:
time: 48.8 us; the launch traced here: 48.6 us
  starting transfers between devices  22.4 us (46%)
  Pallas kernels  13.9 us (28%)
  waiting for transfers between devices  8.59 us (18%)
  other arithmetic  3.39 us (7%)
    pallas_call x2, Pallas kernels, local(): pl.pallas_call(lambda *refs, upper=upper: correction_kernel(upper, *refs)...  5.39 us
    ppermute x1, starting transfers between devices, local(): after = lax.ppermute(first, 'gz', down)  5.06 us
    ppermute x1, waiting for transfers between devices, local(): before = lax.ppermute(last, 'gz', up)  4.96 us
    ppermute x2, starting transfers between devices, local(): lax.ppermute((keep[1] * core[1]).astype(jnp.float16), 'view', [(i, i ^ 2)...  4.43 us
    ppermute x2, starting transfers between devices, local(): other = [lax.ppermute(piece, 'view', swap) for piece in mine]  4.19 us
    pallas_call x2, Pallas kernels, local(): pl.pallas_call(lambda *refs, early=early: inverse_kernel(early, *refs), o...  3.86 us
    ppermute x1, starting transfers between devices, local(): mine = lax.ppermute(rounded, ('gz', 'view'), both_ways)  3.83 us
    ppermute x1, starting transfers between devices, local(): before = lax.ppermute(last, 'gz', up)  3.83 us
  transfers between devices with their start and end apart: 9, of which 3 were waited for; matrix products, arithmetic and copies ran while one was open for 2% of the time, Pallas kernels for 29%

profile of v8, /device:TPU:24, one launch (start us, length us, event | category | flops | bytes accessed | tf_op | source)
XLA Modules:
  0.0 48.6 jit_solution(12856717615467636398)
XLA Ops:
  0.0 0.0 copy-start.1
  0.0 1.4 %convert_element_type.33.refs_3_ = bf16[20,128,128]{2,1,0:T(8,128)(2,1)S(1)} convert(f32[20,128,128]{2,1,0:T(8,128)} %param.3) | non-fusion elementwise | flops 327680 | bytes 1966080 | tf_op jit(solution)/shard_map/convert_element_type | solution.py:311
  1.4 3.8 %collective-permute-start.1 = (bf16[20,128,128]{2,1,0:T(8,128)(2,1)S(1)}, bf16[20,128,128]{2,1,0:T(8,128)(2,1)S(1)}, u32[]{:S(2)}, u32[]{:S(2)}) collective-permute-start(bf16[20,128,128]{2,1,0:T(8,128)(2,1)S(1)} %convert_element_type.33.refs_3_), channel_id=1, source_target_pairs={{0,4},{4,8},{8,12},{12,16},{16,20},{20,24},{24,28},{28,32},{32,36}... | collective-permute-start | bytes 1966088 | tf_op jit(solution)/shard_map/ppermute | solution.py:314
  5.3 2.1 %edges.1 = (bf16[2,10,128,128]{3,2,1,0:T(8,128)(2,1)}, bf16[2,10,128,128]{3,2,1,0:T(8,128)(2,1)}) custom-call(bf16[2,20,128,128]{3,2,1,0:T(8,128)(2,1)} %refs_2_.3), custom_call_target="tpu_custom_call" | custom-call | flops 10000 | bytes 10000 | tf_op jit(solution)/shard_map/edges/pallas_call | solution.py:316
  7.4 3.8 %collective-permute-start.6 = (bf16[2,10,128,128]{3,2,1,0:T(8,128)(2,1)}, bf16[2,10,128,128]{3,2,1,0:T(8,128)(2,1)S(1)}, u32[]{:S(2)}, u32[]{:S(2)}) collective-permute-start(bf16[2,10,128,128]{3,2,1,0:T(8,128)(2,1)} %get-tuple-element.32), channel_id=1, source_target_pairs={{0,4},{4,8},{8,12},{12,16},{16,20},{20,24},{24,28},{28,32},{32,36}... | collective-permute-start | bytes 1966088 | tf_op jit(solution)/shard_map/ppermute | solution.py:328
  11.2 5.1 %collective-permute-start = (bf16[2,10,128,128]{3,2,1,0:T(8,128)(2,1)}, bf16[2,10,128,128]{3,2,1,0:T(8,128)(2,1)S(1)}, u32[]{:S(2)}, u32[]{:S(2)}) collective-permute-start(bf16[2,10,128,128]{3,2,1,0:T(8,128)(2,1)} %get-tuple-element.23), channel_id=1, source_target_pairs={{4,0},{8,4},{12,8},{16,12},{20,16},{24,20},{28,24},{32,28},{36,32}... | collective-permute-start | bytes 1966088 | tf_op jit(solution)/shard_map/ppermute | solution.py:329
  16.3 0.0 copy-done.1
  16.3 2.5 %matrices.1 = (bf16[2,320,256]{2,1,0:T(8,128)(2,1)S(1)}, bf16[2,2,256,256]{3,2,1,0:T(8,128)(2,1)S(1)}, bf16[2,2,128,256]{3,2,1,0:T(8,128)(2,1)S(1)}, f32[2,2,1,128]{3,2,1,0:T(1,128)S(1)}) custom-call(s32[1]{0:T(128)} %bitcast.place_ref.refs_0_, f32[2,3,2,21]{3,2,1,0:T(2,128)S(1)} %copy-done.1), custom_call_target="tpu_custom_call" | custom-call | flops 1000000 | bytes 10000 | tf_op jit(solution)/shard_map/matrices/pallas_call | solution.py:332
  18.9 0.0 collective-permute-done.1
  18.9 4.1 %collective-permute-start.2 = (bf16[10,128,128]{2,1,0:T(8,128)(2,1)S(1)}, bf16[10,128,128]{2,1,0:T(8,128)(2,1)S(1)}, u32[]{:S(2)}, u32[]{:S(2)}) collective-permute-start(bf16[10,128,128]{2,1,0:T(8,128)(2,1)S(1)} %get-tuple-element.44.refs_1_), channel_id=1, source_target_pairs={{0,1},{1,0},{2,3},{3,2},{4,5},{5,4},{6,7},{7,6},{8,9},{9,8},{10,11... | collective-permute-start | bytes 983048 | tf_op jit(solution)/shard_map/ppermute | solution.py:348
  23.0 0.1 collective-permute-start.3
  23.1 1.9 %inverses.2.refs_3_ = f32[2,20,128,128]{3,2,1,0:T(8,128)S(1)} custom-call(s32[1]{0:T(128)} %bitcast.place_ref.refs_0_, bf16[10,128,128]{2,1,0:T(8,128)(2,1)S(1)} %get-tuple-element.44.refs_1_, bf16[10,128,128]{2,1,0:T(8,128)(2,1)S(1)} %get-tuple-element.43.refs_2_, bf16[20,128,128]{2,1,0:T(8,128)(2,1)S(1)} %convert_element_type.33.refs_3_, ...), custom_call_target="tpu_custom_call" | custom-call | flops 1000000 | bytes 10000 | tf_op jit(solution)/shard_map/inverses/pallas_call | solution.py:352
  25.1 0.0 copy-start
  25.1 0.0 collective-permute-done.2.refs_1_
  25.1 0.0 collective-permute-done.3.refs_2_
  25.1 1.9 %inverses.3.refs_4_ = f32[2,20,128,128]{3,2,1,0:T(8,128)S(1)} custom-call(s32[1]{0:T(128)} %bitcast.place_ref.refs_0_, bf16[10,128,128]{2,1,0:T(8,128)(2,1)S(1)} %collective-permute-done.2.refs_1_, bf16[10,128,128]{2,1,0:T(8,128)(2,1)S(1)} %collective-permute-done.3.refs_2_, bf16[20,128,128]{2,1,0:T(8,128)(2,1)S(1)} %convert_element_type.33.refs_3_, ...), custom_call_target="tpu_custom_call" | custom-call | flops 1000000 | bytes 10000 | tf_op jit(solution)/shard_map/inverses/pallas_call | solution.py:352
  27.0 5.0 %collective-permute-done.6.refs_1_ = bf16[2,10,128,128]{3,2,1,0:T(8,128)(2,1)S(1)} collective-permute-done((bf16[2,10,128,128]{3,2,1,0:T(8,128)(2,1)}, bf16[2,10,128,128]{3,2,1,0:T(8,128)(2,1)S(1)}, u32[]{:S(2)}, u32[]{:S(2)}) %collective-permute-start.6) | collective-permute-done | bytes 655392 | tf_op jit(solution)/shard_map/ppermute | solution.py:328
  32.0 0.0 copy-done
  32.0 2.7 %corrections.3 = (f32[2,11,32,128]{3,2,1,0:T(8,128)S(1)}, f32[2,11,32,128]{3,2,1,0:T(8,128)S(1)}) custom-call(s32[1]{0:T(128)} %bitcast.place_ref.refs_0_, bf16[2,10,128,128]{3,2,1,0:T(8,128)(2,1)S(1)} %collective-permute-done.6.refs_1_, bf16[2,20,128,128]{3,2,1,0:T(8,128)(2,1)S(1)} %copy-done, f32[2,20,128,128]{3,2,1,0:T(8,128)S(1)} %inverses.2.refs_3_, ...), custom_call_target="tpu_custom_call" | custom-call | flops 2000000000 | bytes 2000000 | tf_op jit(solution)/shard_map/corrections/pallas_call | solution.py:366
  34.7 1.0 %collective-permute-start.7 = (f32[2,11,32,128]{3,2,1,0:T(8,128)S(1)}, f32[2,11,32,128]{3,2,1,0:T(8,128)S(1)}, u32[]{:S(2)}, u32[]{:S(2)}) collective-permute-start(f32[2,11,32,128]{3,2,1,0:T(8,128)S(1)} %get-tuple-element.34), channel_id=1, source_target_pairs={{0,1},{1,0},{2,3},{3,2},{4,5},{5,4},{6,7},{7,6},{8,9},{9,8},{10,11... | collective-permute-start | bytes 1081352 | tf_op jit(solution)/shard_map/ppermute | solution.py:377
  35.7 0.0 collective-permute-done.refs_1_
  35.7 2.7 %corrections.2 = (f32[2,11,32,128]{3,2,1,0:T(8,128)S(1)}, f32[2,11,32,128]{3,2,1,0:T(8,128)S(1)}) custom-call(s32[1]{0:T(128)} %bitcast.place_ref.refs_0_, bf16[2,10,128,128]{3,2,1,0:T(8,128)(2,1)S(1)} %collective-permute-done.refs_1_, bf16[2,20,128,128]{3,2,1,0:T(8,128)(2,1)S(1)} %copy-done, f32[2,20,128,128]{3,2,1,0:T(8,128)S(1)} %inverses.2.refs_3_, ...), custom_call_target="tpu_custom_call" | custom-call | flops 2000000000 | bytes 2000000 | tf_op jit(solution)/shard_map/corrections/pallas_call | solution.py:366
  38.4 0.1 collective-permute-start.4
  38.5 0.0 collective-permute-done.7
  38.6 2.8 %collective-permute-start.8 = (f16[11,32,128]{2,1,0:T(8,128)(2,1)S(1)}, f16[11,32,128]{2,1,0:T(8,128)(2,1)S(1)}, u32[]{:S(2)}, u32[]{:S(2)}) collective-permute-start(f16[11,32,128]{2,1,0:T(8,128)(2,1)S(1)} %fusion.7), channel_id=1, source_target_pairs={{0,2},{1,3},{2,0},{3,1},{4,6},{5,7},{6,4},{7,5},{8,10},{9,11},{10,... | collective-permute-start | bytes 270344 | tf_op jit(solution)/shard_map/ppermute | solution.py:380
  41.4 0.0 collective-permute-done.4
  41.4 1.6 %collective-permute-start.5 = (f16[11,32,128]{2,1,0:T(8,128)(2,1)S(1)}, f16[11,32,128]{2,1,0:T(8,128)(2,1)S(1)}, u32[]{:S(2)}, u32[]{:S(2)}) collective-permute-start(f16[11,32,128]{2,1,0:T(8,128)(2,1)S(1)} %fusion.6), channel_id=1, source_target_pairs={{0,2},{1,3},{2,0},{3,1},{4,6},{5,7},{6,4},{7,5},{8,10},{9,11},{10,... | collective-permute-start | bytes 270344 | tf_op jit(solution)/shard_map/ppermute | solution.py:380
  43.0 1.1 %fusion.3 = (f32[10,32,128]{2,1,0:T(8,128)S(1)}, f32[10,32,128]{2,1,0:T(8,128)S(1)}) fusion(f32[2,11,32,128]{3,2,1,0:T(8,128)S(1)} %collective-permute-done.7, f32[20,128,128]{2,1,0:T(8,128)} %param.3, s32[]{:T(128)S(6)} %select_n.3, f32[2,11,32,128]{3,2,1,0:T(8,128)S(1)} %get-tuple-element.33, f32[2,11,32,128]{3,2,1,0:T(8,128)S(1)} %collective-permute-done.4, ...), kind=kLoop, calls=%fused_computation.7 | loop fusion | flops 163840 | bytes 1310728 | tf_op jit(solution)/shard_map/mul | solution.py:382
  44.1 1.0 %collective-permute-done.8 = f16[11,32,128]{2,1,0:T(8,128)(2,1)S(1)} collective-permute-done((f16[11,32,128]{2,1,0:T(8,128)(2,1)S(1)}, f16[11,32,128]{2,1,0:T(8,128)(2,1)S(1)}, u32[]{:S(2)}, u32[]{:S(2)}) %collective-permute-start.8) | collective-permute-done | bytes 90144 | tf_op jit(solution)/shard_map/ppermute | solution.py:380
  45.2 2.6 %collective-permute-done.5 = f16[11,32,128]{2,1,0:T(8,128)(2,1)S(1)} collective-permute-done((f16[11,32,128]{2,1,0:T(8,128)(2,1)S(1)}, f16[11,32,128]{2,1,0:T(8,128)(2,1)S(1)}, u32[]{:S(2)}, u32[]{:S(2)}) %collective-permute-start.5) | collective-permute-done | bytes 90144 | tf_op jit(solution)/shard_map/ppermute | solution.py:380
  47.8 0.1 multiply_multiply_fusion
  47.8 0.7 %pad_maximum_fusion = f32[20,32,128]{2,1,0:T(8,128)} fusion(f32[10,32,128]{2,1,0:T(8,128)S(1)} %get-tuple-element.45, f32[10,32,128]{2,1,0:T(8,128)S(1)} %get-tuple-element.46), kind=kLoop, calls=%fused_computation | loop fusion | flops 81920 | bytes 655360 | tf_op jit(solution)/shard_map/concatenate | solution.py:389
  (7 shorter events, 0.1 us)
Async XLA Ops:
  0.0 16.3 %copy-start.1 = (f32[2,3,2,21]{3,2,1,0:T(2,128)S(1)}, f32[2,3,2,21]{3,2,1,0:T(2,128)}, u32[]{:S(2)}) copy-start(f32[2,3,2,21]{3,2,1,0:T(2,128)} %taps_ref.1) | copy-start | bytes 3028
  1.4 17.4 %collective-permute-start.1 = (bf16[20,128,128]{2,1,0:T(8,128)(2,1)S(1)}, bf16[20,128,128]{2,1,0:T(8,128)(2,1)S(1)}, u32[]{:S(2)}, u32[]{:S(2)}) collective-permute-start(bf16[20,128,128]{2,1,0:T(8,128)(2,1)S(1)} %convert_element_type.33.refs_3_), channel_id=1, source_target_pairs={{0,4},{4,8},{8,12},{12,16},{16,20},{20,24},{24,28},{28,32},{32,36}... | collective-permute-start | bytes 1966088 | tf_op jit(solution)/shard_map/ppermute | solution.py:314
  7.4 24.6 %collective-permute-start.6 = (bf16[2,10,128,128]{3,2,1,0:T(8,128)(2,1)}, bf16[2,10,128,128]{3,2,1,0:T(8,128)(2,1)S(1)}, u32[]{:S(2)}, u32[]{:S(2)}) collective-permute-start(bf16[2,10,128,128]{3,2,1,0:T(8,128)(2,1)} %get-tuple-element.32), channel_id=1, source_target_pairs={{0,4},{4,8},{8,12},{12,16},{16,20},{20,24},{24,28},{28,32},{32,36}... | collective-permute-start | bytes 1966088 | tf_op jit(solution)/shard_map/ppermute | solution.py:328
  11.2 24.5 %collective-permute-start = (bf16[2,10,128,128]{3,2,1,0:T(8,128)(2,1)}, bf16[2,10,128,128]{3,2,1,0:T(8,128)(2,1)S(1)}, u32[]{:S(2)}, u32[]{:S(2)}) collective-permute-start(bf16[2,10,128,128]{3,2,1,0:T(8,128)(2,1)} %get-tuple-element.23), channel_id=1, source_target_pairs={{4,0},{8,4},{12,8},{16,12},{20,16},{24,20},{28,24},{32,28},{36,32}... | collective-permute-start | bytes 1966088 | tf_op jit(solution)/shard_map/ppermute | solution.py:329
  18.9 6.1 %collective-permute-start.2 = (bf16[10,128,128]{2,1,0:T(8,128)(2,1)S(1)}, bf16[10,128,128]{2,1,0:T(8,128)(2,1)S(1)}, u32[]{:S(2)}, u32[]{:S(2)}) collective-permute-start(bf16[10,128,128]{2,1,0:T(8,128)(2,1)S(1)} %get-tuple-element.44.refs_1_), channel_id=1, source_target_pairs={{0,1},{1,0},{2,3},{3,2},{4,5},{5,4},{6,7},{7,6},{8,9},{9,8},{10,11... | collective-permute-start | bytes 983048 | tf_op jit(solution)/shard_map/ppermute | solution.py:348
  23.0 2.1 %collective-permute-start.3 = (bf16[10,128,128]{2,1,0:T(8,128)(2,1)S(1)}, bf16[10,128,128]{2,1,0:T(8,128)(2,1)S(1)}, u32[]{:S(2)}, u32[]{:S(2)}) collective-permute-start(bf16[10,128,128]{2,1,0:T(8,128)(2,1)S(1)} %get-tuple-element.43.refs_2_), channel_id=1, source_target_pairs={{0,1},{1,0},{2,3},{3,2},{4,5},{5,4},{6,7},{7,6},{8,9},{9,8},{10,11... | collective-permute-start | bytes 983048 | tf_op jit(solution)/shard_map/ppermute | solution.py:348
  25.1 6.9 %copy-start = (bf16[2,20,128,128]{3,2,1,0:T(8,128)(2,1)S(1)}, bf16[2,20,128,128]{3,2,1,0:T(8,128)(2,1)}, u32[]{:S(2)}) copy-start(bf16[2,20,128,128]{3,2,1,0:T(8,128)(2,1)} %refs_2_.3) | copy-start | bytes 3932164
  34.7 3.8 %collective-permute-start.7 = (f32[2,11,32,128]{3,2,1,0:T(8,128)S(1)}, f32[2,11,32,128]{3,2,1,0:T(8,128)S(1)}, u32[]{:S(2)}, u32[]{:S(2)}) collective-permute-start(f32[2,11,32,128]{3,2,1,0:T(8,128)S(1)} %get-tuple-element.34), channel_id=1, source_target_pairs={{0,1},{1,0},{2,3},{3,2},{4,5},{5,4},{6,7},{7,6},{8,9},{9,8},{10,11... | collective-permute-start | bytes 1081352 | tf_op jit(solution)/shard_map/ppermute | solution.py:377
  38.4 3.0 %collective-permute-start.4 = (f32[2,11,32,128]{3,2,1,0:T(8,128)S(1)}, f32[2,11,32,128]{3,2,1,0:T(8,128)S(1)}, u32[]{:S(2)}, u32[]{:S(2)}) collective-permute-start(f32[2,11,32,128]{3,2,1,0:T(8,128)S(1)} %get-tuple-element.31), channel_id=1, source_target_pairs={{0,1},{1,0},{2,3},{3,2},{4,5},{5,4},{6,7},{7,6},{8,9},{9,8},{10,11... | collective-permute-start | bytes 1081352 | tf_op jit(solution)/shard_map/ppermute | solution.py:377
  38.6 6.6 %collective-permute-start.8 = (f16[11,32,128]{2,1,0:T(8,128)(2,1)S(1)}, f16[11,32,128]{2,1,0:T(8,128)(2,1)S(1)}, u32[]{:S(2)}, u32[]{:S(2)}) collective-permute-start(f16[11,32,128]{2,1,0:T(8,128)(2,1)S(1)} %fusion.7), channel_id=1, source_target_pairs={{0,2},{1,3},{2,0},{3,1},{4,6},{5,7},{6,4},{7,5},{8,10},{9,11},{10,... | collective-permute-start | bytes 270344 | tf_op jit(solution)/shard_map/ppermute | solution.py:380
  41.4 6.3 %collective-permute-start.5 = (f16[11,32,128]{2,1,0:T(8,128)(2,1)S(1)}, f16[11,32,128]{2,1,0:T(8,128)(2,1)S(1)}, u32[]{:S(2)}, u32[]{:S(2)}) collective-permute-start(f16[11,32,128]{2,1,0:T(8,128)(2,1)S(1)} %fusion.6), channel_id=1, source_target_pairs={{0,2},{1,3},{2,0},{3,1},{4,6},{5,7},{6,4},{7,5},{8,10},{9,11},{10,... | collective-permute-start | bytes 270344 | tf_op jit(solution)/shard_map/ppermute | solution.py:380

commit v9 on v6

--- a/solution.py
+++ b/solution.py
@@ -225,13 +225,27 @@
     filter_to(load, views, 2, z_ref.at[0], x_ref.at[0], y_ref.at[0], scale_ref, e_ref, g_ref, False, emit)
 
 
+def arrange_kernel(place_ref, rec_ref, early_ref, late_ref, own_out, rim_out):
+    views, planes = rec_ref.shape[:2]
+    half = planes // 2
+    early_first = place_ref[0] % 2 == 0
+    for v in range(views):
+        for z in range(planes):
+            early, late = early_ref[v, z], late_ref[v, z]
+            first, second = jnp.where(early_first, early, late), jnp.where(early_first, late, early)
+            if z < half:
+                rim_out[v, 0, z] = first
+                own_out[v, half + z] = (rec_ref[v, half + z].astype(F32) * second).astype(BF16)
+            else:
+                own_out[v, z - half] = (rec_ref[v, z - half].astype(F32) * first).astype(BF16)
+                rim_out[v, 1, z - half] = second
+
+
 def correction_kernel(
-    place_ref,
     before_ref,
-    rec_ref,
+    own_ref,
     after_ref,
-    early_ref,
-    late_ref,
+    rim_ref,
     z_ref,
     x_ref,
     y_ref,
@@ -242,18 +256,16 @@
     g_ref,
     product_ref,
 ):
-    views, planes = rec_ref.shape[:2]
+    views, planes = own_ref.shape[:2]
     part = keep_ref.shape[2]
     tall = z_ref.shape[1] // views
-    early_first = place_ref[0] % 2 == 0
     most = [jnp.zeros((8, product_ref.shape[2]), F32)]
     for v in range(views):
 
         def load(at, v=v):
-            rec = [ref[v, :, at, :].astype(F32) for ref in (before_ref, rec_ref, after_ref)]
-            early, late = early_ref[v, :, at, :], late_ref[v, :, at, :]
-            inverse = [jnp.where(early_first, early, late), jnp.where(early_first, late, early)]
-            return jnp.concatenate(rec, axis=0) * jnp.concatenate(inverse, axis=0)
+            before = before_ref[v, :, at, :].astype(F32) * rim_ref[v, 0, :, at, :]
+            after = after_ref[v, :, at, :].astype(F32) * rim_ref[v, 1, :, at, :]
+            return jnp.concatenate([before, own_ref[v, :, at, :].astype(F32), after], axis=0)
 
         def emit(_, z, value, v=v):
             if v > 0:
@@ -355,16 +367,24 @@
                 **params(10**6, 10**4),
             )(place_array, *side, rounded, z_mat, x_mat, y_mat, scales)
         )
+    own, rim = pl.pallas_call(
+        arrange_kernel,
+        out_shape=[shape((views, planes, rows, cols), BF16), shape((views, 2, margin, rows, cols), F32)],
+        in_specs=[SMEM] + [VMEM] * 3,
+        out_specs=[VMEM] * 2,
+        name="arrange",
+        **params(10**5, 10**4),
+    )(place_array, recordings, *inverses)
     part = rows // 4
     keep, send = pl.pallas_call(
         correction_kernel,
         out_shape=[shape((2, planes + 1, part, cols), F32)] * 2,
-        in_specs=[SMEM] + [VMEM] * 9,
+        in_specs=[VMEM] * 8,
         out_specs=[VMEM] * 2,
         scratch_shapes=scratch(1, 2, 2, z_out, rows, cols) + [pltpu.VMEM((planes, rows, cols), F32)],
         name="corrections",
         **params(4 * 10**9, 5 * 10**6),
-    )(place_array, before, recordings, after, *inverses, z_mat, x_mat, y_mat, scales)
+    )(before, own, after, rim, z_mat, x_mat, y_mat, scales)
     core = lax.ppermute(send, "view", swap)
     across = lax.ppermute((keep[1] * core[1]).astype(jnp.float16), "view", [(i, i ^ 2) for i in range(4)])
     own_rows = lax.dynamic_slice_in_dim(estimate, place * part, part, 1)

time: 48.1 us -> 47.8 us (level)
  transfers between devices with their start and end apart: 7 -> 7, of which waited for: 3 -> 3; matrix products, arithmetic and copies ran while one was open for 2% -> 2% of each run, Pallas kernels for 18% -> 19%
where the time goes in v9:
time: 47.8 us; the launch traced here: 47.5 us
  starting transfers between devices  20.6 us (43%)
  Pallas kernels  12.8 us (27%)
  waiting for transfers between devices  10.7 us (22%)
  other arithmetic  3.33 us (7%)
    ppermute x1, starting transfers between devices, local(): after = lax.ppermute(first, 'gz', down)  5.06 us
    ppermute x1, waiting for transfers between devices, local(): before = lax.ppermute(last, 'gz', up)  4.54 us
    ppermute x1, waiting for transfers between devices, local(): lax.ppermute((keep[1] * core[1]).astype(jnp.float16), 'view', [(i, i ^ 2)...  4.35 us
    ppermute x2, starting transfers between devices, local(): other = [lax.ppermute(piece, 'view', swap) for piece in mine]  4.19 us
    pallas_call x2, Pallas kernels, local(): pl.pallas_call(lambda *refs, early=early: inverse_kernel(early, *refs), o...  3.86 us
    pallas_call x1, Pallas kernels, local(): pl.pallas_call(correction_kernel, out_shape=[shape((2, planes + 1, part,...  3.84 us
    ppermute x1, starting transfers between devices, local(): mine = lax.ppermute(rounded, ('gz', 'view'), both_ways)  3.83 us
    ppermute x1, starting transfers between devices, local(): before = lax.ppermute(last, 'gz', up)  3.83 us
  transfers between devices with their start and end apart: 7, of which 3 were waited for; matrix products, arithmetic and copies ran while one was open for 2% of the time, Pallas kernels for 19%

profile of v9, /device:TPU:24, one launch (start us, length us, event | category | flops | bytes accessed | tf_op | source)
XLA Modules:
  0.0 47.5 jit_solution(6174408633052103040)
XLA Ops:
  0.0 0.0 copy-start.1
  0.0 1.4 %convert_element_type.18.refs_3_ = bf16[20,128,128]{2,1,0:T(8,128)(2,1)S(1)} convert(f32[20,128,128]{2,1,0:T(8,128)} %param.3) | non-fusion elementwise | flops 327680 | bytes 1966080 | tf_op jit(solution)/shard_map/convert_element_type | solution.py:319
  1.4 3.8 %collective-permute-start.1 = (bf16[20,128,128]{2,1,0:T(8,128)(2,1)S(1)}, bf16[20,128,128]{2,1,0:T(8,128)(2,1)S(1)}, u32[]{:S(2)}, u32[]{:S(2)}) collective-permute-start(bf16[20,128,128]{2,1,0:T(8,128)(2,1)S(1)} %convert_element_type.18.refs_3_), channel_id=1, source_target_pairs={{0,4},{4,8},{8,12},{12,16},{16,20},{20,24},{24,28},{28,32},{32,36}... | collective-permute-start | bytes 1966088 | tf_op jit(solution)/shard_map/ppermute | solution.py:322
  5.3 2.1 %edges.1 = (bf16[2,10,128,128]{3,2,1,0:T(8,128)(2,1)}, bf16[2,10,128,128]{3,2,1,0:T(8,128)(2,1)}) custom-call(bf16[2,20,128,128]{3,2,1,0:T(8,128)(2,1)} %rec_ref.3), custom_call_target="tpu_custom_call" | custom-call | flops 10000 | bytes 10000 | tf_op jit(solution)/shard_map/edges/pallas_call | solution.py:324
  7.4 3.8 %collective-permute-start = (bf16[2,10,128,128]{3,2,1,0:T(8,128)(2,1)}, bf16[2,10,128,128]{3,2,1,0:T(8,128)(2,1)S(1)}, u32[]{:S(2)}, u32[]{:S(2)}) collective-permute-start(bf16[2,10,128,128]{3,2,1,0:T(8,128)(2,1)} %get-tuple-element.20), channel_id=1, source_target_pairs={{0,4},{4,8},{8,12},{12,16},{16,20},{20,24},{24,28},{28,32},{32,36}... | collective-permute-start | bytes 1966088 | tf_op jit(solution)/shard_map/ppermute | solution.py:336
  11.2 5.1 %collective-permute-start.4 = (bf16[2,10,128,128]{3,2,1,0:T(8,128)(2,1)}, bf16[2,10,128,128]{3,2,1,0:T(8,128)(2,1)S(1)}, u32[]{:S(2)}, u32[]{:S(2)}) collective-permute-start(bf16[2,10,128,128]{3,2,1,0:T(8,128)(2,1)} %get-tuple-element.28), channel_id=1, source_target_pairs={{4,0},{8,4},{12,8},{16,12},{20,16},{24,20},{28,24},{32,28},{36,32}... | collective-permute-start | bytes 1966088 | tf_op jit(solution)/shard_map/ppermute | solution.py:337
  16.3 0.0 copy-done.1
  16.3 2.5 %matrices.1 = (bf16[2,320,256]{2,1,0:T(8,128)(2,1)S(1)}, bf16[2,2,256,256]{3,2,1,0:T(8,128)(2,1)S(1)}, bf16[2,2,128,256]{3,2,1,0:T(8,128)(2,1)S(1)}, f32[2,2,1,128]{3,2,1,0:T(1,128)S(1)}) custom-call(s32[1]{0:T(128)} %bitcast.place_ref.refs_0_, f32[2,3,2,21]{3,2,1,0:T(2,128)S(1)} %copy-done.1), custom_call_target="tpu_custom_call" | custom-call | flops 1000000 | bytes 10000 | tf_op jit(solution)/shard_map/matrices/pallas_call | solution.py:340
  18.9 0.0 collective-permute-done.1
  18.9 4.1 %collective-permute-start.2 = (bf16[10,128,128]{2,1,0:T(8,128)(2,1)S(1)}, bf16[10,128,128]{2,1,0:T(8,128)(2,1)S(1)}, u32[]{:S(2)}, u32[]{:S(2)}) collective-permute-start(bf16[10,128,128]{2,1,0:T(8,128)(2,1)S(1)} %get-tuple-element.36.refs_1_), channel_id=1, source_target_pairs={{0,1},{1,0},{2,3},{3,2},{4,5},{5,4},{6,7},{7,6},{8,9},{9,8},{10,11... | collective-permute-start | bytes 983048 | tf_op jit(solution)/shard_map/ppermute | solution.py:356
  23.0 0.1 collective-permute-start.3
  23.1 1.9 %inverses.2.early_ref = f32[2,20,128,128]{3,2,1,0:T(8,128)S(1)} custom-call(s32[1]{0:T(128)} %bitcast.place_ref.refs_0_, bf16[10,128,128]{2,1,0:T(8,128)(2,1)S(1)} %get-tuple-element.36.refs_1_, bf16[10,128,128]{2,1,0:T(8,128)(2,1)S(1)} %get-tuple-element.35.refs_2_, bf16[20,128,128]{2,1,0:T(8,128)(2,1)S(1)} %convert_element_type.18.refs_3_, ...), custom_call_target="tpu_custom_call" | custom-call | flops 1000000 | bytes 10000 | tf_op jit(solution)/shard_map/inverses/pallas_call | solution.py:360
  25.1 0.0 copy-start
  25.1 0.0 collective-permute-done.2.refs_1_
  25.1 0.0 collective-permute-done.3.refs_2_
  25.1 1.9 %inverses.3.late_ref = f32[2,20,128,128]{3,2,1,0:T(8,128)S(1)} custom-call(s32[1]{0:T(128)} %bitcast.place_ref.refs_0_, bf16[10,128,128]{2,1,0:T(8,128)(2,1)S(1)} %collective-permute-done.2.refs_1_, bf16[10,128,128]{2,1,0:T(8,128)(2,1)S(1)} %collective-permute-done.3.refs_2_, bf16[20,128,128]{2,1,0:T(8,128)(2,1)S(1)} %convert_element_type.18.refs_3_, ...), custom_call_target="tpu_custom_call" | custom-call | flops 1000000 | bytes 10000 | tf_op jit(solution)/shard_map/inverses/pallas_call | solution.py:360
  27.0 0.0 copy-done
  27.1 0.4 arrange.1
  27.5 4.5 %collective-permute-done.before_ref = bf16[2,10,128,128]{3,2,1,0:T(8,128)(2,1)S(1)} collective-permute-done((bf16[2,10,128,128]{3,2,1,0:T(8,128)(2,1)}, bf16[2,10,128,128]{3,2,1,0:T(8,128)(2,1)S(1)}, u32[]{:S(2)}, u32[]{:S(2)}) %collective-permute-start) | collective-permute-done | bytes 655392 | tf_op jit(solution)/shard_map/ppermute | solution.py:336
  32.0 0.0 collective-permute-done.4.after_ref
  32.0 3.8 %corrections.1 = (f32[2,21,32,128]{3,2,1,0:T(8,128)S(1)}, f32[2,21,32,128]{3,2,1,0:T(8,128)S(1)}) custom-call(bf16[2,10,128,128]{3,2,1,0:T(8,128)(2,1)S(1)} %collective-permute-done.before_ref, bf16[2,20,128,128]{3,2,1,0:T(8,128)(2,1)S(1)} %get-tuple-element.27.own_ref, bf16[2,10,128,128]{3,2,1,0:T(8,128)(2,1)S(1)} %collective-permute-done.4.after_ref, ...), custom_call_target="tpu_custom_call" | custom-call | flops 4000000000 | bytes 5000000 | tf_op jit(solution)/shard_map/corrections/pallas_call | solution.py:379
  35.9 0.8 %collective-permute-start.5 = (f32[2,21,32,128]{3,2,1,0:T(8,128)S(1)}, f32[2,21,32,128]{3,2,1,0:T(8,128)S(1)}, u32[]{:S(2)}, u32[]{:S(2)}) collective-permute-start(f32[2,21,32,128]{3,2,1,0:T(8,128)S(1)} %get-tuple-element.31), channel_id=1, source_target_pairs={{0,1},{1,0},{2,3},{3,2},{4,5},{5,4},{6,7},{7,6},{8,9},{9,8},{10,11... | collective-permute-start | bytes 2064392 | tf_op jit(solution)/shard_map/ppermute | solution.py:388
  36.7 1.8 %collective-permute-done.5 = f32[2,21,32,128]{3,2,1,0:T(8,128)S(1)} collective-permute-done((f32[2,21,32,128]{3,2,1,0:T(8,128)S(1)}, f32[2,21,32,128]{3,2,1,0:T(8,128)S(1)}, u32[]{:S(2)}, u32[]{:S(2)}) %collective-permute-start.5) | collective-permute-done | bytes 688160 | tf_op jit(solution)/shard_map/ppermute | solution.py:388
  38.5 0.1 fusion.3
  38.5 2.8 %collective-permute-start.6 = (f16[21,32,128]{2,1,0:T(8,128)(2,1)S(1)}, f16[21,32,128]{2,1,0:T(8,128)(2,1)S(1)}, u32[]{:S(2)}, u32[]{:S(2)}) collective-permute-start(f16[21,32,128]{2,1,0:T(8,128)(2,1)S(1)} %fusion.3), channel_id=1, source_target_pairs={{0,2},{1,3},{2,0},{3,1},{4,6},{5,7},{6,4},{7,5},{8,10},{9,11},{10,... | collective-permute-start | bytes 516104 | tf_op jit(solution)/shard_map/ppermute | solution.py:389
  41.3 1.1 %fusion.2 = f32[20,32,128]{2,1,0:T(8,128)S(1)} fusion(f32[2,21,32,128]{3,2,1,0:T(8,128)S(1)} %collective-permute-done.5, f32[2,21,32,128]{3,2,1,0:T(8,128)S(1)} %get-tuple-element.30, f32[20,128,128]{2,1,0:T(8,128)} %param.3, s32[]{:T(128)S(6)} %select_n.3), kind=kLoop, calls=%fused_computation.4 | loop fusion | flops 163840 | bytes 1310724 | tf_op jit(solution)/shard_map/mul | solution.py:392
  42.4 4.3 %collective-permute-done.6 = f16[21,32,128]{2,1,0:T(8,128)(2,1)S(1)} collective-permute-done((f16[21,32,128]{2,1,0:T(8,128)(2,1)S(1)}, f16[21,32,128]{2,1,0:T(8,128)(2,1)S(1)}, u32[]{:S(2)}, u32[]{:S(2)}) %collective-permute-start.6) | collective-permute-done | bytes 172064 | tf_op jit(solution)/shard_map/ppermute | solution.py:389
  46.8 0.8 %multiply_multiply_fusion = f32[20,32,128]{2,1,0:T(8,128)} fusion(f32[20,32,128]{2,1,0:T(8,128)S(1)} %fusion.2, f32[32,128]{1,0:T(8,128)S(1)} %multiply_multiply_fusion.1, f16[21,32,128]{2,1,0:T(8,128)(2,1)S(1)} %collective-permute-done.6), kind=kLoop, calls=%fused_computation.5 | loop fusion | flops 245760 | bytes 835584 | tf_op jit(solution)/shard_map/mul | solution.py:395
  (3 shorter events, 0.1 us)
Async XLA Ops:
  0.0 16.3 %copy-start.1 = (f32[2,3,2,21]{3,2,1,0:T(2,128)S(1)}, f32[2,3,2,21]{3,2,1,0:T(2,128)}, u32[]{:S(2)}) copy-start(f32[2,3,2,21]{3,2,1,0:T(2,128)} %taps_ref.1) | copy-start | bytes 3028
  1.4 17.4 %collective-permute-start.1 = (bf16[20,128,128]{2,1,0:T(8,128)(2,1)S(1)}, bf16[20,128,128]{2,1,0:T(8,128)(2,1)S(1)}, u32[]{:S(2)}, u32[]{:S(2)}) collective-permute-start(bf16[20,128,128]{2,1,0:T(8,128)(2,1)S(1)} %convert_element_type.18.refs_3_), channel_id=1, source_target_pairs={{0,4},{4,8},{8,12},{12,16},{16,20},{20,24},{24,28},{28,32},{32,36}... | collective-permute-start | bytes 1966088 | tf_op jit(solution)/shard_map/ppermute | solution.py:322
  7.4 24.6 %collective-permute-start = (bf16[2,10,128,128]{3,2,1,0:T(8,128)(2,1)}, bf16[2,10,128,128]{3,2,1,0:T(8,128)(2,1)S(1)}, u32[]{:S(2)}, u32[]{:S(2)}) collective-permute-start(bf16[2,10,128,128]{3,2,1,0:T(8,128)(2,1)} %get-tuple-element.20), channel_id=1, source_target_pairs={{0,4},{4,8},{8,12},{12,16},{16,20},{20,24},{24,28},{28,32},{32,36}... | collective-permute-start | bytes 1966088 | tf_op jit(solution)/shard_map/ppermute | solution.py:336
  11.2 20.8 %collective-permute-start.4 = (bf16[2,10,128,128]{3,2,1,0:T(8,128)(2,1)}, bf16[2,10,128,128]{3,2,1,0:T(8,128)(2,1)S(1)}, u32[]{:S(2)}, u32[]{:S(2)}) collective-permute-start(bf16[2,10,128,128]{3,2,1,0:T(8,128)(2,1)} %get-tuple-element.28), channel_id=1, source_target_pairs={{4,0},{8,4},{12,8},{16,12},{20,16},{24,20},{28,24},{32,28},{36,32}... | collective-permute-start | bytes 1966088 | tf_op jit(solution)/shard_map/ppermute | solution.py:337
  18.9 6.1 %collective-permute-start.2 = (bf16[10,128,128]{2,1,0:T(8,128)(2,1)S(1)}, bf16[10,128,128]{2,1,0:T(8,128)(2,1)S(1)}, u32[]{:S(2)}, u32[]{:S(2)}) collective-permute-start(bf16[10,128,128]{2,1,0:T(8,128)(2,1)S(1)} %get-tuple-element.36.refs_1_), channel_id=1, source_target_pairs={{0,1},{1,0},{2,3},{3,2},{4,5},{5,4},{6,7},{7,6},{8,9},{9,8},{10,11... | collective-permute-start | bytes 983048 | tf_op jit(solution)/shard_map/ppermute | solution.py:356
  23.0 2.1 %collective-permute-start.3 = (bf16[10,128,128]{2,1,0:T(8,128)(2,1)S(1)}, bf16[10,128,128]{2,1,0:T(8,128)(2,1)S(1)}, u32[]{:S(2)}, u32[]{:S(2)}) collective-permute-start(bf16[10,128,128]{2,1,0:T(8,128)(2,1)S(1)} %get-tuple-element.35.refs_2_), channel_id=1, source_target_pairs={{0,1},{1,0},{2,3},{3,2},{4,5},{5,4},{6,7},{7,6},{8,9},{9,8},{10,11... | collective-permute-start | bytes 983048 | tf_op jit(solution)/shard_map/ppermute | solution.py:356
  25.1 2.0 %copy-start = (bf16[2,20,128,128]{3,2,1,0:T(8,128)(2,1)S(1)}, bf16[2,20,128,128]{3,2,1,0:T(8,128)(2,1)}, u32[]{:S(2)}) copy-start(bf16[2,20,128,128]{3,2,1,0:T(8,128)(2,1)} %rec_ref.3) | copy-start | bytes 3932164
  35.9 2.6 %collective-permute-start.5 = (f32[2,21,32,128]{3,2,1,0:T(8,128)S(1)}, f32[2,21,32,128]{3,2,1,0:T(8,128)S(1)}, u32[]{:S(2)}, u32[]{:S(2)}) collective-permute-start(f32[2,21,32,128]{3,2,1,0:T(8,128)S(1)} %get-tuple-element.31), channel_id=1, source_target_pairs={{0,1},{1,0},{2,3},{3,2},{4,5},{5,4},{6,7},{7,6},{8,9},{9,8},{10,11... | collective-permute-start | bytes 2064392 | tf_op jit(solution)/shard_map/ppermute | solution.py:388
  38.5 8.2 %collective-permute-start.6 = (f16[21,32,128]{2,1,0:T(8,128)(2,1)S(1)}, f16[21,32,128]{2,1,0:T(8,128)(2,1)S(1)}, u32[]{:S(2)}, u32[]{:S(2)}) collective-permute-start(f16[21,32,128]{2,1,0:T(8,128)(2,1)S(1)} %fusion.3), channel_id=1, source_target_pairs={{0,2},{1,3},{2,0},{3,1},{4,6},{5,7},{6,4},{7,5},{8,10},{9,11},{10,... | collective-permute-start | bytes 516104 | tf_op jit(solution)/shard_map/ppermute | solution.py:389

commit v10 on v9

--- a/solution.py
+++ b/solution.py
@@ -251,7 +251,8 @@
     y_ref,
     scale_ref,
     keep_ref,
-    send_ref,
+    near_ref,
+    far_ref,
     e_ref,
     g_ref,
     product_ref,
@@ -293,13 +294,13 @@
     quarter = jnp.ceil(jnp.log2(top) * 0.25)
     scale = jnp.exp2(-4.0 * quarter)
     root = jnp.broadcast_to(jnp.exp2(quarter), (part, product_ref.shape[2]))
+    targets = (keep_ref.at[0], near_ref, keep_ref.at[1], far_ref)
     for z in range(planes):
         value = product_ref[z] * scale
         for b in range(4):
-            (keep_ref, send_ref)[b % 2][b // 2, z] = value[b * part : (b + 1) * part]
-    for ref in (keep_ref, send_ref):
-        for b in range(2):
-            ref[b, planes] = root
+            targets[b][z] = value[b * part : (b + 1) * part]
+    for target in targets:
+        target[planes] = root
 
 
 def local(estimate, recordings, psf_taps):
@@ -376,20 +377,21 @@
         **params(10**5, 10**4),
     )(place_array, recordings, *inverses)
     part = rows // 4
-    keep, send = pl.pallas_call(
+    keep, near, far = pl.pallas_call(
         correction_kernel,
-        out_shape=[shape((2, planes + 1, part, cols), F32)] * 2,
+        out_shape=[shape((2, planes + 1, part, cols), F32)] + [shape((planes + 1, part, cols), F32)] * 2,
         in_specs=[VMEM] * 8,
-        out_specs=[VMEM] * 2,
+        out_specs=[VMEM] * 3,
         scratch_shapes=scratch(1, 2, 2, z_out, rows, cols) + [pltpu.VMEM((planes, rows, cols), F32)],
         name="corrections",
         **params(4 * 10**9, 5 * 10**6),
     )(before, own, after, rim, z_mat, x_mat, y_mat, scales)
-    core = lax.ppermute(send, "view", swap)
-    across = lax.ppermute((keep[1] * core[1]).astype(jnp.float16), "view", [(i, i ^ 2) for i in range(4)])
+    core_far = lax.ppermute(far, "view", swap)
+    core_near = lax.ppermute(near, "view", swap)
+    across = lax.ppermute((keep[1] * core_far).astype(jnp.float16), "view", [(i, i ^ 2) for i in range(4)])
     own_rows = lax.dynamic_slice_in_dim(estimate, place * part, part, 1)
-    root = keep[0, planes] * core[0, planes]
-    partial = own_rows * (keep[0, :planes] * core[0, :planes])
+    root = keep[0, planes] * core_near[planes]
+    partial = own_rows * (keep[0, :planes] * core_near[:planes])
     partial, root, across = lax.optimization_barrier((partial, root, across))
     root = root * across[planes].astype(F32)
     return partial * (across[:planes].astype(F32) * (root * root * root * root))

time: 47.8 us -> 47.3 us (0.990)
  waiting for transfers between devices: 10.7 us -> 9.92 us
    ppermute x2 -> x3, waiting for transfers between devices: 6.12 us -> 5.52 us  [the longest x1 4.34 us: local(): lax.ppermute((keep[1] * core_far).astype(jnp.float16), 'view', [(i, i ^ 2...]
    ppermute x2 -> x3, starting transfers between devices: 3.66 us -> 3.76 us  [the longest x1 2.84 us: local(): lax.ppermute((keep[1] * core_far).astype(jnp.float16), 'view', [(i, i ^ 2...]
  transfers between devices with their start and end apart: 7 -> 8, of which waited for: 3 -> 3; matrix products, arithmetic and copies ran while one was open for 2% -> 2% of each run, Pallas kernels for 19% -> 19%
where the time goes in v10:
time: 47.3 us; the launch traced here: 47.1 us
  starting transfers between devices  20.7 us (44%)
  Pallas kernels  12.9 us (27%)
  waiting for transfers between devices  9.92 us (21%)
  other arithmetic  3.33 us (7%)
    ppermute x1, starting transfers between devices, local(): after = lax.ppermute(first, 'gz', down)  5.06 us
    ppermute x1, waiting for transfers between devices, local(): before = lax.ppermute(last, 'gz', up)  4.39 us
    ppermute x1, waiting for transfers between devices, local(): lax.ppermute((keep[1] * core_far).astype(jnp.float16), 'view', [(i, i ^ 2...  4.34 us
    ppermute x2, starting transfers between devices, local(): other = [lax.ppermute(piece, 'view', swap) for piece in mine]  4.19 us
    pallas_call x2, Pallas kernels, local(): pl.pallas_call(lambda *refs, early=early: inverse_kernel(early, *refs), o...  3.9 us
    pallas_call x1, Pallas kernels, local(): pl.pallas_call(correction_kernel, out_shape=[shape((2, planes + 1, part,...  3.85 us
    ppermute x1, starting transfers between devices, local(): mine = lax.ppermute(rounded, ('gz', 'view'), both_ways)  3.83 us
    ppermute x1, starting transfers between devices, local(): before = lax.ppermute(last, 'gz', up)  3.83 us
  transfers between devices with their start and end apart: 8, of which 3 were waited for; matrix products, arithmetic and copies ran while one was open for 2% of the time, Pallas kernels for 19%

profile of v10, /device:TPU:24, one launch (start us, length us, event | category | flops | bytes accessed | tf_op | source)
XLA Modules:
  0.0 47.1 jit_solution(10866862620306501034)
XLA Ops:
  0.0 0.0 copy-start.1
  0.0 1.4 %convert_element_type.15.refs_3_ = bf16[20,128,128]{2,1,0:T(8,128)(2,1)S(1)} convert(f32[20,128,128]{2,1,0:T(8,128)} %param.3) | non-fusion elementwise | flops 327680 | bytes 1966080 | tf_op jit(solution)/shard_map/convert_element_type | solution.py:320
  1.4 3.8 %collective-permute-start.1 = (bf16[20,128,128]{2,1,0:T(8,128)(2,1)S(1)}, bf16[20,128,128]{2,1,0:T(8,128)(2,1)S(1)}, u32[]{:S(2)}, u32[]{:S(2)}) collective-permute-start(bf16[20,128,128]{2,1,0:T(8,128)(2,1)S(1)} %convert_element_type.15.refs_3_), channel_id=1, source_target_pairs={{0,4},{4,8},{8,12},{12,16},{16,20},{20,24},{24,28},{28,32},{32,36}... | collective-permute-start | bytes 1966088 | tf_op jit(solution)/shard_map/ppermute | solution.py:323
  5.3 2.1 %edges.1 = (bf16[2,10,128,128]{3,2,1,0:T(8,128)(2,1)}, bf16[2,10,128,128]{3,2,1,0:T(8,128)(2,1)}) custom-call(bf16[2,20,128,128]{3,2,1,0:T(8,128)(2,1)} %rec_ref.3), custom_call_target="tpu_custom_call" | custom-call | flops 10000 | bytes 10000 | tf_op jit(solution)/shard_map/edges/pallas_call | solution.py:325
  7.4 3.8 %collective-permute-start = (bf16[2,10,128,128]{3,2,1,0:T(8,128)(2,1)}, bf16[2,10,128,128]{3,2,1,0:T(8,128)(2,1)S(1)}, u32[]{:S(2)}, u32[]{:S(2)}) collective-permute-start(bf16[2,10,128,128]{3,2,1,0:T(8,128)(2,1)} %get-tuple-element.21), channel_id=1, source_target_pairs={{0,4},{4,8},{8,12},{12,16},{16,20},{20,24},{24,28},{28,32},{32,36}... | collective-permute-start | bytes 1966088 | tf_op jit(solution)/shard_map/ppermute | solution.py:337
  11.2 5.1 %collective-permute-start.4 = (bf16[2,10,128,128]{3,2,1,0:T(8,128)(2,1)}, bf16[2,10,128,128]{3,2,1,0:T(8,128)(2,1)S(1)}, u32[]{:S(2)}, u32[]{:S(2)}) collective-permute-start(bf16[2,10,128,128]{3,2,1,0:T(8,128)(2,1)} %get-tuple-element.29), channel_id=1, source_target_pairs={{4,0},{8,4},{12,8},{16,12},{20,16},{24,20},{28,24},{32,28},{36,32}... | collective-permute-start | bytes 1966088 | tf_op jit(solution)/shard_map/ppermute | solution.py:338
  16.3 0.0 copy-done.1
  16.3 2.5 %matrices.1 = (bf16[2,320,256]{2,1,0:T(8,128)(2,1)S(1)}, bf16[2,2,256,256]{3,2,1,0:T(8,128)(2,1)S(1)}, bf16[2,2,128,256]{3,2,1,0:T(8,128)(2,1)S(1)}, f32[2,2,1,128]{3,2,1,0:T(1,128)S(1)}) custom-call(s32[1]{0:T(128)} %bitcast.place_ref.refs_0_, f32[2,3,2,21]{3,2,1,0:T(2,128)S(1)} %copy-done.1), custom_call_target="tpu_custom_call" | custom-call | flops 1000000 | bytes 10000 | tf_op jit(solution)/shard_map/matrices/pallas_call | solution.py:341
  18.9 0.0 collective-permute-done.1
  18.9 4.1 %collective-permute-start.2 = (bf16[10,128,128]{2,1,0:T(8,128)(2,1)S(1)}, bf16[10,128,128]{2,1,0:T(8,128)(2,1)S(1)}, u32[]{:S(2)}, u32[]{:S(2)}) collective-permute-start(bf16[10,128,128]{2,1,0:T(8,128)(2,1)S(1)} %get-tuple-element.38.refs_1_), channel_id=1, source_target_pairs={{0,1},{1,0},{2,3},{3,2},{4,5},{5,4},{6,7},{7,6},{8,9},{9,8},{10,11... | collective-permute-start | bytes 983048 | tf_op jit(solution)/shard_map/ppermute | solution.py:357
  23.0 0.1 collective-permute-start.3
  23.1 1.9 %inverses.2.early_ref = f32[2,20,128,128]{3,2,1,0:T(8,128)S(1)} custom-call(s32[1]{0:T(128)} %bitcast.place_ref.refs_0_, bf16[10,128,128]{2,1,0:T(8,128)(2,1)S(1)} %get-tuple-element.38.refs_1_, bf16[10,128,128]{2,1,0:T(8,128)(2,1)S(1)} %get-tuple-element.37.refs_2_, bf16[20,128,128]{2,1,0:T(8,128)(2,1)S(1)} %convert_element_type.15.refs_3_, ...), custom_call_target="tpu_custom_call" | custom-call | flops 1000000 | bytes 10000 | tf_op jit(solution)/shard_map/inverses/pallas_call | solution.py:361
  25.1 0.0 copy-start
  25.1 0.0 collective-permute-done.2.refs_1_
  25.1 0.0 collective-permute-done.3.refs_2_
  25.1 2.0 %inverses.3.late_ref = f32[2,20,128,128]{3,2,1,0:T(8,128)S(1)} custom-call(s32[1]{0:T(128)} %bitcast.place_ref.refs_0_, bf16[10,128,128]{2,1,0:T(8,128)(2,1)S(1)} %collective-permute-done.2.refs_1_, bf16[10,128,128]{2,1,0:T(8,128)(2,1)S(1)} %collective-permute-done.3.refs_2_, bf16[20,128,128]{2,1,0:T(8,128)(2,1)S(1)} %convert_element_type.15.refs_3_, ...), custom_call_target="tpu_custom_call" | custom-call | flops 1000000 | bytes 10000 | tf_op jit(solution)/shard_map/inverses/pallas_call | solution.py:361
  27.1 0.0 copy-done
  27.1 0.5 %arrange.1 = (bf16[2,20,128,128]{3,2,1,0:T(8,128)(2,1)S(1)}, f32[2,2,10,128,128]{4,3,2,1,0:T(8,128)S(1)}) custom-call(s32[1]{0:T(128)} %bitcast.place_ref.refs_0_, bf16[2,20,128,128]{3,2,1,0:T(8,128)(2,1)S(1)} %copy-done, f32[2,20,128,128]{3,2,1,0:T(8,128)S(1)} %inverses.2.early_ref, f32[2,20,128,128]{3,2,1,0:T(8,128)S(1)} %inverses.3.late_ref), custom_call_target="tpu_custom_call" | custom-call | flops 100000 | bytes 10000 | tf_op jit(solution)/shard_map/arrange/pallas_call | solution.py:371
  27.6 4.4 %collective-permute-done.before_ref = bf16[2,10,128,128]{3,2,1,0:T(8,128)(2,1)S(1)} collective-permute-done((bf16[2,10,128,128]{3,2,1,0:T(8,128)(2,1)}, bf16[2,10,128,128]{3,2,1,0:T(8,128)(2,1)S(1)}, u32[]{:S(2)}, u32[]{:S(2)}) %collective-permute-start) | collective-permute-done | bytes 655392 | tf_op jit(solution)/shard_map/ppermute | solution.py:337
  32.0 0.0 collective-permute-done.4.after_ref
  32.0 3.9 %corrections.1 = (f32[2,21,32,128]{3,2,1,0:T(8,128)S(1)}, f32[21,32,128]{2,1,0:T(8,128)S(1)}, f32[21,32,128]{2,1,0:T(8,128)S(1)}) custom-call(bf16[2,10,128,128]{3,2,1,0:T(8,128)(2,1)S(1)} %collective-permute-done.before_ref, bf16[2,20,128,128]{3,2,1,0:T(8,128)(2,1)S(1)} %get-tuple-element.28.own_ref, ...), custom_call_target="tpu_custom_call" | custom-call | flops 4000000000 | bytes 5000000 | tf_op jit(solution)/shard_map/corrections/pallas_call | solution.py:380
  35.9 0.8 %collective-permute-start.6 = (f32[21,32,128]{2,1,0:T(8,128)S(1)}, f32[21,32,128]{2,1,0:T(8,128)S(1)}, u32[]{:S(2)}, u32[]{:S(2)}) collective-permute-start(f32[21,32,128]{2,1,0:T(8,128)S(1)} %get-tuple-element.33), channel_id=1, source_target_pairs={{0,1},{1,0},{2,3},{3,2},{4,5},{5,4},{6,7},{7,6},{8,9},{9,8},{10,11... | collective-permute-start | bytes 1032200 | tf_op jit(solution)/shard_map/ppermute | solution.py:389
  36.7 0.1 collective-permute-start.5
  36.8 1.2 %collective-permute-done.6 = f32[21,32,128]{2,1,0:T(8,128)S(1)} collective-permute-done((f32[21,32,128]{2,1,0:T(8,128)S(1)}, f32[21,32,128]{2,1,0:T(8,128)S(1)}, u32[]{:S(2)}, u32[]{:S(2)}) %collective-permute-start.6) | collective-permute-done | bytes 344096 | tf_op jit(solution)/shard_map/ppermute | solution.py:389
  38.0 0.1 fusion
  38.0 2.8 %collective-permute-start.7 = (f16[21,32,128]{2,1,0:T(8,128)(2,1)S(1)}, f16[21,32,128]{2,1,0:T(8,128)(2,1)S(1)}, u32[]{:S(2)}, u32[]{:S(2)}) collective-permute-start(f16[21,32,128]{2,1,0:T(8,128)(2,1)S(1)} %fusion), channel_id=1, source_target_pairs={{0,2},{1,3},{2,0},{3,1},{4,6},{5,7},{6,4},{7,5},{8,10},{9,11},{10,... | collective-permute-start | bytes 516104 | tf_op jit(solution)/shard_map/ppermute | solution.py:391
  40.9 0.0 collective-permute-done.5
  40.9 1.1 %fusion.1 = f32[20,32,128]{2,1,0:T(8,128)S(1)} fusion(f32[21,32,128]{2,1,0:T(8,128)S(1)} %collective-permute-done.5, f32[2,21,32,128]{3,2,1,0:T(8,128)S(1)} %get-tuple-element.31, f32[20,128,128]{2,1,0:T(8,128)} %param.3, s32[]{:T(128)S(6)} %select_n.3), kind=kLoop, calls=%fused_computation.3 | loop fusion | flops 163840 | bytes 1310724 | tf_op jit(solution)/shard_map/mul | solution.py:394
  41.9 4.3 %collective-permute-done.7 = f16[21,32,128]{2,1,0:T(8,128)(2,1)S(1)} collective-permute-done((f16[21,32,128]{2,1,0:T(8,128)(2,1)S(1)}, f16[21,32,128]{2,1,0:T(8,128)(2,1)S(1)}, u32[]{:S(2)}, u32[]{:S(2)}) %collective-permute-start.7) | collective-permute-done | bytes 172064 | tf_op jit(solution)/shard_map/ppermute | solution.py:391
  46.3 0.8 %multiply_multiply_fusion = f32[20,32,128]{2,1,0:T(8,128)} fusion(f32[20,32,128]{2,1,0:T(8,128)S(1)} %fusion.1, f32[32,128]{1,0:T(8,128)S(1)} %multiply_multiply_fusion.1, f16[21,32,128]{2,1,0:T(8,128)(2,1)S(1)} %collective-permute-done.7), kind=kLoop, calls=%fused_computation.4 | loop fusion | flops 245760 | bytes 835584 | tf_op jit(solution)/shard_map/mul | solution.py:397
  (3 shorter events, 0.1 us)
Async XLA Ops:
  0.0 16.3 %copy-start.1 = (f32[2,3,2,21]{3,2,1,0:T(2,128)S(1)}, f32[2,3,2,21]{3,2,1,0:T(2,128)}, u32[]{:S(2)}) copy-start(f32[2,3,2,21]{3,2,1,0:T(2,128)} %taps_ref.1) | copy-start | bytes 3028
  1.4 17.4 %collective-permute-start.1 = (bf16[20,128,128]{2,1,0:T(8,128)(2,1)S(1)}, bf16[20,128,128]{2,1,0:T(8,128)(2,1)S(1)}, u32[]{:S(2)}, u32[]{:S(2)}) collective-permute-start(bf16[20,128,128]{2,1,0:T(8,128)(2,1)S(1)} %convert_element_type.15.refs_3_), channel_id=1, source_target_pairs={{0,4},{4,8},{8,12},{12,16},{16,20},{20,24},{24,28},{28,32},{32,36}... | collective-permute-start | bytes 1966088 | tf_op jit(solution)/shard_map/ppermute | solution.py:323
  7.4 24.6 %collective-permute-start = (bf16[2,10,128,128]{3,2,1,0:T(8,128)(2,1)}, bf16[2,10,128,128]{3,2,1,0:T(8,128)(2,1)S(1)}, u32[]{:S(2)}, u32[]{:S(2)}) collective-permute-start(bf16[2,10,128,128]{3,2,1,0:T(8,128)(2,1)} %get-tuple-element.21), channel_id=1, source_target_pairs={{0,4},{4,8},{8,12},{12,16},{16,20},{20,24},{24,28},{28,32},{32,36}... | collective-permute-start | bytes 1966088 | tf_op jit(solution)/shard_map/ppermute | solution.py:337
  11.2 20.8 %collective-permute-start.4 = (bf16[2,10,128,128]{3,2,1,0:T(8,128)(2,1)}, bf16[2,10,128,128]{3,2,1,0:T(8,128)(2,1)S(1)}, u32[]{:S(2)}, u32[]{:S(2)}) collective-permute-start(bf16[2,10,128,128]{3,2,1,0:T(8,128)(2,1)} %get-tuple-element.29), channel_id=1, source_target_pairs={{4,0},{8,4},{12,8},{16,12},{20,16},{24,20},{28,24},{32,28},{36,32}... | collective-permute-start | bytes 1966088 | tf_op jit(solution)/shard_map/ppermute | solution.py:338
  18.9 6.2 %collective-permute-start.2 = (bf16[10,128,128]{2,1,0:T(8,128)(2,1)S(1)}, bf16[10,128,128]{2,1,0:T(8,128)(2,1)S(1)}, u32[]{:S(2)}, u32[]{:S(2)}) collective-permute-start(bf16[10,128,128]{2,1,0:T(8,128)(2,1)S(1)} %get-tuple-element.38.refs_1_), channel_id=1, source_target_pairs={{0,1},{1,0},{2,3},{3,2},{4,5},{5,4},{6,7},{7,6},{8,9},{9,8},{10,11... | collective-permute-start | bytes 983048 | tf_op jit(solution)/shard_map/ppermute | solution.py:357
  23.0 2.1 %collective-permute-start.3 = (bf16[10,128,128]{2,1,0:T(8,128)(2,1)S(1)}, bf16[10,128,128]{2,1,0:T(8,128)(2,1)S(1)}, u32[]{:S(2)}, u32[]{:S(2)}) collective-permute-start(bf16[10,128,128]{2,1,0:T(8,128)(2,1)S(1)} %get-tuple-element.37.refs_2_), channel_id=1, source_target_pairs={{0,1},{1,0},{2,3},{3,2},{4,5},{5,4},{6,7},{7,6},{8,9},{9,8},{10,11... | collective-permute-start | bytes 983048 | tf_op jit(solution)/shard_map/ppermute | solution.py:357
  25.1 2.0 %copy-start = (bf16[2,20,128,128]{3,2,1,0:T(8,128)(2,1)S(1)}, bf16[2,20,128,128]{3,2,1,0:T(8,128)(2,1)}, u32[]{:S(2)}) copy-start(bf16[2,20,128,128]{3,2,1,0:T(8,128)(2,1)} %rec_ref.3) | copy-start | bytes 3932164
  35.9 2.1 %collective-permute-start.6 = (f32[21,32,128]{2,1,0:T(8,128)S(1)}, f32[21,32,128]{2,1,0:T(8,128)S(1)}, u32[]{:S(2)}, u32[]{:S(2)}) collective-permute-start(f32[21,32,128]{2,1,0:T(8,128)S(1)} %get-tuple-element.33), channel_id=1, source_target_pairs={{0,1},{1,0},{2,3},{3,2},{4,5},{5,4},{6,7},{7,6},{8,9},{9,8},{10,11... | collective-permute-start | bytes 1032200 | tf_op jit(solution)/shard_map/ppermute | solution.py:389
  36.7 4.2 %collective-permute-start.5 = (f32[21,32,128]{2,1,0:T(8,128)S(1)}, f32[21,32,128]{2,1,0:T(8,128)S(1)}, u32[]{:S(2)}, u32[]{:S(2)}) collective-permute-start(f32[21,32,128]{2,1,0:T(8,128)S(1)} %get-tuple-element.32), channel_id=1, source_target_pairs={{0,1},{1,0},{2,3},{3,2},{4,5},{5,4},{6,7},{7,6},{8,9},{9,8},{10,11... | collective-permute-start | bytes 1032200 | tf_op jit(solution)/shard_map/ppermute | solution.py:390
  38.0 8.2 %collective-permute-start.7 = (f16[21,32,128]{2,1,0:T(8,128)(2,1)S(1)}, f16[21,32,128]{2,1,0:T(8,128)(2,1)S(1)}, u32[]{:S(2)}, u32[]{:S(2)}) collective-permute-start(f16[21,32,128]{2,1,0:T(8,128)(2,1)S(1)} %fusion), channel_id=1, source_target_pairs={{0,2},{1,3},{2,0},{3,1},{4,6},{5,7},{6,4},{7,5},{8,10},{9,11},{10,... | collective-permute-start | bytes 516104 | tf_op jit(solution)/shard_map/ppermute | solution.py:391

commit v11 on v10

--- a/solution.py
+++ b/solution.py
@@ -143,22 +143,25 @@
     return guess * (2.0 - value * guess)
 
 
-def filter_to(load, views, groups, z_ref, x_ref, y_ref, scale_ref, e_ref, g_ref, exact, emit):
+def filter_to(loads, views, groups, z_ref, x_ref, y_ref, scale_ref, e_ref, g_ref, exact, emit):
     tall = z_ref.shape[0] // (2 * views)
     z_out = tall // 8
     rows = y_ref.shape[1]
-    for pair in range(rows // 16):
-        block = load(slice(pair * 16, pair * 16 + 16))
+    sets = len(loads)
+    for pair, own in [(pair, own) for pair in range(rows // 16) for own in range(sets)]:
+        block = loads[own](slice(pair * 16, pair * 16 + 16))
+        of = range(views) if sets == 1 else range(own, own + 1)
+        top_z, end_z = of.start * 2 * tall, of.stop * 2 * tall
         planes = block.shape[0]
         depth = (planes - (groups - 1) * z_out) * 8
         octets = [block[:, 8 * o : 8 * o + 8, :].reshape(planes * 8, rows).astype(BF16) for o in range(2)]
         octets = jnp.concatenate(octets, axis=1)
         for part in range(groups):
             data = octets[part * z_out * 8 : part * z_out * 8 + depth]
-            all_e = dot(z_ref[:, :depth], data)
-            for v in range(views):
+            all_e = dot(z_ref[top_z:end_z, :depth], data)
+            for v in of:
                 for r in range(2):
-                    top = (2 * v + r) * tall
+                    top = (2 * (v - of.start) + r) * tall
                     e = all_e[top : top + tall]
                     e = jnp.concatenate([e[:, :rows], e[:, rows:]], axis=0)
                     lanes = slice(r * rows, (r + 1) * rows)
@@ -222,7 +225,7 @@
         out_ref[v, z] = inverted(blurred)
 
     views = out_ref.shape[0]
-    filter_to(load, views, 2, z_ref.at[0], x_ref.at[0], y_ref.at[0], scale_ref, e_ref, g_ref, False, emit)
+    filter_to([load], views, 2, z_ref.at[0], x_ref.at[0], y_ref.at[0], scale_ref, e_ref, g_ref, False, emit)
 
 
 def arrange_kernel(place_ref, rec_ref, early_ref, late_ref, own_out, rim_out):
@@ -259,37 +262,23 @@
 ):
     views, planes = own_ref.shape[:2]
     part = keep_ref.shape[2]
-    tall = z_ref.shape[1] // views
     most = [jnp.zeros((8, product_ref.shape[2]), F32)]
-    for v in range(views):
-
-        def load(at, v=v):
-            before = before_ref[v, :, at, :].astype(F32) * rim_ref[v, 0, :, at, :]
-            after = after_ref[v, :, at, :].astype(F32) * rim_ref[v, 1, :, at, :]
-            return jnp.concatenate([before, own_ref[v, :, at, :].astype(F32), after], axis=0)
-
-        def emit(_, z, value, v=v):
-            if v > 0:
-                value = value * product_ref[z]
-            product_ref[z] = value
-            if v == views - 1:
-                for top in range(0, value.shape[0], 8):
-                    most[0] = jnp.maximum(most[0], value[top : top + 8])
-
-        z_view = z_ref.at[1, v * tall : (v + 1) * tall]
-        filter_to(
-            load,
-            1,
-            2,
-            z_view,
-            x_ref.at[1, v : v + 1],
-            y_ref.at[1, v : v + 1],
-            scale_ref.at[v : v + 1],
-            e_ref,
-            g_ref,
-            True,
-            emit,
-        )
+
+    def load(at, v):
+        before = before_ref[v, :, at, :].astype(F32) * rim_ref[v, 0, :, at, :]
+        after = after_ref[v, :, at, :].astype(F32) * rim_ref[v, 1, :, at, :]
+        return jnp.concatenate([before, own_ref[v, :, at, :].astype(F32), after], axis=0)
+
+    def emit(v, z, value):
+        if v > 0:
+            value = value * product_ref[z]
+        product_ref[z] = value
+        if v == views - 1:
+            for top in range(0, value.shape[0], 8):
+                most[0] = jnp.maximum(most[0], value[top : top + 8])
+
+    loads = [lambda at, v=v: load(at, v) for v in range(views)]
+    filter_to(loads, views, 2, z_ref.at[1], x_ref.at[1], y_ref.at[1], scale_ref, e_ref, g_ref, True, emit)
     top = jnp.maximum(jnp.max(most[0], axis=(0, 1), keepdims=True), 1e-30)
     quarter = jnp.ceil(jnp.log2(top) * 0.25)
     scale = jnp.exp2(-4.0 * quarter)
@@ -382,7 +371,7 @@
         out_shape=[shape((2, planes + 1, part, cols), F32)] + [shape((planes + 1, part, cols), F32)] * 2,
         in_specs=[VMEM] * 8,
         out_specs=[VMEM] * 3,
-        scratch_shapes=scratch(1, 2, 2, z_out, rows, cols) + [pltpu.VMEM((planes, rows, cols), F32)],
+        scratch_shapes=scratch(views, 2, 2, z_out, rows, cols) + [pltpu.VMEM((planes, rows, cols), F32)],
         name="corrections",
         **params(4 * 10**9, 5 * 10**6),
     )(before, own, after, rim, z_mat, x_mat, y_mat, scales)

time: 47.3 us -> 47.2 us (level)
  no operation moved by 1% of the time
where the time goes in v11:
time: 47.2 us; the launch traced here: 46.9 us
  starting transfers between devices  20.7 us (44%)
  Pallas kernels  12.8 us (27%)
  waiting for transfers between devices  9.93 us (21%)
  other arithmetic  3.33 us (7%)
    ppermute x1, starting transfers between devices, local(): after = lax.ppermute(first, 'gz', down)  5.06 us
    ppermute x1, waiting for transfers between devices, local(): before = lax.ppermute(last, 'gz', up)  4.39 us
    ppermute x1, waiting for transfers between devices, local(): lax.ppermute((keep[1] * core_far).astype(jnp.float16), 'view', [(i, i ^ 2...  4.34 us
    ppermute x2, starting transfers between devices, local(): other = [lax.ppermute(piece, 'view', swap) for piece in mine]  4.19 us
    pallas_call x2, Pallas kernels, local(): pl.pallas_call(lambda *refs, early=early: inverse_kernel(early, *refs), o...  3.9 us
    ppermute x1, starting transfers between devices, local(): mine = lax.ppermute(rounded, ('gz', 'view'), both_ways)  3.83 us
    ppermute x1, starting transfers between devices, local(): before = lax.ppermute(last, 'gz', up)  3.83 us
    pallas_call x1, Pallas kernels, local(): pl.pallas_call(correction_kernel, out_shape=[shape((2, planes + 1, part,...  3.71 us
  transfers between devices with their start and end apart: 8, of which 3 were waited for; matrix products, arithmetic and copies ran while one was open for 2% of the time, Pallas kernels for 19%

profile of v11, /device:TPU:24, one launch (start us, length us, event | category | flops | bytes accessed | tf_op | source)
XLA Modules:
  0.0 46.9 jit_solution(15502660409011093699)
XLA Ops:
  0.0 0.0 copy-start.1
  0.0 1.4 %convert_element_type.15.refs_3_ = bf16[20,128,128]{2,1,0:T(8,128)(2,1)S(1)} convert(f32[20,128,128]{2,1,0:T(8,128)} %param.3) | non-fusion elementwise | flops 327680 | bytes 1966080 | tf_op jit(solution)/shard_map/convert_element_type | solution.py:309
  1.4 3.8 %collective-permute-start.1 = (bf16[20,128,128]{2,1,0:T(8,128)(2,1)S(1)}, bf16[20,128,128]{2,1,0:T(8,128)(2,1)S(1)}, u32[]{:S(2)}, u32[]{:S(2)}) collective-permute-start(bf16[20,128,128]{2,1,0:T(8,128)(2,1)S(1)} %convert_element_type.15.refs_3_), channel_id=1, source_target_pairs={{0,4},{4,8},{8,12},{12,16},{16,20},{20,24},{24,28},{28,32},{32,36}... | collective-permute-start | bytes 1966088 | tf_op jit(solution)/shard_map/ppermute | solution.py:312
  5.3 2.1 %edges.1 = (bf16[2,10,128,128]{3,2,1,0:T(8,128)(2,1)}, bf16[2,10,128,128]{3,2,1,0:T(8,128)(2,1)}) custom-call(bf16[2,20,128,128]{3,2,1,0:T(8,128)(2,1)} %rec_ref.3), custom_call_target="tpu_custom_call" | custom-call | flops 10000 | bytes 10000 | tf_op jit(solution)/shard_map/edges/pallas_call | solution.py:314
  7.4 3.8 %collective-permute-start = (bf16[2,10,128,128]{3,2,1,0:T(8,128)(2,1)}, bf16[2,10,128,128]{3,2,1,0:T(8,128)(2,1)S(1)}, u32[]{:S(2)}, u32[]{:S(2)}) collective-permute-start(bf16[2,10,128,128]{3,2,1,0:T(8,128)(2,1)} %get-tuple-element.21), channel_id=1, source_target_pairs={{0,4},{4,8},{8,12},{12,16},{16,20},{20,24},{24,28},{28,32},{32,36}... | collective-permute-start | bytes 1966088 | tf_op jit(solution)/shard_map/ppermute | solution.py:326
  11.2 5.1 %collective-permute-start.4 = (bf16[2,10,128,128]{3,2,1,0:T(8,128)(2,1)}, bf16[2,10,128,128]{3,2,1,0:T(8,128)(2,1)S(1)}, u32[]{:S(2)}, u32[]{:S(2)}) collective-permute-start(bf16[2,10,128,128]{3,2,1,0:T(8,128)(2,1)} %get-tuple-element.29), channel_id=1, source_target_pairs={{4,0},{8,4},{12,8},{16,12},{20,16},{24,20},{28,24},{32,28},{36,32}... | collective-permute-start | bytes 1966088 | tf_op jit(solution)/shard_map/ppermute | solution.py:327
  16.3 0.0 copy-done.1
  16.3 2.5 %matrices.1 = (bf16[2,320,256]{2,1,0:T(8,128)(2,1)S(1)}, bf16[2,2,256,256]{3,2,1,0:T(8,128)(2,1)S(1)}, bf16[2,2,128,256]{3,2,1,0:T(8,128)(2,1)S(1)}, f32[2,2,1,128]{3,2,1,0:T(1,128)S(1)}) custom-call(s32[1]{0:T(128)} %bitcast.place_ref.refs_0_, f32[2,3,2,21]{3,2,1,0:T(2,128)S(1)} %copy-done.1), custom_call_target="tpu_custom_call" | custom-call | flops 1000000 | bytes 10000 | tf_op jit(solution)/shard_map/matrices/pallas_call | solution.py:330
  18.9 0.0 collective-permute-done.1
  18.9 4.1 %collective-permute-start.2 = (bf16[10,128,128]{2,1,0:T(8,128)(2,1)S(1)}, bf16[10,128,128]{2,1,0:T(8,128)(2,1)S(1)}, u32[]{:S(2)}, u32[]{:S(2)}) collective-permute-start(bf16[10,128,128]{2,1,0:T(8,128)(2,1)S(1)} %get-tuple-element.38.refs_1_), channel_id=1, source_target_pairs={{0,1},{1,0},{2,3},{3,2},{4,5},{5,4},{6,7},{7,6},{8,9},{9,8},{10,11... | collective-permute-start | bytes 983048 | tf_op jit(solution)/shard_map/ppermute | solution.py:346
  23.0 0.1 collective-permute-start.3
  23.1 1.9 %inverses.2.early_ref = f32[2,20,128,128]{3,2,1,0:T(8,128)S(1)} custom-call(s32[1]{0:T(128)} %bitcast.place_ref.refs_0_, bf16[10,128,128]{2,1,0:T(8,128)(2,1)S(1)} %get-tuple-element.38.refs_1_, bf16[10,128,128]{2,1,0:T(8,128)(2,1)S(1)} %get-tuple-element.37.refs_2_, bf16[20,128,128]{2,1,0:T(8,128)(2,1)S(1)} %convert_element_type.15.refs_3_, ...), custom_call_target="tpu_custom_call" | custom-call | flops 1000000 | bytes 10000 | tf_op jit(solution)/shard_map/inverses/pallas_call | solution.py:350
  25.1 0.0 copy-start
  25.1 0.0 collective-permute-done.2.refs_1_
  25.1 0.0 collective-permute-done.3.refs_2_
  25.1 2.0 %inverses.3.late_ref = f32[2,20,128,128]{3,2,1,0:T(8,128)S(1)} custom-call(s32[1]{0:T(128)} %bitcast.place_ref.refs_0_, bf16[10,128,128]{2,1,0:T(8,128)(2,1)S(1)} %collective-permute-done.2.refs_1_, bf16[10,128,128]{2,1,0:T(8,128)(2,1)S(1)} %collective-permute-done.3.refs_2_, bf16[20,128,128]{2,1,0:T(8,128)(2,1)S(1)} %convert_element_type.15.refs_3_, ...), custom_call_target="tpu_custom_call" | custom-call | flops 1000000 | bytes 10000 | tf_op jit(solution)/shard_map/inverses/pallas_call | solution.py:350
  27.1 0.0 copy-done
  27.1 0.5 %arrange.1 = (bf16[2,20,128,128]{3,2,1,0:T(8,128)(2,1)S(1)}, f32[2,2,10,128,128]{4,3,2,1,0:T(8,128)S(1)}) custom-call(s32[1]{0:T(128)} %bitcast.place_ref.refs_0_, bf16[2,20,128,128]{3,2,1,0:T(8,128)(2,1)S(1)} %copy-done, f32[2,20,128,128]{3,2,1,0:T(8,128)S(1)} %inverses.2.early_ref, f32[2,20,128,128]{3,2,1,0:T(8,128)S(1)} %inverses.3.late_ref), custom_call_target="tpu_custom_call" | custom-call | flops 100000 | bytes 10000 | tf_op jit(solution)/shard_map/arrange/pallas_call | solution.py:360
  27.6 4.4 %collective-permute-done.before_ref = bf16[2,10,128,128]{3,2,1,0:T(8,128)(2,1)S(1)} collective-permute-done((bf16[2,10,128,128]{3,2,1,0:T(8,128)(2,1)}, bf16[2,10,128,128]{3,2,1,0:T(8,128)(2,1)S(1)}, u32[]{:S(2)}, u32[]{:S(2)}) %collective-permute-start) | collective-permute-done | bytes 655392 | tf_op jit(solution)/shard_map/ppermute | solution.py:326
  32.0 0.0 collective-permute-done.4.after_ref
  32.0 3.7 %corrections.1 = (f32[2,21,32,128]{3,2,1,0:T(8,128)S(1)}, f32[21,32,128]{2,1,0:T(8,128)S(1)}, f32[21,32,128]{2,1,0:T(8,128)S(1)}) custom-call(bf16[2,10,128,128]{3,2,1,0:T(8,128)(2,1)S(1)} %collective-permute-done.before_ref, bf16[2,20,128,128]{3,2,1,0:T(8,128)(2,1)S(1)} %get-tuple-element.28.own_ref, ...), custom_call_target="tpu_custom_call" | custom-call | flops 4000000000 | bytes 5000000 | tf_op jit(solution)/shard_map/corrections/pallas_call | solution.py:369
  35.7 0.8 %collective-permute-start.6 = (f32[21,32,128]{2,1,0:T(8,128)S(1)}, f32[21,32,128]{2,1,0:T(8,128)S(1)}, u32[]{:S(2)}, u32[]{:S(2)}) collective-permute-start(f32[21,32,128]{2,1,0:T(8,128)S(1)} %get-tuple-element.33), channel_id=1, source_target_pairs={{0,1},{1,0},{2,3},{3,2},{4,5},{5,4},{6,7},{7,6},{8,9},{9,8},{10,11... | collective-permute-start | bytes 1032200 | tf_op jit(solution)/shard_map/ppermute | solution.py:378
  36.5 0.1 collective-permute-start.5
  36.6 1.2 %collective-permute-done.6 = f32[21,32,128]{2,1,0:T(8,128)S(1)} collective-permute-done((f32[21,32,128]{2,1,0:T(8,128)S(1)}, f32[21,32,128]{2,1,0:T(8,128)S(1)}, u32[]{:S(2)}, u32[]{:S(2)}) %collective-permute-start.6) | collective-permute-done | bytes 344096 | tf_op jit(solution)/shard_map/ppermute | solution.py:378
  37.8 0.1 fusion
  37.9 2.8 %collective-permute-start.7 = (f16[21,32,128]{2,1,0:T(8,128)(2,1)S(1)}, f16[21,32,128]{2,1,0:T(8,128)(2,1)S(1)}, u32[]{:S(2)}, u32[]{:S(2)}) collective-permute-start(f16[21,32,128]{2,1,0:T(8,128)(2,1)S(1)} %fusion), channel_id=1, source_target_pairs={{0,2},{1,3},{2,0},{3,1},{4,6},{5,7},{6,4},{7,5},{8,10},{9,11},{10,... | collective-permute-start | bytes 516104 | tf_op jit(solution)/shard_map/ppermute | solution.py:380
  40.7 0.0 collective-permute-done.5
  40.7 1.1 %fusion.1 = f32[20,32,128]{2,1,0:T(8,128)S(1)} fusion(f32[21,32,128]{2,1,0:T(8,128)S(1)} %collective-permute-done.5, f32[2,21,32,128]{3,2,1,0:T(8,128)S(1)} %get-tuple-element.31, f32[20,128,128]{2,1,0:T(8,128)} %param.3, s32[]{:T(128)S(6)} %select_n.3), kind=kLoop, calls=%fused_computation.3 | loop fusion | flops 163840 | bytes 1310724 | tf_op jit(solution)/shard_map/mul | solution.py:383
  41.8 4.3 %collective-permute-done.7 = f16[21,32,128]{2,1,0:T(8,128)(2,1)S(1)} collective-permute-done((f16[21,32,128]{2,1,0:T(8,128)(2,1)S(1)}, f16[21,32,128]{2,1,0:T(8,128)(2,1)S(1)}, u32[]{:S(2)}, u32[]{:S(2)}) %collective-permute-start.7) | collective-permute-done | bytes 172064 | tf_op jit(solution)/shard_map/ppermute | solution.py:380
  46.1 0.8 %multiply_multiply_fusion = f32[20,32,128]{2,1,0:T(8,128)} fusion(f32[20,32,128]{2,1,0:T(8,128)S(1)} %fusion.1, f32[32,128]{1,0:T(8,128)S(1)} %multiply_multiply_fusion.1, f16[21,32,128]{2,1,0:T(8,128)(2,1)S(1)} %collective-permute-done.7), kind=kLoop, calls=%fused_computation.4 | loop fusion | flops 245760 | bytes 835584 | tf_op jit(solution)/shard_map/mul | solution.py:386
  (3 shorter events, 0.1 us)
Async XLA Ops:
  0.0 16.3 %copy-start.1 = (f32[2,3,2,21]{3,2,1,0:T(2,128)S(1)}, f32[2,3,2,21]{3,2,1,0:T(2,128)}, u32[]{:S(2)}) copy-start(f32[2,3,2,21]{3,2,1,0:T(2,128)} %taps_ref.1) | copy-start | bytes 3028
  1.4 17.4 %collective-permute-start.1 = (bf16[20,128,128]{2,1,0:T(8,128)(2,1)S(1)}, bf16[20,128,128]{2,1,0:T(8,128)(2,1)S(1)}, u32[]{:S(2)}, u32[]{:S(2)}) collective-permute-start(bf16[20,128,128]{2,1,0:T(8,128)(2,1)S(1)} %convert_element_type.15.refs_3_), channel_id=1, source_target_pairs={{0,4},{4,8},{8,12},{12,16},{16,20},{20,24},{24,28},{28,32},{32,36}... | collective-permute-start | bytes 1966088 | tf_op jit(solution)/shard_map/ppermute | solution.py:312
  7.4 24.6 %collective-permute-start = (bf16[2,10,128,128]{3,2,1,0:T(8,128)(2,1)}, bf16[2,10,128,128]{3,2,1,0:T(8,128)(2,1)S(1)}, u32[]{:S(2)}, u32[]{:S(2)}) collective-permute-start(bf16[2,10,128,128]{3,2,1,0:T(8,128)(2,1)} %get-tuple-element.21), channel_id=1, source_target_pairs={{0,4},{4,8},{8,12},{12,16},{16,20},{20,24},{24,28},{28,32},{32,36}... | collective-permute-start | bytes 1966088 | tf_op jit(solution)/shard_map/ppermute | solution.py:326
  11.2 20.8 %collective-permute-start.4 = (bf16[2,10,128,128]{3,2,1,0:T(8,128)(2,1)}, bf16[2,10,128,128]{3,2,1,0:T(8,128)(2,1)S(1)}, u32[]{:S(2)}, u32[]{:S(2)}) collective-permute-start(bf16[2,10,128,128]{3,2,1,0:T(8,128)(2,1)} %get-tuple-element.29), channel_id=1, source_target_pairs={{4,0},{8,4},{12,8},{16,12},{20,16},{24,20},{28,24},{32,28},{36,32}... | collective-permute-start | bytes 1966088 | tf_op jit(solution)/shard_map/ppermute | solution.py:327
  18.9 6.2 %collective-permute-start.2 = (bf16[10,128,128]{2,1,0:T(8,128)(2,1)S(1)}, bf16[10,128,128]{2,1,0:T(8,128)(2,1)S(1)}, u32[]{:S(2)}, u32[]{:S(2)}) collective-permute-start(bf16[10,128,128]{2,1,0:T(8,128)(2,1)S(1)} %get-tuple-element.38.refs_1_), channel_id=1, source_target_pairs={{0,1},{1,0},{2,3},{3,2},{4,5},{5,4},{6,7},{7,6},{8,9},{9,8},{10,11... | collective-permute-start | bytes 983048 | tf_op jit(solution)/shard_map/ppermute | solution.py:346
  23.0 2.1 %collective-permute-start.3 = (bf16[10,128,128]{2,1,0:T(8,128)(2,1)S(1)}, bf16[10,128,128]{2,1,0:T(8,128)(2,1)S(1)}, u32[]{:S(2)}, u32[]{:S(2)}) collective-permute-start(bf16[10,128,128]{2,1,0:T(8,128)(2,1)S(1)} %get-tuple-element.37.refs_2_), channel_id=1, source_target_pairs={{0,1},{1,0},{2,3},{3,2},{4,5},{5,4},{6,7},{7,6},{8,9},{9,8},{10,11... | collective-permute-start | bytes 983048 | tf_op jit(solution)/shard_map/ppermute | solution.py:346
  25.1 2.0 %copy-start = (bf16[2,20,128,128]{3,2,1,0:T(8,128)(2,1)S(1)}, bf16[2,20,128,128]{3,2,1,0:T(8,128)(2,1)}, u32[]{:S(2)}) copy-start(bf16[2,20,128,128]{3,2,1,0:T(8,128)(2,1)} %rec_ref.3) | copy-start | bytes 3932164
  35.7 2.1 %collective-permute-start.6 = (f32[21,32,128]{2,1,0:T(8,128)S(1)}, f32[21,32,128]{2,1,0:T(8,128)S(1)}, u32[]{:S(2)}, u32[]{:S(2)}) collective-permute-start(f32[21,32,128]{2,1,0:T(8,128)S(1)} %get-tuple-element.33), channel_id=1, source_target_pairs={{0,1},{1,0},{2,3},{3,2},{4,5},{5,4},{6,7},{7,6},{8,9},{9,8},{10,11... | collective-permute-start | bytes 1032200 | tf_op jit(solution)/shard_map/ppermute | solution.py:378
  36.5 4.2 %collective-permute-start.5 = (f32[21,32,128]{2,1,0:T(8,128)S(1)}, f32[21,32,128]{2,1,0:T(8,128)S(1)}, u32[]{:S(2)}, u32[]{:S(2)}) collective-permute-start(f32[21,32,128]{2,1,0:T(8,128)S(1)} %get-tuple-element.32), channel_id=1, source_target_pairs={{0,1},{1,0},{2,3},{3,2},{4,5},{5,4},{6,7},{7,6},{8,9},{9,8},{10,11... | collective-permute-start | bytes 1032200 | tf_op jit(solution)/shard_map/ppermute | solution.py:379
  37.9 8.2 %collective-permute-start.7 = (f16[21,32,128]{2,1,0:T(8,128)(2,1)S(1)}, f16[21,32,128]{2,1,0:T(8,128)(2,1)S(1)}, u32[]{:S(2)}, u32[]{:S(2)}) collective-permute-start(f16[21,32,128]{2,1,0:T(8,128)(2,1)S(1)} %fusion), channel_id=1, source_target_pairs={{0,2},{1,3},{2,0},{3,1},{4,6},{5,7},{6,4},{7,5},{8,10},{9,11},{10,... | collective-permute-start | bytes 516104 | tf_op jit(solution)/shard_map/ppermute | solution.py:380

commit v12 on v11

--- a/solution.py
+++ b/solution.py
@@ -43,23 +43,23 @@
         out.wait()
 
 
-def rounded_scale(tap, total):
+def rounded_scales(taps, totals):
     factor = jnp.exp2(lax.broadcasted_iota(jnp.int32, (1, 128), 1).astype(F32) * (1.0 / 128.0))
-    scale = factor / jnp.full((1, 128), total, F32)
-    sums, running = [], jnp.zeros((1, 128), F32)
-    for value in tap:
-        exact = value * scale
-        running = running + (exact.astype(BF16).astype(F32) - exact)
-        sums.append(running)
+    scales = [factor / jnp.full((1, 128), total, F32) for total in totals]
     error = jnp.zeros((1, 128), F32)
-    for partial in sums:
-        rest = running - partial
-        error = error + partial * partial + rest * rest
+    for tap, scale in zip(taps, scales):
+        sums, running = [], jnp.zeros((1, 128), F32)
+        for value in tap:
+            exact = value * scale
+            running = running + (exact.astype(BF16).astype(F32) - exact)
+            sums.append(running)
+        for partial in sums:
+            rest = running - partial
+            error = error + partial * partial + rest * rest
     error = error / (factor * factor)
     best = error == jnp.min(error, axis=1, keepdims=True)
-    factor = jnp.max(jnp.where(best, factor, 0.0), axis=1, keepdims=True)
-    scale = jnp.max(jnp.where(best, scale, 0.0), axis=1, keepdims=True)
-    return jnp.broadcast_to(scale, (1, 128)), jnp.broadcast_to(factor, (1, 128))
+    chosen = [jnp.max(jnp.where(best, row, 0.0), axis=1, keepdims=True) for row in scales + [factor]]
+    return [jnp.broadcast_to(row, (1, 128)) for row in chosen]
 
 
 def matrices_kernel(place_ref, taps_ref, z_ref, x_ref, y_ref, scale_ref):
@@ -74,16 +74,18 @@
             (d, r): [taps_ref[v, d, r, j] for j in range(taps)] for d in range(3) for r in range(2)
         }
         scale = {}
-        for r in range(2):
-            undo = jnp.ones((1, 128), F32)
-            for d in range(3):
+        undo = jnp.ones((1, 128), F32)
+        for d in range(3):
+            totals = []
+            for r in range(2):
                 values = tap[d, r] if d < 2 else tap[2, 0] + tap[2, 1]
                 total = values[0]
                 for value in values[1:]:
                     total = total + value
-                scale[d, r], factor = rounded_scale(tap[d, r], total)
-                undo = undo / factor
-            scale_ref[v, r] = undo
+                totals.append(total)
+            scale[d, 0], scale[d, 1], factor = rounded_scales([tap[d, 0], tap[d, 1]], totals)
+            undo = undo / factor
+        scale_ref[v] = undo
         for direction in range(2):
             for r in range(2):
                 other = 1 - r
@@ -186,7 +188,6 @@
                     g_rows = jnp.concatenate(
                         [g[o * tall : (o + 1) * tall, lanes].reshape(z_out, 8, rows) for o in range(2)], axis=1
                     )
-                    g_rows = g_rows * scale_ref[v, r]
                     target = slice(r * rows + pair * 16, r * rows + pair * 16 + 16)
                     planes_at = slice(part * z_out, (part + 1) * z_out)
                     if exact:
@@ -202,8 +203,8 @@
             if exact:
                 data = jnp.concatenate([g_ref[v, 1, z], g_ref[v, 1, z + 1]], axis=1)
                 out = out + dot(y_ref[v], data)
-            emit(v, z, out[:, :rows])
-            emit(v, z + 1, out[:, rows:])
+            emit(v, z, out[:, :rows] * scale_ref[v])
+            emit(v, z + 1, out[:, rows:] * scale_ref[v])
 
 
 def scratch(views, groups, halves, z_out, rows, cols):
@@ -333,7 +334,7 @@
             shape((2, views * 2 * z_out * 8, wide), BF16),
             shape((2, views, 2 * cols, 2 * cols), BF16),
             shape((2, views, rows, 2 * rows), BF16),
-            shape((views, 2, 1, 128), F32),
+            shape((views, 1, 128), F32),
         ],
         in_specs=[SMEM, SMEM],
         out_specs=[VMEM] * 4,

time: 47.2 us -> 47.2 us (level)
  transfers between devices with their start and end apart: 8 -> 8, of which waited for: 3 -> 3; matrix products, arithmetic and copies ran while one was open for 2% -> 2% of each run, Pallas kernels for 19% -> 20%
where the time goes in v12:
time: 47.2 us; the launch traced here: 46.9 us
  starting transfers between devices  20.7 us (44%)
  Pallas kernels  13 us (28%)
  waiting for transfers between devices  9.71 us (21%)
  other arithmetic  3.33 us (7%)
    ppermute x1, starting transfers between devices, local(): after = lax.ppermute(first, 'gz', down)  5.06 us
    ppermute x1, waiting for transfers between devices, local(): lax.ppermute((keep[1] * core_far).astype(jnp.float16), 'view', [(i, i ^ 2...  4.34 us
    ppermute x2, starting transfers between devices, local(): other = [lax.ppermute(piece, 'view', swap) for piece in mine]  4.19 us
    ppermute x1, waiting for transfers between devices, local(): before = lax.ppermute(last, 'gz', up)  4.17 us
    pallas_call x2, Pallas kernels, local(): pl.pallas_call(lambda *refs, early=early: inverse_kernel(early, *refs), o...  4.1 us
    ppermute x1, starting transfers between devices, local(): mine = lax.ppermute(rounded, ('gz', 'view'), both_ways)  3.83 us
    ppermute x1, starting transfers between devices, local(): before = lax.ppermute(last, 'gz', up)  3.83 us
    pallas_call x1, Pallas kernels, local(): pl.pallas_call(correction_kernel, out_shape=[shape((2, planes + 1, part,...  3.72 us
  transfers between devices with their start and end apart: 8, of which 3 were waited for; matrix products, arithmetic and copies ran while one was open for 2% of the time, Pallas kernels for 20%

profile of v12, /device:TPU:24, one launch (start us, length us, event | category | flops | bytes accessed | tf_op | source)
XLA Modules:
  0.0 46.9 jit_solution(10910607851336677820)
XLA Ops:
  0.0 0.0 copy-start.1
  0.0 1.4 %convert_element_type.15.refs_3_ = bf16[20,128,128]{2,1,0:T(8,128)(2,1)S(1)} convert(f32[20,128,128]{2,1,0:T(8,128)} %param.3) | non-fusion elementwise | flops 327680 | bytes 1966080 | tf_op jit(solution)/shard_map/convert_element_type | solution.py:310
  1.4 3.8 %collective-permute-start.1 = (bf16[20,128,128]{2,1,0:T(8,128)(2,1)S(1)}, bf16[20,128,128]{2,1,0:T(8,128)(2,1)S(1)}, u32[]{:S(2)}, u32[]{:S(2)}) collective-permute-start(bf16[20,128,128]{2,1,0:T(8,128)(2,1)S(1)} %convert_element_type.15.refs_3_), channel_id=1, source_target_pairs={{0,4},{4,8},{8,12},{12,16},{16,20},{20,24},{24,28},{28,32},{32,36}... | collective-permute-start | bytes 1966088 | tf_op jit(solution)/shard_map/ppermute | solution.py:313
  5.3 2.1 %edges.1 = (bf16[2,10,128,128]{3,2,1,0:T(8,128)(2,1)}, bf16[2,10,128,128]{3,2,1,0:T(8,128)(2,1)}) custom-call(bf16[2,20,128,128]{3,2,1,0:T(8,128)(2,1)} %rec_ref.3), custom_call_target="tpu_custom_call" | custom-call | flops 10000 | bytes 10000 | tf_op jit(solution)/shard_map/edges/pallas_call | solution.py:315
  7.4 3.8 %collective-permute-start = (bf16[2,10,128,128]{3,2,1,0:T(8,128)(2,1)}, bf16[2,10,128,128]{3,2,1,0:T(8,128)(2,1)S(1)}, u32[]{:S(2)}, u32[]{:S(2)}) collective-permute-start(bf16[2,10,128,128]{3,2,1,0:T(8,128)(2,1)} %get-tuple-element.21), channel_id=1, source_target_pairs={{0,4},{4,8},{8,12},{12,16},{16,20},{20,24},{24,28},{28,32},{32,36}... | collective-permute-start | bytes 1966088 | tf_op jit(solution)/shard_map/ppermute | solution.py:327
  11.2 5.1 %collective-permute-start.4 = (bf16[2,10,128,128]{3,2,1,0:T(8,128)(2,1)}, bf16[2,10,128,128]{3,2,1,0:T(8,128)(2,1)S(1)}, u32[]{:S(2)}, u32[]{:S(2)}) collective-permute-start(bf16[2,10,128,128]{3,2,1,0:T(8,128)(2,1)} %get-tuple-element.29), channel_id=1, source_target_pairs={{4,0},{8,4},{12,8},{16,12},{20,16},{24,20},{28,24},{32,28},{36,32}... | collective-permute-start | bytes 1966088 | tf_op jit(solution)/shard_map/ppermute | solution.py:328
  16.3 0.0 copy-done.1
  16.3 2.6 %matrices.1 = (bf16[2,320,256]{2,1,0:T(8,128)(2,1)S(1)}, bf16[2,2,256,256]{3,2,1,0:T(8,128)(2,1)S(1)}, bf16[2,2,128,256]{3,2,1,0:T(8,128)(2,1)S(1)}, f32[2,1,128]{2,1,0:T(1,128)S(1)}) custom-call(s32[1]{0:T(128)} %bitcast.place_ref.refs_0_, f32[2,3,2,21]{3,2,1,0:T(2,128)S(1)} %copy-done.1), custom_call_target="tpu_custom_call" | custom-call | flops 1000000 | bytes 10000 | tf_op jit(solution)/shard_map/matrices/pallas_call | solution.py:331
  18.9 0.0 collective-permute-done.1
  19.0 4.1 %collective-permute-start.2 = (bf16[10,128,128]{2,1,0:T(8,128)(2,1)S(1)}, bf16[10,128,128]{2,1,0:T(8,128)(2,1)S(1)}, u32[]{:S(2)}, u32[]{:S(2)}) collective-permute-start(bf16[10,128,128]{2,1,0:T(8,128)(2,1)S(1)} %get-tuple-element.38.refs_1_), channel_id=1, source_target_pairs={{0,1},{1,0},{2,3},{3,2},{4,5},{5,4},{6,7},{7,6},{8,9},{9,8},{10,11... | collective-permute-start | bytes 983048 | tf_op jit(solution)/shard_map/ppermute | solution.py:347
  23.1 0.1 collective-permute-start.3
  23.2 2.0 %inverses.2.early_ref = f32[2,20,128,128]{3,2,1,0:T(8,128)S(1)} custom-call(s32[1]{0:T(128)} %bitcast.place_ref.refs_0_, bf16[10,128,128]{2,1,0:T(8,128)(2,1)S(1)} %get-tuple-element.38.refs_1_, bf16[10,128,128]{2,1,0:T(8,128)(2,1)S(1)} %get-tuple-element.37.refs_2_, bf16[20,128,128]{2,1,0:T(8,128)(2,1)S(1)} %convert_element_type.15.refs_3_, ...), custom_call_target="tpu_custom_call" | custom-call | flops 1000000 | bytes 10000 | tf_op jit(solution)/shard_map/inverses/pallas_call | solution.py:351
  25.2 0.0 copy-start
  25.2 0.0 collective-permute-done.2.refs_1_
  25.2 0.0 collective-permute-done.3.refs_2_
  25.2 2.0 %inverses.3.late_ref = f32[2,20,128,128]{3,2,1,0:T(8,128)S(1)} custom-call(s32[1]{0:T(128)} %bitcast.place_ref.refs_0_, bf16[10,128,128]{2,1,0:T(8,128)(2,1)S(1)} %collective-permute-done.2.refs_1_, bf16[10,128,128]{2,1,0:T(8,128)(2,1)S(1)} %collective-permute-done.3.refs_2_, bf16[20,128,128]{2,1,0:T(8,128)(2,1)S(1)} %convert_element_type.15.refs_3_, ...), custom_call_target="tpu_custom_call" | custom-call | flops 1000000 | bytes 10000 | tf_op jit(solution)/shard_map/inverses/pallas_call | solution.py:351
  27.3 0.0 copy-done
  27.3 0.5 %arrange.1 = (bf16[2,20,128,128]{3,2,1,0:T(8,128)(2,1)S(1)}, f32[2,2,10,128,128]{4,3,2,1,0:T(8,128)S(1)}) custom-call(s32[1]{0:T(128)} %bitcast.place_ref.refs_0_, bf16[2,20,128,128]{3,2,1,0:T(8,128)(2,1)S(1)} %copy-done, f32[2,20,128,128]{3,2,1,0:T(8,128)S(1)} %inverses.2.early_ref, f32[2,20,128,128]{3,2,1,0:T(8,128)S(1)} %inverses.3.late_ref), custom_call_target="tpu_custom_call" | custom-call | flops 100000 | bytes 10000 | tf_op jit(solution)/shard_map/arrange/pallas_call | solution.py:361
  27.8 4.2 %collective-permute-done.before_ref = bf16[2,10,128,128]{3,2,1,0:T(8,128)(2,1)S(1)} collective-permute-done((bf16[2,10,128,128]{3,2,1,0:T(8,128)(2,1)}, bf16[2,10,128,128]{3,2,1,0:T(8,128)(2,1)S(1)}, u32[]{:S(2)}, u32[]{:S(2)}) %collective-permute-start) | collective-permute-done | bytes 655392 | tf_op jit(solution)/shard_map/ppermute | solution.py:327
  32.0 0.0 collective-permute-done.4.after_ref
  32.0 3.7 %corrections.1 = (f32[2,21,32,128]{3,2,1,0:T(8,128)S(1)}, f32[21,32,128]{2,1,0:T(8,128)S(1)}, f32[21,32,128]{2,1,0:T(8,128)S(1)}) custom-call(bf16[2,10,128,128]{3,2,1,0:T(8,128)(2,1)S(1)} %collective-permute-done.before_ref, bf16[2,20,128,128]{3,2,1,0:T(8,128)(2,1)S(1)} %get-tuple-element.28.own_ref, ...), custom_call_target="tpu_custom_call" | custom-call | flops 4000000000 | bytes 5000000 | tf_op jit(solution)/shard_map/corrections/pallas_call | solution.py:370
  35.7 0.8 %collective-permute-start.6 = (f32[21,32,128]{2,1,0:T(8,128)S(1)}, f32[21,32,128]{2,1,0:T(8,128)S(1)}, u32[]{:S(2)}, u32[]{:S(2)}) collective-permute-start(f32[21,32,128]{2,1,0:T(8,128)S(1)} %get-tuple-element.33), channel_id=1, source_target_pairs={{0,1},{1,0},{2,3},{3,2},{4,5},{5,4},{6,7},{7,6},{8,9},{9,8},{10,11... | collective-permute-start | bytes 1032200 | tf_op jit(solution)/shard_map/ppermute | solution.py:379
  36.6 0.1 collective-permute-start.5
  36.7 1.2 %collective-permute-done.6 = f32[21,32,128]{2,1,0:T(8,128)S(1)} collective-permute-done((f32[21,32,128]{2,1,0:T(8,128)S(1)}, f32[21,32,128]{2,1,0:T(8,128)S(1)}, u32[]{:S(2)}, u32[]{:S(2)}) %collective-permute-start.6) | collective-permute-done | bytes 344096 | tf_op jit(solution)/shard_map/ppermute | solution.py:379
  37.8 0.1 fusion
  37.9 2.8 %collective-permute-start.7 = (f16[21,32,128]{2,1,0:T(8,128)(2,1)S(1)}, f16[21,32,128]{2,1,0:T(8,128)(2,1)S(1)}, u32[]{:S(2)}, u32[]{:S(2)}) collective-permute-start(f16[21,32,128]{2,1,0:T(8,128)(2,1)S(1)} %fusion), channel_id=1, source_target_pairs={{0,2},{1,3},{2,0},{3,1},{4,6},{5,7},{6,4},{7,5},{8,10},{9,11},{10,... | collective-permute-start | bytes 516104 | tf_op jit(solution)/shard_map/ppermute | solution.py:381
  40.7 0.0 collective-permute-done.5
  40.7 1.1 %fusion.1 = f32[20,32,128]{2,1,0:T(8,128)S(1)} fusion(f32[21,32,128]{2,1,0:T(8,128)S(1)} %collective-permute-done.5, f32[2,21,32,128]{3,2,1,0:T(8,128)S(1)} %get-tuple-element.31, f32[20,128,128]{2,1,0:T(8,128)} %param.3, s32[]{:T(128)S(6)} %select_n.3), kind=kLoop, calls=%fused_computation.3 | loop fusion | flops 163840 | bytes 1310724 | tf_op jit(solution)/shard_map/mul | solution.py:384
  41.8 4.3 %collective-permute-done.7 = f16[21,32,128]{2,1,0:T(8,128)(2,1)S(1)} collective-permute-done((f16[21,32,128]{2,1,0:T(8,128)(2,1)S(1)}, f16[21,32,128]{2,1,0:T(8,128)(2,1)S(1)}, u32[]{:S(2)}, u32[]{:S(2)}) %collective-permute-start.7) | collective-permute-done | bytes 172064 | tf_op jit(solution)/shard_map/ppermute | solution.py:381
  46.2 0.8 %multiply_multiply_fusion = f32[20,32,128]{2,1,0:T(8,128)} fusion(f32[20,32,128]{2,1,0:T(8,128)S(1)} %fusion.1, f32[32,128]{1,0:T(8,128)S(1)} %multiply_multiply_fusion.1, f16[21,32,128]{2,1,0:T(8,128)(2,1)S(1)} %collective-permute-done.7), kind=kLoop, calls=%fused_computation.4 | loop fusion | flops 245760 | bytes 835584 | tf_op jit(solution)/shard_map/mul | solution.py:387
  (3 shorter events, 0.1 us)
Async XLA Ops:
  0.0 16.3 %copy-start.1 = (f32[2,3,2,21]{3,2,1,0:T(2,128)S(1)}, f32[2,3,2,21]{3,2,1,0:T(2,128)}, u32[]{:S(2)}) copy-start(f32[2,3,2,21]{3,2,1,0:T(2,128)} %taps_ref.1) | copy-start | bytes 3028
  1.4 17.5 %collective-permute-start.1 = (bf16[20,128,128]{2,1,0:T(8,128)(2,1)S(1)}, bf16[20,128,128]{2,1,0:T(8,128)(2,1)S(1)}, u32[]{:S(2)}, u32[]{:S(2)}) collective-permute-start(bf16[20,128,128]{2,1,0:T(8,128)(2,1)S(1)} %convert_element_type.15.refs_3_), channel_id=1, source_target_pairs={{0,4},{4,8},{8,12},{12,16},{16,20},{20,24},{24,28},{28,32},{32,36}... | collective-permute-start | bytes 1966088 | tf_op jit(solution)/shard_map/ppermute | solution.py:313
  7.4 24.6 %collective-permute-start = (bf16[2,10,128,128]{3,2,1,0:T(8,128)(2,1)}, bf16[2,10,128,128]{3,2,1,0:T(8,128)(2,1)S(1)}, u32[]{:S(2)}, u32[]{:S(2)}) collective-permute-start(bf16[2,10,128,128]{3,2,1,0:T(8,128)(2,1)} %get-tuple-element.21), channel_id=1, source_target_pairs={{0,4},{4,8},{8,12},{12,16},{16,20},{20,24},{24,28},{28,32},{32,36}... | collective-permute-start | bytes 1966088 | tf_op jit(solution)/shard_map/ppermute | solution.py:327
  11.2 20.8 %collective-permute-start.4 = (bf16[2,10,128,128]{3,2,1,0:T(8,128)(2,1)}, bf16[2,10,128,128]{3,2,1,0:T(8,128)(2,1)S(1)}, u32[]{:S(2)}, u32[]{:S(2)}) collective-permute-start(bf16[2,10,128,128]{3,2,1,0:T(8,128)(2,1)} %get-tuple-element.29), channel_id=1, source_target_pairs={{4,0},{8,4},{12,8},{16,12},{20,16},{24,20},{28,24},{32,28},{36,32}... | collective-permute-start | bytes 1966088 | tf_op jit(solution)/shard_map/ppermute | solution.py:328
  19.0 6.3 %collective-permute-start.2 = (bf16[10,128,128]{2,1,0:T(8,128)(2,1)S(1)}, bf16[10,128,128]{2,1,0:T(8,128)(2,1)S(1)}, u32[]{:S(2)}, u32[]{:S(2)}) collective-permute-start(bf16[10,128,128]{2,1,0:T(8,128)(2,1)S(1)} %get-tuple-element.38.refs_1_), channel_id=1, source_target_pairs={{0,1},{1,0},{2,3},{3,2},{4,5},{5,4},{6,7},{7,6},{8,9},{9,8},{10,11... | collective-permute-start | bytes 983048 | tf_op jit(solution)/shard_map/ppermute | solution.py:347
  23.1 2.2 %collective-permute-start.3 = (bf16[10,128,128]{2,1,0:T(8,128)(2,1)S(1)}, bf16[10,128,128]{2,1,0:T(8,128)(2,1)S(1)}, u32[]{:S(2)}, u32[]{:S(2)}) collective-permute-start(bf16[10,128,128]{2,1,0:T(8,128)(2,1)S(1)} %get-tuple-element.37.refs_2_), channel_id=1, source_target_pairs={{0,1},{1,0},{2,3},{3,2},{4,5},{5,4},{6,7},{7,6},{8,9},{9,8},{10,11... | collective-permute-start | bytes 983048 | tf_op jit(solution)/shard_map/ppermute | solution.py:347
  25.2 2.1 %copy-start = (bf16[2,20,128,128]{3,2,1,0:T(8,128)(2,1)S(1)}, bf16[2,20,128,128]{3,2,1,0:T(8,128)(2,1)}, u32[]{:S(2)}) copy-start(bf16[2,20,128,128]{3,2,1,0:T(8,128)(2,1)} %rec_ref.3) | copy-start | bytes 3932164
  35.7 2.1 %collective-permute-start.6 = (f32[21,32,128]{2,1,0:T(8,128)S(1)}, f32[21,32,128]{2,1,0:T(8,128)S(1)}, u32[]{:S(2)}, u32[]{:S(2)}) collective-permute-start(f32[21,32,128]{2,1,0:T(8,128)S(1)} %get-tuple-element.33), channel_id=1, source_target_pairs={{0,1},{1,0},{2,3},{3,2},{4,5},{5,4},{6,7},{7,6},{8,9},{9,8},{10,11... | collective-permute-start | bytes 1032200 | tf_op jit(solution)/shard_map/ppermute | solution.py:379
  36.6 4.2 %collective-permute-start.5 = (f32[21,32,128]{2,1,0:T(8,128)S(1)}, f32[21,32,128]{2,1,0:T(8,128)S(1)}, u32[]{:S(2)}, u32[]{:S(2)}) collective-permute-start(f32[21,32,128]{2,1,0:T(8,128)S(1)} %get-tuple-element.32), channel_id=1, source_target_pairs={{0,1},{1,0},{2,3},{3,2},{4,5},{5,4},{6,7},{7,6},{8,9},{9,8},{10,11... | collective-permute-start | bytes 1032200 | tf_op jit(solution)/shard_map/ppermute | solution.py:380
  37.9 8.2 %collective-permute-start.7 = (f16[21,32,128]{2,1,0:T(8,128)(2,1)S(1)}, f16[21,32,128]{2,1,0:T(8,128)(2,1)S(1)}, u32[]{:S(2)}, u32[]{:S(2)}) collective-permute-start(f16[21,32,128]{2,1,0:T(8,128)(2,1)S(1)} %fusion), channel_id=1, source_target_pairs={{0,2},{1,3},{2,0},{3,1},{4,6},{5,7},{6,4},{7,5},{8,10},{9,11},{10,... | collective-permute-start | bytes 516104 | tf_op jit(solution)/shard_map/ppermute | solution.py:381

commit v13 on v12

--- a/solution.py
+++ b/solution.py
@@ -137,7 +137,7 @@
     return jnp.dot(a, b, preferred_element_type=F32)
 
 
-CHUNK = 4
+CHUNK = 8
 
 
 def inverted(value):

time: 47.2 us -> 47.3 us (level)
  no operation moved by 1% of the time
where the time goes in v13:
time: 47.3 us; the launch traced here: 47 us
  starting transfers between devices  20.7 us (44%)
  Pallas kernels  13.3 us (28%)
  waiting for transfers between devices  9.51 us (20%)
  other arithmetic  3.33 us (7%)
    ppermute x1, starting transfers between devices, local(): after = lax.ppermute(first, 'gz', down)  5.06 us
    ppermute x1, waiting for transfers between devices, local(): lax.ppermute((keep[1] * core_far).astype(jnp.float16), 'view', [(i, i ^ 2...  4.34 us
    pallas_call x2, Pallas kernels, local(): pl.pallas_call(lambda *refs, early=early: inverse_kernel(early, *refs), o...  4.29 us
    ppermute x2, starting transfers between devices, local(): other = [lax.ppermute(piece, 'view', swap) for piece in mine]  4.19 us
    ppermute x1, waiting for transfers between devices, local(): before = lax.ppermute(last, 'gz', up)  3.97 us
    ppermute x1, starting transfers between devices, local(): mine = lax.ppermute(rounded, ('gz', 'view'), both_ways)  3.83 us
    ppermute x1, starting transfers between devices, local(): before = lax.ppermute(last, 'gz', up)  3.83 us
    pallas_call x1, Pallas kernels, local(): pl.pallas_call(correction_kernel, out_shape=[shape((2, planes + 1, part,...  3.82 us
  transfers between devices with their start and end apart: 8, of which 3 were waited for; matrix products, arithmetic and copies ran while one was open for 2% of the time, Pallas kernels for 20%

profile of v13, /device:TPU:24, one launch (start us, length us, event | category | flops | bytes accessed | tf_op | source)
XLA Modules:
  0.0 47.0 jit_solution(1159012022038301514)
XLA Ops:
  0.0 0.0 copy-start.1
  0.0 1.4 %convert_element_type.15.refs_3_ = bf16[20,128,128]{2,1,0:T(8,128)(2,1)S(1)} convert(f32[20,128,128]{2,1,0:T(8,128)} %param.3) | non-fusion elementwise | flops 327680 | bytes 1966080 | tf_op jit(solution)/shard_map/convert_element_type | solution.py:310
  1.4 3.8 %collective-permute-start.1 = (bf16[20,128,128]{2,1,0:T(8,128)(2,1)S(1)}, bf16[20,128,128]{2,1,0:T(8,128)(2,1)S(1)}, u32[]{:S(2)}, u32[]{:S(2)}) collective-permute-start(bf16[20,128,128]{2,1,0:T(8,128)(2,1)S(1)} %convert_element_type.15.refs_3_), channel_id=1, source_target_pairs={{0,4},{4,8},{8,12},{12,16},{16,20},{20,24},{24,28},{28,32},{32,36}... | collective-permute-start | bytes 1966088 | tf_op jit(solution)/shard_map/ppermute | solution.py:313
  5.3 2.1 %edges.1 = (bf16[2,10,128,128]{3,2,1,0:T(8,128)(2,1)}, bf16[2,10,128,128]{3,2,1,0:T(8,128)(2,1)}) custom-call(bf16[2,20,128,128]{3,2,1,0:T(8,128)(2,1)} %rec_ref.3), custom_call_target="tpu_custom_call" | custom-call | flops 10000 | bytes 10000 | tf_op jit(solution)/shard_map/edges/pallas_call | solution.py:315
  7.4 3.8 %collective-permute-start = (bf16[2,10,128,128]{3,2,1,0:T(8,128)(2,1)}, bf16[2,10,128,128]{3,2,1,0:T(8,128)(2,1)S(1)}, u32[]{:S(2)}, u32[]{:S(2)}) collective-permute-start(bf16[2,10,128,128]{3,2,1,0:T(8,128)(2,1)} %get-tuple-element.21), channel_id=1, source_target_pairs={{0,4},{4,8},{8,12},{12,16},{16,20},{20,24},{24,28},{28,32},{32,36}... | collective-permute-start | bytes 1966088 | tf_op jit(solution)/shard_map/ppermute | solution.py:327
  11.2 5.1 %collective-permute-start.4 = (bf16[2,10,128,128]{3,2,1,0:T(8,128)(2,1)}, bf16[2,10,128,128]{3,2,1,0:T(8,128)(2,1)S(1)}, u32[]{:S(2)}, u32[]{:S(2)}) collective-permute-start(bf16[2,10,128,128]{3,2,1,0:T(8,128)(2,1)} %get-tuple-element.29), channel_id=1, source_target_pairs={{4,0},{8,4},{12,8},{16,12},{20,16},{24,20},{28,24},{32,28},{36,32}... | collective-permute-start | bytes 1966088 | tf_op jit(solution)/shard_map/ppermute | solution.py:328
  16.3 0.0 copy-done.1
  16.3 2.6 %matrices.1 = (bf16[2,320,256]{2,1,0:T(8,128)(2,1)S(1)}, bf16[2,2,256,256]{3,2,1,0:T(8,128)(2,1)S(1)}, bf16[2,2,128,256]{3,2,1,0:T(8,128)(2,1)S(1)}, f32[2,1,128]{2,1,0:T(1,128)S(1)}) custom-call(s32[1]{0:T(128)} %bitcast.place_ref.refs_0_, f32[2,3,2,21]{3,2,1,0:T(2,128)S(1)} %copy-done.1), custom_call_target="tpu_custom_call" | custom-call | flops 1000000 | bytes 10000 | tf_op jit(solution)/shard_map/matrices/pallas_call | solution.py:331
  18.9 0.0 collective-permute-done.1
  19.0 4.1 %collective-permute-start.2 = (bf16[10,128,128]{2,1,0:T(8,128)(2,1)S(1)}, bf16[10,128,128]{2,1,0:T(8,128)(2,1)S(1)}, u32[]{:S(2)}, u32[]{:S(2)}) collective-permute-start(bf16[10,128,128]{2,1,0:T(8,128)(2,1)S(1)} %get-tuple-element.38.refs_1_), channel_id=1, source_target_pairs={{0,1},{1,0},{2,3},{3,2},{4,5},{5,4},{6,7},{7,6},{8,9},{9,8},{10,11... | collective-permute-start | bytes 983048 | tf_op jit(solution)/shard_map/ppermute | solution.py:347
  23.1 0.1 collective-permute-start.3
  23.2 2.1 %inverses.2.early_ref = f32[2,20,128,128]{3,2,1,0:T(8,128)S(1)} custom-call(s32[1]{0:T(128)} %bitcast.place_ref.refs_0_, bf16[10,128,128]{2,1,0:T(8,128)(2,1)S(1)} %get-tuple-element.38.refs_1_, bf16[10,128,128]{2,1,0:T(8,128)(2,1)S(1)} %get-tuple-element.37.refs_2_, bf16[20,128,128]{2,1,0:T(8,128)(2,1)S(1)} %convert_element_type.15.refs_3_, ...), custom_call_target="tpu_custom_call" | custom-call | flops 1000000 | bytes 10000 | tf_op jit(solution)/shard_map/inverses/pallas_call | solution.py:351
  25.3 0.0 copy-start
  25.3 0.0 collective-permute-done.2.refs_1_
  25.3 0.0 collective-permute-done.3.refs_2_
  25.3 2.1 %inverses.3.late_ref = f32[2,20,128,128]{3,2,1,0:T(8,128)S(1)} custom-call(s32[1]{0:T(128)} %bitcast.place_ref.refs_0_, bf16[10,128,128]{2,1,0:T(8,128)(2,1)S(1)} %collective-permute-done.2.refs_1_, bf16[10,128,128]{2,1,0:T(8,128)(2,1)S(1)} %collective-permute-done.3.refs_2_, bf16[20,128,128]{2,1,0:T(8,128)(2,1)S(1)} %convert_element_type.15.refs_3_, ...), custom_call_target="tpu_custom_call" | custom-call | flops 1000000 | bytes 10000 | tf_op jit(solution)/shard_map/inverses/pallas_call | solution.py:351
  27.5 0.0 copy-done
  27.5 0.5 %arrange.1 = (bf16[2,20,128,128]{3,2,1,0:T(8,128)(2,1)S(1)}, f32[2,2,10,128,128]{4,3,2,1,0:T(8,128)S(1)}) custom-call(s32[1]{0:T(128)} %bitcast.place_ref.refs_0_, bf16[2,20,128,128]{3,2,1,0:T(8,128)(2,1)S(1)} %copy-done, f32[2,20,128,128]{3,2,1,0:T(8,128)S(1)} %inverses.2.early_ref, f32[2,20,128,128]{3,2,1,0:T(8,128)S(1)} %inverses.3.late_ref), custom_call_target="tpu_custom_call" | custom-call | flops 100000 | bytes 10000 | tf_op jit(solution)/shard_map/arrange/pallas_call | solution.py:361
  28.0 4.0 %collective-permute-done.before_ref = bf16[2,10,128,128]{3,2,1,0:T(8,128)(2,1)S(1)} collective-permute-done((bf16[2,10,128,128]{3,2,1,0:T(8,128)(2,1)}, bf16[2,10,128,128]{3,2,1,0:T(8,128)(2,1)S(1)}, u32[]{:S(2)}, u32[]{:S(2)}) %collective-permute-start) | collective-permute-done | bytes 655392 | tf_op jit(solution)/shard_map/ppermute | solution.py:327
  32.0 0.0 collective-permute-done.4.after_ref
  32.0 3.8 %corrections.1 = (f32[2,21,32,128]{3,2,1,0:T(8,128)S(1)}, f32[21,32,128]{2,1,0:T(8,128)S(1)}, f32[21,32,128]{2,1,0:T(8,128)S(1)}) custom-call(bf16[2,10,128,128]{3,2,1,0:T(8,128)(2,1)S(1)} %collective-permute-done.before_ref, bf16[2,20,128,128]{3,2,1,0:T(8,128)(2,1)S(1)} %get-tuple-element.28.own_ref, ...), custom_call_target="tpu_custom_call" | custom-call | flops 4000000000 | bytes 5000000 | tf_op jit(solution)/shard_map/corrections/pallas_call | solution.py:370
  35.8 0.8 %collective-permute-start.6 = (f32[21,32,128]{2,1,0:T(8,128)S(1)}, f32[21,32,128]{2,1,0:T(8,128)S(1)}, u32[]{:S(2)}, u32[]{:S(2)}) collective-permute-start(f32[21,32,128]{2,1,0:T(8,128)S(1)} %get-tuple-element.33), channel_id=1, source_target_pairs={{0,1},{1,0},{2,3},{3,2},{4,5},{5,4},{6,7},{7,6},{8,9},{9,8},{10,11... | collective-permute-start | bytes 1032200 | tf_op jit(solution)/shard_map/ppermute | solution.py:379
  36.7 0.1 collective-permute-start.5
  36.8 1.2 %collective-permute-done.6 = f32[21,32,128]{2,1,0:T(8,128)S(1)} collective-permute-done((f32[21,32,128]{2,1,0:T(8,128)S(1)}, f32[21,32,128]{2,1,0:T(8,128)S(1)}, u32[]{:S(2)}, u32[]{:S(2)}) %collective-permute-start.6) | collective-permute-done | bytes 344096 | tf_op jit(solution)/shard_map/ppermute | solution.py:379
  37.9 0.1 fusion
  38.0 2.8 %collective-permute-start.7 = (f16[21,32,128]{2,1,0:T(8,128)(2,1)S(1)}, f16[21,32,128]{2,1,0:T(8,128)(2,1)S(1)}, u32[]{:S(2)}, u32[]{:S(2)}) collective-permute-start(f16[21,32,128]{2,1,0:T(8,128)(2,1)S(1)} %fusion), channel_id=1, source_target_pairs={{0,2},{1,3},{2,0},{3,1},{4,6},{5,7},{6,4},{7,5},{8,10},{9,11},{10,... | collective-permute-start | bytes 516104 | tf_op jit(solution)/shard_map/ppermute | solution.py:381
  40.8 0.0 collective-permute-done.5
  40.8 1.1 %fusion.1 = f32[20,32,128]{2,1,0:T(8,128)S(1)} fusion(f32[21,32,128]{2,1,0:T(8,128)S(1)} %collective-permute-done.5, f32[2,21,32,128]{3,2,1,0:T(8,128)S(1)} %get-tuple-element.31, f32[20,128,128]{2,1,0:T(8,128)} %param.3, s32[]{:T(128)S(6)} %select_n.3), kind=kLoop, calls=%fused_computation.3 | loop fusion | flops 163840 | bytes 1310724 | tf_op jit(solution)/shard_map/mul | solution.py:384
  41.9 4.3 %collective-permute-done.7 = f16[21,32,128]{2,1,0:T(8,128)(2,1)S(1)} collective-permute-done((f16[21,32,128]{2,1,0:T(8,128)(2,1)S(1)}, f16[21,32,128]{2,1,0:T(8,128)(2,1)S(1)}, u32[]{:S(2)}, u32[]{:S(2)}) %collective-permute-start.7) | collective-permute-done | bytes 172064 | tf_op jit(solution)/shard_map/ppermute | solution.py:381
  46.2 0.8 %multiply_multiply_fusion = f32[20,32,128]{2,1,0:T(8,128)} fusion(f32[20,32,128]{2,1,0:T(8,128)S(1)} %fusion.1, f32[32,128]{1,0:T(8,128)S(1)} %multiply_multiply_fusion.1, f16[21,32,128]{2,1,0:T(8,128)(2,1)S(1)} %collective-permute-done.7), kind=kLoop, calls=%fused_computation.4 | loop fusion | flops 245760 | bytes 835584 | tf_op jit(solution)/shard_map/mul | solution.py:387
  (3 shorter events, 0.1 us)
Async XLA Ops:
  0.0 16.3 %copy-start.1 = (f32[2,3,2,21]{3,2,1,0:T(2,128)S(1)}, f32[2,3,2,21]{3,2,1,0:T(2,128)}, u32[]{:S(2)}) copy-start(f32[2,3,2,21]{3,2,1,0:T(2,128)} %taps_ref.1) | copy-start | bytes 3028
  1.4 17.5 %collective-permute-start.1 = (bf16[20,128,128]{2,1,0:T(8,128)(2,1)S(1)}, bf16[20,128,128]{2,1,0:T(8,128)(2,1)S(1)}, u32[]{:S(2)}, u32[]{:S(2)}) collective-permute-start(bf16[20,128,128]{2,1,0:T(8,128)(2,1)S(1)} %convert_element_type.15.refs_3_), channel_id=1, source_target_pairs={{0,4},{4,8},{8,12},{12,16},{16,20},{20,24},{24,28},{28,32},{32,36}... | collective-permute-start | bytes 1966088 | tf_op jit(solution)/shard_map/ppermute | solution.py:313
  7.4 24.6 %collective-permute-start = (bf16[2,10,128,128]{3,2,1,0:T(8,128)(2,1)}, bf16[2,10,128,128]{3,2,1,0:T(8,128)(2,1)S(1)}, u32[]{:S(2)}, u32[]{:S(2)}) collective-permute-start(bf16[2,10,128,128]{3,2,1,0:T(8,128)(2,1)} %get-tuple-element.21), channel_id=1, source_target_pairs={{0,4},{4,8},{8,12},{12,16},{16,20},{20,24},{24,28},{28,32},{32,36}... | collective-permute-start | bytes 1966088 | tf_op jit(solution)/shard_map/ppermute | solution.py:327
  11.2 20.8 %collective-permute-start.4 = (bf16[2,10,128,128]{3,2,1,0:T(8,128)(2,1)}, bf16[2,10,128,128]{3,2,1,0:T(8,128)(2,1)S(1)}, u32[]{:S(2)}, u32[]{:S(2)}) collective-permute-start(bf16[2,10,128,128]{3,2,1,0:T(8,128)(2,1)} %get-tuple-element.29), channel_id=1, source_target_pairs={{4,0},{8,4},{12,8},{16,12},{20,16},{24,20},{28,24},{32,28},{36,32}... | collective-permute-start | bytes 1966088 | tf_op jit(solution)/shard_map/ppermute | solution.py:328
  19.0 6.4 %collective-permute-start.2 = (bf16[10,128,128]{2,1,0:T(8,128)(2,1)S(1)}, bf16[10,128,128]{2,1,0:T(8,128)(2,1)S(1)}, u32[]{:S(2)}, u32[]{:S(2)}) collective-permute-start(bf16[10,128,128]{2,1,0:T(8,128)(2,1)S(1)} %get-tuple-element.38.refs_1_), channel_id=1, source_target_pairs={{0,1},{1,0},{2,3},{3,2},{4,5},{5,4},{6,7},{7,6},{8,9},{9,8},{10,11... | collective-permute-start | bytes 983048 | tf_op jit(solution)/shard_map/ppermute | solution.py:347
  23.1 2.3 %collective-permute-start.3 = (bf16[10,128,128]{2,1,0:T(8,128)(2,1)S(1)}, bf16[10,128,128]{2,1,0:T(8,128)(2,1)S(1)}, u32[]{:S(2)}, u32[]{:S(2)}) collective-permute-start(bf16[10,128,128]{2,1,0:T(8,128)(2,1)S(1)} %get-tuple-element.37.refs_2_), channel_id=1, source_target_pairs={{0,1},{1,0},{2,3},{3,2},{4,5},{5,4},{6,7},{7,6},{8,9},{9,8},{10,11... | collective-permute-start | bytes 983048 | tf_op jit(solution)/shard_map/ppermute | solution.py:347
  25.3 2.2 %copy-start = (bf16[2,20,128,128]{3,2,1,0:T(8,128)(2,1)S(1)}, bf16[2,20,128,128]{3,2,1,0:T(8,128)(2,1)}, u32[]{:S(2)}) copy-start(bf16[2,20,128,128]{3,2,1,0:T(8,128)(2,1)} %rec_ref.3) | copy-start | bytes 3932164
  35.8 2.1 %collective-permute-start.6 = (f32[21,32,128]{2,1,0:T(8,128)S(1)}, f32[21,32,128]{2,1,0:T(8,128)S(1)}, u32[]{:S(2)}, u32[]{:S(2)}) collective-permute-start(f32[21,32,128]{2,1,0:T(8,128)S(1)} %get-tuple-element.33), channel_id=1, source_target_pairs={{0,1},{1,0},{2,3},{3,2},{4,5},{5,4},{6,7},{7,6},{8,9},{9,8},{10,11... | collective-permute-start | bytes 1032200 | tf_op jit(solution)/shard_map/ppermute | solution.py:379
  36.7 4.2 %collective-permute-start.5 = (f32[21,32,128]{2,1,0:T(8,128)S(1)}, f32[21,32,128]{2,1,0:T(8,128)S(1)}, u32[]{:S(2)}, u32[]{:S(2)}) collective-permute-start(f32[21,32,128]{2,1,0:T(8,128)S(1)} %get-tuple-element.32), channel_id=1, source_target_pairs={{0,1},{1,0},{2,3},{3,2},{4,5},{5,4},{6,7},{7,6},{8,9},{9,8},{10,11... | collective-permute-start | bytes 1032200 | tf_op jit(solution)/shard_map/ppermute | solution.py:380
  38.0 8.2 %collective-permute-start.7 = (f16[21,32,128]{2,1,0:T(8,128)(2,1)S(1)}, f16[21,32,128]{2,1,0:T(8,128)(2,1)S(1)}, u32[]{:S(2)}, u32[]{:S(2)}) collective-permute-start(f16[21,32,128]{2,1,0:T(8,128)(2,1)S(1)} %fusion), channel_id=1, source_target_pairs={{0,2},{1,3},{2,0},{3,1},{4,6},{5,7},{6,4},{7,5},{8,10},{9,11},{10,... | collective-permute-start | bytes 516104 | tf_op jit(solution)/shard_map/ppermute | solution.py:381

commit v14 on v13

--- a/solution.py
+++ b/solution.py
@@ -137,7 +137,7 @@
     return jnp.dot(a, b, preferred_element_type=F32)
 
 
-CHUNK = 8
+CHUNK = 2
 
 
 def inverted(value):

time: 47.3 us -> 47.2 us (level)
  no operation moved by 1% of the time
where the time goes in v14:
time: 47.2 us; the launch traced here: 47 us
  starting transfers between devices  20.7 us (44%)
  Pallas kernels  13.1 us (28%)
  waiting for transfers between devices  9.68 us (21%)
  other arithmetic  3.33 us (7%)
    ppermute x1, starting transfers between devices, local(): after = lax.ppermute(first, 'gz', down)  5.06 us
    ppermute x1, waiting for transfers between devices, local(): lax.ppermute((keep[1] * core_far).astype(jnp.float16), 'view', [(i, i ^ 2...  4.34 us
    ppermute x2, starting transfers between devices, local(): other = [lax.ppermute(piece, 'view', swap) for piece in mine]  4.19 us
    ppermute x1, waiting for transfers between devices, local(): before = lax.ppermute(last, 'gz', up)  4.15 us
    pallas_call x2, Pallas kernels, local(): pl.pallas_call(lambda *refs, early=early: inverse_kernel(early, *refs), o...  4.12 us
    ppermute x1, starting transfers between devices, local(): mine = lax.ppermute(rounded, ('gz', 'view'), both_ways)  3.83 us
    ppermute x1, starting transfers between devices, local(): before = lax.ppermute(last, 'gz', up)  3.83 us
    pallas_call x1, Pallas kernels, local(): pl.pallas_call(correction_kernel, out_shape=[shape((2, planes + 1, part,...  3.76 us
  transfers between devices with their start and end apart: 8, of which 3 were waited for; matrix products, arithmetic and copies ran while one was open for 2% of the time, Pallas kernels for 20%

profile of v14, /device:TPU:24, one launch (start us, length us, event | category | flops | bytes accessed | tf_op | source)
XLA Modules:
  0.0 47.0 jit_solution(18236084831878815678)
XLA Ops:
  0.0 0.0 copy-start.1
  0.0 1.4 %convert_element_type.15.refs_3_ = bf16[20,128,128]{2,1,0:T(8,128)(2,1)S(1)} convert(f32[20,128,128]{2,1,0:T(8,128)} %param.3) | non-fusion elementwise | flops 327680 | bytes 1966080 | tf_op jit(solution)/shard_map/convert_element_type | solution.py:310
  1.4 3.8 %collective-permute-start.1 = (bf16[20,128,128]{2,1,0:T(8,128)(2,1)S(1)}, bf16[20,128,128]{2,1,0:T(8,128)(2,1)S(1)}, u32[]{:S(2)}, u32[]{:S(2)}) collective-permute-start(bf16[20,128,128]{2,1,0:T(8,128)(2,1)S(1)} %convert_element_type.15.refs_3_), channel_id=1, source_target_pairs={{0,4},{4,8},{8,12},{12,16},{16,20},{20,24},{24,28},{28,32},{32,36}... | collective-permute-start | bytes 1966088 | tf_op jit(solution)/shard_map/ppermute | solution.py:313
  5.3 2.1 %edges.1 = (bf16[2,10,128,128]{3,2,1,0:T(8,128)(2,1)}, bf16[2,10,128,128]{3,2,1,0:T(8,128)(2,1)}) custom-call(bf16[2,20,128,128]{3,2,1,0:T(8,128)(2,1)} %rec_ref.3), custom_call_target="tpu_custom_call" | custom-call | flops 10000 | bytes 10000 | tf_op jit(solution)/shard_map/edges/pallas_call | solution.py:315
  7.4 3.8 %collective-permute-start = (bf16[2,10,128,128]{3,2,1,0:T(8,128)(2,1)}, bf16[2,10,128,128]{3,2,1,0:T(8,128)(2,1)S(1)}, u32[]{:S(2)}, u32[]{:S(2)}) collective-permute-start(bf16[2,10,128,128]{3,2,1,0:T(8,128)(2,1)} %get-tuple-element.21), channel_id=1, source_target_pairs={{0,4},{4,8},{8,12},{12,16},{16,20},{20,24},{24,28},{28,32},{32,36}... | collective-permute-start | bytes 1966088 | tf_op jit(solution)/shard_map/ppermute | solution.py:327
  11.2 5.1 %collective-permute-start.4 = (bf16[2,10,128,128]{3,2,1,0:T(8,128)(2,1)}, bf16[2,10,128,128]{3,2,1,0:T(8,128)(2,1)S(1)}, u32[]{:S(2)}, u32[]{:S(2)}) collective-permute-start(bf16[2,10,128,128]{3,2,1,0:T(8,128)(2,1)} %get-tuple-element.29), channel_id=1, source_target_pairs={{4,0},{8,4},{12,8},{16,12},{20,16},{24,20},{28,24},{32,28},{36,32}... | collective-permute-start | bytes 1966088 | tf_op jit(solution)/shard_map/ppermute | solution.py:328
  16.3 0.0 copy-done.1
  16.3 2.6 %matrices.1 = (bf16[2,320,256]{2,1,0:T(8,128)(2,1)S(1)}, bf16[2,2,256,256]{3,2,1,0:T(8,128)(2,1)S(1)}, bf16[2,2,128,256]{3,2,1,0:T(8,128)(2,1)S(1)}, f32[2,1,128]{2,1,0:T(1,128)S(1)}) custom-call(s32[1]{0:T(128)} %bitcast.place_ref.refs_0_, f32[2,3,2,21]{3,2,1,0:T(2,128)S(1)} %copy-done.1), custom_call_target="tpu_custom_call" | custom-call | flops 1000000 | bytes 10000 | tf_op jit(solution)/shard_map/matrices/pallas_call | solution.py:331
  18.9 0.0 collective-permute-done.1
  19.0 4.1 %collective-permute-start.2 = (bf16[10,128,128]{2,1,0:T(8,128)(2,1)S(1)}, bf16[10,128,128]{2,1,0:T(8,128)(2,1)S(1)}, u32[]{:S(2)}, u32[]{:S(2)}) collective-permute-start(bf16[10,128,128]{2,1,0:T(8,128)(2,1)S(1)} %get-tuple-element.38.refs_1_), channel_id=1, source_target_pairs={{0,1},{1,0},{2,3},{3,2},{4,5},{5,4},{6,7},{7,6},{8,9},{9,8},{10,11... | collective-permute-start | bytes 983048 | tf_op jit(solution)/shard_map/ppermute | solution.py:347
  23.1 0.1 collective-permute-start.3
  23.2 2.1 %inverses.2.early_ref = f32[2,20,128,128]{3,2,1,0:T(8,128)S(1)} custom-call(s32[1]{0:T(128)} %bitcast.place_ref.refs_0_, bf16[10,128,128]{2,1,0:T(8,128)(2,1)S(1)} %get-tuple-element.38.refs_1_, bf16[10,128,128]{2,1,0:T(8,128)(2,1)S(1)} %get-tuple-element.37.refs_2_, bf16[20,128,128]{2,1,0:T(8,128)(2,1)S(1)} %convert_element_type.15.refs_3_, ...), custom_call_target="tpu_custom_call" | custom-call | flops 1000000 | bytes 10000 | tf_op jit(solution)/shard_map/inverses/pallas_call | solution.py:351
  25.2 0.0 copy-start
  25.2 0.0 collective-permute-done.2.refs_1_
  25.2 0.0 collective-permute-done.3.refs_2_
  25.3 2.1 %inverses.3.late_ref = f32[2,20,128,128]{3,2,1,0:T(8,128)S(1)} custom-call(s32[1]{0:T(128)} %bitcast.place_ref.refs_0_, bf16[10,128,128]{2,1,0:T(8,128)(2,1)S(1)} %collective-permute-done.2.refs_1_, bf16[10,128,128]{2,1,0:T(8,128)(2,1)S(1)} %collective-permute-done.3.refs_2_, bf16[20,128,128]{2,1,0:T(8,128)(2,1)S(1)} %convert_element_type.15.refs_3_, ...), custom_call_target="tpu_custom_call" | custom-call | flops 1000000 | bytes 10000 | tf_op jit(solution)/shard_map/inverses/pallas_call | solution.py:351
  27.3 0.0 copy-done
  27.3 0.5 %arrange.1 = (bf16[2,20,128,128]{3,2,1,0:T(8,128)(2,1)S(1)}, f32[2,2,10,128,128]{4,3,2,1,0:T(8,128)S(1)}) custom-call(s32[1]{0:T(128)} %bitcast.place_ref.refs_0_, bf16[2,20,128,128]{3,2,1,0:T(8,128)(2,1)S(1)} %copy-done, f32[2,20,128,128]{3,2,1,0:T(8,128)S(1)} %inverses.2.early_ref, f32[2,20,128,128]{3,2,1,0:T(8,128)S(1)} %inverses.3.late_ref), custom_call_target="tpu_custom_call" | custom-call | flops 100000 | bytes 10000 | tf_op jit(solution)/shard_map/arrange/pallas_call | solution.py:361
  27.9 4.1 %collective-permute-done.before_ref = bf16[2,10,128,128]{3,2,1,0:T(8,128)(2,1)S(1)} collective-permute-done((bf16[2,10,128,128]{3,2,1,0:T(8,128)(2,1)}, bf16[2,10,128,128]{3,2,1,0:T(8,128)(2,1)S(1)}, u32[]{:S(2)}, u32[]{:S(2)}) %collective-permute-start) | collective-permute-done | bytes 655392 | tf_op jit(solution)/shard_map/ppermute | solution.py:327
  32.0 0.0 collective-permute-done.4.after_ref
  32.0 3.8 %corrections.1 = (f32[2,21,32,128]{3,2,1,0:T(8,128)S(1)}, f32[21,32,128]{2,1,0:T(8,128)S(1)}, f32[21,32,128]{2,1,0:T(8,128)S(1)}) custom-call(bf16[2,10,128,128]{3,2,1,0:T(8,128)(2,1)S(1)} %collective-permute-done.before_ref, bf16[2,20,128,128]{3,2,1,0:T(8,128)(2,1)S(1)} %get-tuple-element.28.own_ref, ...), custom_call_target="tpu_custom_call" | custom-call | flops 4000000000 | bytes 5000000 | tf_op jit(solution)/shard_map/corrections/pallas_call | solution.py:370
  35.8 0.8 %collective-permute-start.6 = (f32[21,32,128]{2,1,0:T(8,128)S(1)}, f32[21,32,128]{2,1,0:T(8,128)S(1)}, u32[]{:S(2)}, u32[]{:S(2)}) collective-permute-start(f32[21,32,128]{2,1,0:T(8,128)S(1)} %get-tuple-element.33), channel_id=1, source_target_pairs={{0,1},{1,0},{2,3},{3,2},{4,5},{5,4},{6,7},{7,6},{8,9},{9,8},{10,11... | collective-permute-start | bytes 1032200 | tf_op jit(solution)/shard_map/ppermute | solution.py:379
  36.6 0.1 collective-permute-start.5
  36.7 1.2 %collective-permute-done.6 = f32[21,32,128]{2,1,0:T(8,128)S(1)} collective-permute-done((f32[21,32,128]{2,1,0:T(8,128)S(1)}, f32[21,32,128]{2,1,0:T(8,128)S(1)}, u32[]{:S(2)}, u32[]{:S(2)}) %collective-permute-start.6) | collective-permute-done | bytes 344096 | tf_op jit(solution)/shard_map/ppermute | solution.py:379
  37.9 0.1 fusion
  37.9 2.8 %collective-permute-start.7 = (f16[21,32,128]{2,1,0:T(8,128)(2,1)S(1)}, f16[21,32,128]{2,1,0:T(8,128)(2,1)S(1)}, u32[]{:S(2)}, u32[]{:S(2)}) collective-permute-start(f16[21,32,128]{2,1,0:T(8,128)(2,1)S(1)} %fusion), channel_id=1, source_target_pairs={{0,2},{1,3},{2,0},{3,1},{4,6},{5,7},{6,4},{7,5},{8,10},{9,11},{10,... | collective-permute-start | bytes 516104 | tf_op jit(solution)/shard_map/ppermute | solution.py:381
  40.8 0.0 collective-permute-done.5
  40.8 1.1 %fusion.1 = f32[20,32,128]{2,1,0:T(8,128)S(1)} fusion(f32[21,32,128]{2,1,0:T(8,128)S(1)} %collective-permute-done.5, f32[2,21,32,128]{3,2,1,0:T(8,128)S(1)} %get-tuple-element.31, f32[20,128,128]{2,1,0:T(8,128)} %param.3, s32[]{:T(128)S(6)} %select_n.3), kind=kLoop, calls=%fused_computation.3 | loop fusion | flops 163840 | bytes 1310724 | tf_op jit(solution)/shard_map/mul | solution.py:384
  41.8 4.3 %collective-permute-done.7 = f16[21,32,128]{2,1,0:T(8,128)(2,1)S(1)} collective-permute-done((f16[21,32,128]{2,1,0:T(8,128)(2,1)S(1)}, f16[21,32,128]{2,1,0:T(8,128)(2,1)S(1)}, u32[]{:S(2)}, u32[]{:S(2)}) %collective-permute-start.7) | collective-permute-done | bytes 172064 | tf_op jit(solution)/shard_map/ppermute | solution.py:381
  46.2 0.8 %multiply_multiply_fusion = f32[20,32,128]{2,1,0:T(8,128)} fusion(f32[20,32,128]{2,1,0:T(8,128)S(1)} %fusion.1, f32[32,128]{1,0:T(8,128)S(1)} %multiply_multiply_fusion.1, f16[21,32,128]{2,1,0:T(8,128)(2,1)S(1)} %collective-permute-done.7), kind=kLoop, calls=%fused_computation.4 | loop fusion | flops 245760 | bytes 835584 | tf_op jit(solution)/shard_map/mul | solution.py:387
  (3 shorter events, 0.1 us)
Async XLA Ops:
  0.0 16.3 %copy-start.1 = (f32[2,3,2,21]{3,2,1,0:T(2,128)S(1)}, f32[2,3,2,21]{3,2,1,0:T(2,128)}, u32[]{:S(2)}) copy-start(f32[2,3,2,21]{3,2,1,0:T(2,128)} %taps_ref.1) | copy-start | bytes 3028
  1.4 17.5 %collective-permute-start.1 = (bf16[20,128,128]{2,1,0:T(8,128)(2,1)S(1)}, bf16[20,128,128]{2,1,0:T(8,128)(2,1)S(1)}, u32[]{:S(2)}, u32[]{:S(2)}) collective-permute-start(bf16[20,128,128]{2,1,0:T(8,128)(2,1)S(1)} %convert_element_type.15.refs_3_), channel_id=1, source_target_pairs={{0,4},{4,8},{8,12},{12,16},{16,20},{20,24},{24,28},{28,32},{32,36}... | collective-permute-start | bytes 1966088 | tf_op jit(solution)/shard_map/ppermute | solution.py:313
  7.4 24.6 %collective-permute-start = (bf16[2,10,128,128]{3,2,1,0:T(8,128)(2,1)}, bf16[2,10,128,128]{3,2,1,0:T(8,128)(2,1)S(1)}, u32[]{:S(2)}, u32[]{:S(2)}) collective-permute-start(bf16[2,10,128,128]{3,2,1,0:T(8,128)(2,1)} %get-tuple-element.21), channel_id=1, source_target_pairs={{0,4},{4,8},{8,12},{12,16},{16,20},{20,24},{24,28},{28,32},{32,36}... | collective-permute-start | bytes 1966088 | tf_op jit(solution)/shard_map/ppermute | solution.py:327
  11.2 20.8 %collective-permute-start.4 = (bf16[2,10,128,128]{3,2,1,0:T(8,128)(2,1)}, bf16[2,10,128,128]{3,2,1,0:T(8,128)(2,1)S(1)}, u32[]{:S(2)}, u32[]{:S(2)}) collective-permute-start(bf16[2,10,128,128]{3,2,1,0:T(8,128)(2,1)} %get-tuple-element.29), channel_id=1, source_target_pairs={{4,0},{8,4},{12,8},{16,12},{20,16},{24,20},{28,24},{32,28},{36,32}... | collective-permute-start | bytes 1966088 | tf_op jit(solution)/shard_map/ppermute | solution.py:328
  19.0 6.3 %collective-permute-start.2 = (bf16[10,128,128]{2,1,0:T(8,128)(2,1)S(1)}, bf16[10,128,128]{2,1,0:T(8,128)(2,1)S(1)}, u32[]{:S(2)}, u32[]{:S(2)}) collective-permute-start(bf16[10,128,128]{2,1,0:T(8,128)(2,1)S(1)} %get-tuple-element.38.refs_1_), channel_id=1, source_target_pairs={{0,1},{1,0},{2,3},{3,2},{4,5},{5,4},{6,7},{7,6},{8,9},{9,8},{10,11... | collective-permute-start | bytes 983048 | tf_op jit(solution)/shard_map/ppermute | solution.py:347
  23.1 2.2 %collective-permute-start.3 = (bf16[10,128,128]{2,1,0:T(8,128)(2,1)S(1)}, bf16[10,128,128]{2,1,0:T(8,128)(2,1)S(1)}, u32[]{:S(2)}, u32[]{:S(2)}) collective-permute-start(bf16[10,128,128]{2,1,0:T(8,128)(2,1)S(1)} %get-tuple-element.37.refs_2_), channel_id=1, source_target_pairs={{0,1},{1,0},{2,3},{3,2},{4,5},{5,4},{6,7},{7,6},{8,9},{9,8},{10,11... | collective-permute-start | bytes 983048 | tf_op jit(solution)/shard_map/ppermute | solution.py:347
  25.2 2.1 %copy-start = (bf16[2,20,128,128]{3,2,1,0:T(8,128)(2,1)S(1)}, bf16[2,20,128,128]{3,2,1,0:T(8,128)(2,1)}, u32[]{:S(2)}) copy-start(bf16[2,20,128,128]{3,2,1,0:T(8,128)(2,1)} %rec_ref.3) | copy-start | bytes 3932164
  35.8 2.1 %collective-permute-start.6 = (f32[21,32,128]{2,1,0:T(8,128)S(1)}, f32[21,32,128]{2,1,0:T(8,128)S(1)}, u32[]{:S(2)}, u32[]{:S(2)}) collective-permute-start(f32[21,32,128]{2,1,0:T(8,128)S(1)} %get-tuple-element.33), channel_id=1, source_target_pairs={{0,1},{1,0},{2,3},{3,2},{4,5},{5,4},{6,7},{7,6},{8,9},{9,8},{10,11... | collective-permute-start | bytes 1032200 | tf_op jit(solution)/shard_map/ppermute | solution.py:379
  36.6 4.2 %collective-permute-start.5 = (f32[21,32,128]{2,1,0:T(8,128)S(1)}, f32[21,32,128]{2,1,0:T(8,128)S(1)}, u32[]{:S(2)}, u32[]{:S(2)}) collective-permute-start(f32[21,32,128]{2,1,0:T(8,128)S(1)} %get-tuple-element.32), channel_id=1, source_target_pairs={{0,1},{1,0},{2,3},{3,2},{4,5},{5,4},{6,7},{7,6},{8,9},{9,8},{10,11... | collective-permute-start | bytes 1032200 | tf_op jit(solution)/shard_map/ppermute | solution.py:380
  37.9 8.2 %collective-permute-start.7 = (f16[21,32,128]{2,1,0:T(8,128)(2,1)S(1)}, f16[21,32,128]{2,1,0:T(8,128)(2,1)S(1)}, u32[]{:S(2)}, u32[]{:S(2)}) collective-permute-start(f16[21,32,128]{2,1,0:T(8,128)(2,1)S(1)} %fusion), channel_id=1, source_target_pairs={{0,2},{1,3},{2,0},{3,1},{4,6},{5,7},{6,4},{7,5},{8,10},{9,11},{10,... | collective-permute-start | bytes 516104 | tf_op jit(solution)/shard_map/ppermute | solution.py:381
